TPU v7x, 32 devices: a whole 2x2x4 slice. The times are simulated.
32 devices in a mesh: dom: 4 (over x, core), block: 8 (over z, y).
Axes of the slice: x: 2, y: 2, z: 4, core: 2. Of those that a mesh axis runs over, the one named last changes fastest.
Arguments:
- entities: float32 [1024, 400], P(('dom', 'block')), may hold values from -2.5 to 2.5
- relations: float32 [4096, 400], replicated, may hold values from -4 to 4
- src_index: int32 [4, 16, 256], P('dom', 'block'), may hold values from 0 to 255
- dst_index: int32 [4, 16, 256], P('dom', 'block'), may hold values from 0 to 255
- rel_index: int32 [4, 16, 256], P('dom', 'block'), may hold values from 0 to 4095
- neg_index: int32 [4, 16, 1024], P('dom', 'block'), may hold values from 0 to 255
- counts: int32 [4, 16], P('dom', 'block'), may hold values from 1 to 256, 2048 in all within a row
- edge_weight: float32 [4, 16, 256], P('dom', 'block'), may hold values from 0.25 to 4
Outputs:
- entity_grad: float32 [1024, 400], P(('dom', 'block'))
- relation_grad: float32 [4096, 400], replicated
Inputs may be any that keep to these rules, and one draw needn't show every extreme that they name: The counts of one bucket sum to 2048.
All inputs are finite; a program needn't handle non-finite values. No bound on the sum of `counts` on one device may be relied on, other than what follows from the above.
Results may differ from a plain program's by a relative error of at most 0.0003.
Values sent between devices are 32-bit elements; how exact they have to be, the bound alone decides.
No kernel may reach another device: no remote copies, remote signals or barrier semaphores. Data moves between devices by JAX's collectives and lax.ppermute only.
A program may use at most 128 MiB of HBM per device.

v0:
```python
import jax
import jax.numpy as jnp
from jax import lax
from jax.sharding import PartitionSpec as P


def partner(block, axis, bit):
    count = lax.axis_size(axis)
    route = []
    for low in range(count):
        high = low | 1 << bit
        if high != low and high < count:
            route += [(low, high), (high, low)]
    return lax.ppermute(block, axis, route)


def block_gradients(
    source_rows,
    target_rows,
    relations,
    source_ids,
    target_ids,
    relation_ids,
    negative_ids,
    live_count,
    edge_weight,
):
    half_width = source_rows.shape[1] // 2
    sources = source_rows[source_ids]
    targets = target_rows[target_ids]
    factors = relations[relation_ids]
    negatives = target_rows[negative_ids]
    source_real, source_imag = (sources[:, :half_width], sources[:, half_width:])
    factor_real, factor_imag = (factors[:, :half_width], factors[:, half_width:])
    queries = jnp.concatenate(
        [
            source_real * factor_real - source_imag * factor_imag,
            source_real * factor_imag + source_imag * factor_real,
        ],
        axis=1,
    )
    positive = jnp.sum(queries * targets, axis=1)
    negative = jnp.dot(
        queries, negatives.T, precision=lax.Precision.HIGHEST, preferred_element_type=jnp.float32
    )
    live_mask = (jnp.arange(queries.shape[0], dtype=jnp.int32) < live_count).astype(jnp.float32)
    scaled = edge_weight * live_mask
    negative_count = negatives.shape[0]
    grad_positive = -jax.nn.sigmoid(-positive) * scaled
    grad_negative = jax.nn.sigmoid(negative) * (scaled / negative_count)[:, None]
    grad_query = grad_positive[:, None] * targets + jnp.dot(
        grad_negative,
        negatives,
        precision=lax.Precision.HIGHEST,
        preferred_element_type=jnp.float32,
    )
    grad_target = grad_positive[:, None] * queries
    grad_drawn = jnp.dot(
        grad_negative.T,
        queries,
        precision=lax.Precision.HIGHEST,
        preferred_element_type=jnp.float32,
    )
    query_real, query_imag = (grad_query[:, :half_width], grad_query[:, half_width:])
    grad_source = jnp.concatenate(
        [
            query_real * factor_real + query_imag * factor_imag,
            query_imag * factor_real - query_real * factor_imag,
        ],
        axis=1,
    )
    grad_factor = jnp.concatenate(
        [
            query_real * source_real + query_imag * source_imag,
            query_imag * source_real - query_real * source_imag,
        ],
        axis=1,
    )
    return (grad_source, grad_target, grad_drawn, grad_factor)


def body(entities, relations, src_index, dst_index, rel_index, neg_index, counts, edge_weight):
    partner_bit = lax.axis_size("dom").bit_length() - 2
    partner_slice = partner(entities, "dom", partner_bit)
    source_rows, target_rows = (
        lax.all_gather(entities, "block", axis=0, tiled=True),
        lax.all_gather(partner_slice, "block", axis=0, tiled=True),
    )
    source_total = jnp.zeros(source_rows.shape, jnp.float32)
    target_total = jnp.zeros(target_rows.shape, jnp.float32)
    relation_total = jnp.zeros(relations.shape, jnp.float32)
    for which_block in range(src_index.shape[1]):
        source_ids = src_index[0, which_block]
        target_ids = dst_index[0, which_block]
        relation_ids = rel_index[0, which_block]
        negative_ids = neg_index[0, which_block]
        grad_source, grad_target, grad_drawn, grad_factor = block_gradients(
            source_rows,
            target_rows,
            relations,
            source_ids,
            target_ids,
            relation_ids,
            negative_ids,
            counts[0, which_block],
            edge_weight[0, which_block],
        )
        source_total = source_total.at[source_ids].add(grad_source)
        target_total = target_total.at[target_ids].add(grad_target).at[negative_ids].add(grad_drawn)
        relation_total = relation_total.at[relation_ids].add(grad_factor)
    relation_grad = lax.psum(relation_total, ("dom", "block"))
    owned_source, owned_target = (
        lax.psum_scatter(source_total, "block", scatter_dimension=0, tiled=True),
        lax.psum_scatter(target_total, "block", scatter_dimension=0, tiled=True),
    )
    returned = partner(owned_target, "dom", partner_bit)
    entity_grad = owned_source + returned
    return (entity_grad, relation_grad)


def solution(mesh):
    placed = (
        P(("dom", "block"), None),
        P(),
        P("dom", "block", None),
        P("dom", "block", None),
        P("dom", "block", None),
        P("dom", "block", None),
        P("dom", "block"),
        P("dom", "block", None),
    )
    return jax.shard_map(
        body,
        mesh=mesh,
        in_specs=placed,
        out_specs=(P(("dom", "block"), None), P()),
        check_vma=False,
    )
```

profile of v0, /device:TPU:0, one launch (start us, length us, event | category | flops | bytes accessed | tf_op | source)
XLA Modules:
  0.0 388.8 jit_solution(9108828632327441664)
XLA Ops:
  8.0 3.0 collective-permute-start
  11.0 32.1 %all_gather.6 = f32[256,400]{1,0:T(8,128)S(1)} all-gather(f32[32,400]{1,0:T(8,128)} %param.8), channel_id=1, replica_groups=mesh['dom'=4,'block'=8] {'block'}, dimensions={0}, use_global_device_ids=true | all-gather | bytes 460800 | tf_op jit(solution)/shard_map/all_gather | solution.py:86
  43.1 1.3 fusion.27
  44.5 0.8 compare_select_fusion.4
  45.3 0.8 compare_select_fusion.2
  46.0 0.8 compare_select_fusion.3
  46.8 1.3 fusion.26
  48.2 0.8 compare_select_fusion
  49.6 1.0 gather_fusion.4
  50.6 1.0 gather_fusion
  52.4 8.7 %copy.25 = f32[4096,400]{1,0:T(8,128)} copy(f32[4096,400]{0,1:T(8,128)} %param.9) | data formatting | bytes 13107200 | tf_op args[1]
  61.0 4.6 %gather_fusion.5 = f32[256,400]{1,0:T(8,128)S(1)} fusion(f32[4096,400]{1,0:T(8,128)} %copy.25, s32[1024]{0:T(1024)S(1)} %pad_clamp_fusion.1), kind=kCustom, calls=%fused_computation.5 | custom fusion | bytes 820224 | tf_op jit(solution)/shard_map/gather | solution.py:31
  65.6 4.6 %gather_fusion.1 = f32[256,400]{1,0:T(8,128)S(1)} fusion(f32[4096,400]{1,0:T(8,128)} %copy.25, s32[1024]{0:T(1024)S(1)} %pad_clamp_fusion.4), kind=kCustom, calls=%fused_computation.1 | custom fusion | bytes 820224 | tf_op jit(solution)/shard_map/gather | solution.py:31
  71.0 0.8 multiply_subtract_fusion.5
  71.9 0.8 multiply_subtract_fusion.3
  72.7 31.2 %all_gather.7 = f32[256,400]{1,0:T(8,128)S(1)} all-gather(f32[32,400]{1,0:T(8,128)S(1)} %collective-permute-done), channel_id=1, replica_groups=mesh['dom'=4,'block'=8] {'block'}, dimensions={0}, use_global_device_ids=true | all-gather | bytes 460800 | tf_op jit(solution)/shard_map/all_gather | solution.py:87
  103.9 1.0 gather_fusion.6
  105.1 1.0 gather_fusion.2
  106.2 3.5 gather_fusion.7
  109.7 5.0 %gather_fusion.3 = f32[1024,400]{1,0:T(8,128)} fusion(f32[256,400]{1,0:T(8,128)S(1)} %all_gather.7, s32[1024]{0:T(1024)S(1)} %broadcast_clamp_fusion.1), kind=kCustom, calls=%fused_computation.3 | custom fusion | bytes 3280896 | tf_op jit(solution)/shard_map/gather | solution.py:32
  114.8 1.1 multiply_reduce_fusion
  116.5 4.6 %fusion.9 = f32[256,1024]{1,0:T(8,128)S(1)} fusion(f32[1024,400]{1,0:T(8,128)S(1)} %gather_fusion.7, f32[256]{0:T(256)S(1)} %get-tuple-element.43, f32[256,200]{0,1:T(8,128)} %get-tuple-element.11, f32[256,200]{0,1:T(8,128)} %get-tuple-element.10), kind=kOutput, calls=%fused_computation.27 | convolution fusion | flops 1259442176 | bytes 3097600 | tf_op jit(solution)/shard_map/dot_general | solution.py:43
  121.2 3.5 fusion.14
  124.8 4.4 %broadcast_multiply_fusion = (f32[256,400]{0,1:T(8,128)}, f32[256,400]{0,1:T(8,128)}) fusion(f32[256]{0:T(256)S(1)} %get-tuple-element.42, f32[256,200]{0,1:T(8,128)S(1)} %copy-done.8, f32[256,200]{0,1:T(8,128)S(1)} %copy-done.7, f32[256,400]{0,1:T(8,128)S(1)} %copy.37, f32[256,1024]{1,0:T(8,128)S(1)} %fusion.9, f32[1024,400]{1,0:T(8,128)S(1)} %copy-done.4), kind=kOutput, calls=%fused_computation.48 | convolution fusion | flops 1258700800 | bytes 4326400 | tf_op jit(solution)/shard_map/dot_general | solution.py:51
  129.1 1.2 copy.42
  130.5 0.6 negate_multiply_fusion.1
  131.1 5.6 %fusion.6 = f32[256,1024]{1,0:T(8,128)S(1)} fusion(f32[1024,400]{1,0:T(8,128)} %gather_fusion.3, f32[256]{0:T(256)S(1)} %get-tuple-element.45, f32[256,200]{0,1:T(8,128)S(1)} %copy-done.6, f32[256,200]{0,1:T(8,128)S(1)} %copy-done.5), kind=kOutput, calls=%fused_computation.24 | convolution fusion | flops 1259442176 | bytes 3097600 | tf_op jit(solution)/shard_map/dot_general | solution.py:43
  136.7 4.9 %fusion.15 = f32[1024,400]{1,0:T(8,128)} fusion(f32[256,1024]{1,0:T(8,128)S(1)} %fusion.6, f32[256,200]{0,1:T(8,128)S(1)} %copy-done.6, f32[256,200]{0,1:T(8,128)S(1)} %copy-done.5), kind=kOutput, calls=%fused_computation.57 | convolution fusion | flops 1258393600 | bytes 3096576 | tf_op jit(solution)/shard_map/dot_general | solution.py:58
  141.6 4.4 %broadcast_multiply_fusion.1 = (f32[256,400]{0,1:T(8,128)}, f32[256,400]{0,1:T(8,128)}) fusion(f32[256]{0:T(256)S(1)} %get-tuple-element.44, f32[256,200]{0,1:T(8,128)S(1)} %copy-done.6, f32[256,200]{0,1:T(8,128)S(1)} %copy-done.5, f32[256,400]{0,1:T(8,128)S(1)} %copy.29, f32[256,1024]{1,0:T(8,128)S(1)} %fusion.6, f32[1024,400]{1,0:T(8,128)S(1)} %copy-done.2), kind=kOutput, calls=%fused_computation.53 | convolution fusion | flops 1258700800 | bytes 4326400 | tf_op jit(solution)/shard_map/dot_general | solution.py:51
  145.9 2.0 copy.40
  147.9 2.7 scatter_custom_fusion.2
  150.7 7.6 %scatter_fusion.1 = f32[256,400]{1,0:T(8,128)S(1)} fusion(f32[256,400]{1,0:T(8,128)S(1)} %scatter_custom_fusion.2, s32[1024]{0:T(1024)} %bitcast.39, f32[1024,400]{1,0:T(8,128)} %fusion.15), kind=kCustom, calls=%fused_computation.11 | custom fusion | flops 409600 | bytes 4919296 | tf_op jit(solution)/shard_map/scatter-add | solution.py:109
  158.3 2.3 scatter_fusion.2
  160.7 7.1 %scatter_fusion.3 = f32[256,400]{1,0:T(8,128)S(1)} fusion(f32[256,400]{1,0:T(8,128)S(1)} %scatter_fusion.2, s32[1024]{0:T(1024)} %bitcast.37, f32[1024,400]{1,0:T(8,128)S(1)} %fusion.14), kind=kCustom, calls=%fused_computation.13 | custom fusion | flops 409600 | bytes 4919296 | tf_op jit(solution)/shard_map/scatter-add | solution.py:109
  167.8 0.8 copy-done
  168.7 1.2 multiply_add_fusion.2
  170.3 0.7 copy-done.25
  171.4 2.3 scatter_custom_fusion
  173.8 2.3 scatter_fusion
  176.1 0.8 copy-done.1
  177.4 5.9 %scatter_custom_fusion.6 = f32[4096,400]{1,0:T(8,128)} fusion(s32[256]{0:T(256)} %bitcast.47, f32[256,400]{1,0:T(8,128)S(1)} %copy.44, f32[]{:T(128)} %constant.6.clone.1), kind=kCustom, calls=%fused_computation.16 | custom fusion | flops 102400 | bytes 6554112 | tf_op jit(solution)/shard_map/scatter-add | solution.py:110
  183.3 8.7 %scatter_fusion.4 = f32[4096,400]{1,0:T(8,128)} fusion(f32[4096,400]{1,0:T(8,128)} %scatter_custom_fusion.6, s32[256]{0:T(256)S(1)} %bitcast.41, f32[256,400]{1,0:T(8,128)S(1)} %copy.45), kind=kCustom, calls=%fused_computation.15 | custom fusion | flops 102400 | bytes 1229824 | tf_op jit(solution)/shard_map/scatter-add | solution.py:110
  192.0 50.9 %reduce-scatter.5.cloned.1.call-done = f32[32,400]{1,0:T(8,128)} async-done(((f32[256,400]{1,0:T(8,128)}), f32[32,400]{1,0:T(8,128)}) %reduce-scatter.5.cloned.1.call-update) | async-done | bytes 51216 | tf_op jit(solution)/shard_map/reduce_scatter | solution.py:114
  243.0 1.5 collective-permute-start.1
  244.5 65.3 %reduce-scatter.3.cloned.1.call-done = f32[32,400]{1,0:T(8,128)} async-done(((f32[256,400]{1,0:T(8,128)}), f32[32,400]{1,0:T(8,128)}) %reduce-scatter.3.cloned.1.call-update) | async-done | bytes 51216 | tf_op jit(solution)/shard_map/reduce_scatter | solution.py:113
  309.8 1.5 add.175
  311.3 61.3 %all-reduce.2.cloned.1.call-done = f32[4096,400]{1,0:T(8,128)} async-done(((f32[4096,400]{1,0:T(8,128)}), f32[4096,400]{1,0:T(8,128)}) %all-reduce.2.cloned.1.call-update) | async-done | bytes 6553616 | tf_op jit(solution)/shard_map/psum | solution.py:111
  372.6 8.5 %copy.46 = f32[4096,400]{0,1:T(8,128)} copy(f32[4096,400]{1,0:T(8,128)} %all-reduce.2.cloned.1.call-done) | data formatting | bytes 13107200
  (112 shorter events, 4.5 us)
Async XLA Ops:
  8.0 235.0 %reduce-scatter.5.cloned.1.call-start = ((), (), s32[]{:S(2)}) async-start(), calls=%async_computation.3 | async-start | bytes 589824 | tf_op jit(solution)/shard_map/reduce_scatter | solution.py:114
  8.0 64.7 %collective-permute-start = (f32[32,400]{1,0:T(8,128)}, f32[32,400]{1,0:T(8,128)S(1)}, u32[]{:S(2)}, u32[]{:S(2)}) collective-permute-start(f32[32,400]{1,0:T(8,128)} %param.8), channel_id=1, source_target_pairs={{0,16},{16,0},{8,24},{24,8},{1,17},{17,1},{9,25},{25,9},{2,18},{18... | collective-permute-start | bytes 153608 | tf_op jit(solution)/shard_map/ppermute | solution.py:14
  45.3 2.9 copy-start.35
  45.3 2.9 copy-start.30
  46.0 4.5 %copy-start.36 = (s32[256,1]{0,1:T(1,128)}, s32[256,1]{0,1:T(1,128)S(1)}, u32[]{:S(2)}) copy-start(s32[256,1]{0,1:T(1,128)S(1)} %get-tuple-element.31) | copy-start | bytes 3076
  46.0 26.6 %copy-start.32 = (s32[256,1]{0,1:T(1,128)}, s32[256,1]{0,1:T(1,128)S(1)}, u32[]{:S(2)}) copy-start(s32[256,1]{0,1:T(1,128)S(1)} %get-tuple-element.30) | copy-start | bytes 3076
  46.8 1.3 copy-start.34
  46.8 1.4 copy-start.28
  49.0 0.6 copy-start.26
  49.0 0.6 copy-start.27
  51.8 19.2 %copy-start.9 = (f32[256,200]{0,1:T(8,128)}, f32[256,200]{0,1:T(8,128)S(1)}, u32[]{:S(2)}) copy-start(f32[256,200]{0,1:T(8,128)S(1)} %copy.49) | copy-start | bytes 614404
  52.1 19.8 %copy-start.15 = (f32[256,200]{0,1:T(8,128)}, f32[256,200]{0,1:T(8,128)S(1)}, u32[]{:S(2)}) copy-start(f32[256,200]{0,1:T(8,128)S(1)} %copy.53) | copy-start | bytes 614404
  52.2 19.7 %copy-start.17 = (f32[256,200]{0,1:T(8,128)}, f32[256,200]{0,1:T(8,128)S(1)}, u32[]{:S(2)}) copy-start(f32[256,200]{0,1:T(8,128)S(1)} %copy.55) | copy-start | bytes 614404
  52.3 18.7 %copy-start.11 = (f32[256,200]{0,1:T(8,128)}, f32[256,200]{0,1:T(8,128)S(1)}, u32[]{:S(2)}) copy-start(f32[256,200]{0,1:T(8,128)S(1)} %copy.51) | copy-start | bytes 614404
  70.5 2.2 copy-start.13
  70.7 1.9 copy-start.21
  70.9 1.8 copy-start.23
  71.0 1.7 copy-start.19
  109.7 6.8 %copy-start.3 = (f32[1024,400]{1,0:T(8,128)}, f32[1024,400]{1,0:T(8,128)S(1)}, u32[]{:S(2)}) copy-start(f32[1024,400]{1,0:T(8,128)S(1)} %gather_fusion.7) | copy-start | bytes 4915204
  116.5 4.6 %copy-start.7 = (f32[256,200]{0,1:T(8,128)S(1)}, f32[256,200]{0,1:T(8,128)}, u32[]{:S(2)}) copy-start(f32[256,200]{0,1:T(8,128)} %get-tuple-element.10) | copy-start | bytes 614404
  116.5 4.6 %copy-start.8 = (f32[256,200]{0,1:T(8,128)S(1)}, f32[256,200]{0,1:T(8,128)}, u32[]{:S(2)}) copy-start(f32[256,200]{0,1:T(8,128)} %get-tuple-element.11) | copy-start | bytes 614404
  121.2 3.5 copy-start.4
  124.8 5.6 %copy-start.5 = (f32[256,200]{0,1:T(8,128)S(1)}, f32[256,200]{0,1:T(8,128)}, u32[]{:S(2)}) copy-start(f32[256,200]{0,1:T(8,128)} %get-tuple-element.14) | copy-start | bytes 614404
  124.8 5.6 %copy-start.6 = (f32[256,200]{0,1:T(8,128)S(1)}, f32[256,200]{0,1:T(8,128)}, u32[]{:S(2)}) copy-start(f32[256,200]{0,1:T(8,128)} %get-tuple-element.15) | copy-start | bytes 614404
  124.8 5.7 %copy-start.37 = (f32[1,1,256]{2,1,0:T(1,128)S(1)}, f32[1,1,256]{2,1,0:T(1,128)}, u32[]{:S(2)}) copy-start(f32[1,1,256]{2,1,0:T(1,128)} %get-tuple-element.33) | copy-start | bytes 3076
  136.7 4.9 %copy-start.2 = (f32[1024,400]{1,0:T(8,128)S(1)}, f32[1024,400]{1,0:T(8,128)}, u32[]{:S(2)}) copy-start(f32[1024,400]{1,0:T(8,128)} %gather_fusion.3) | copy-start | bytes 4915204
  150.7 7.7 %copy-start.33 = (s32[256,1]{0,1:T(1,128)S(1)}, s32[256,1]{0,1:T(1,128)}, u32[]{:S(2)}) copy-start(s32[256,1]{0,1:T(1,128)} %copy-done.32) | copy-start | bytes 3076
  160.7 8.0 %copy-start.16 = (f32[256,200]{0,1:T(8,128)S(1)}, f32[256,200]{0,1:T(8,128)}, u32[]{:S(2)}) copy-start(f32[256,200]{0,1:T(8,128)} %copy-done.15) | copy-start | bytes 614404
  160.7 8.0 %copy-start.18 = (f32[256,200]{0,1:T(8,128)S(1)}, f32[256,200]{0,1:T(8,128)}, u32[]{:S(2)}) copy-start(f32[256,200]{0,1:T(8,128)} %copy-done.17) | copy-start | bytes 614404
  160.7 8.0 %copy-start.22 = (f32[256,200]{0,1:T(8,128)S(1)}, f32[256,200]{0,1:T(8,128)}, u32[]{:S(2)}) copy-start(f32[256,200]{0,1:T(8,128)} %copy-done.21) | copy-start | bytes 614404
  160.7 8.0 %copy-start.24 = (f32[256,200]{0,1:T(8,128)S(1)}, f32[256,200]{0,1:T(8,128)}, u32[]{:S(2)}) copy-start(f32[256,200]{0,1:T(8,128)} %copy-done.23) | copy-start | bytes 614404
  167.8 0.8 copy-start
  168.6 141.2 %reduce-scatter.3.cloned.1.call-start = ((), (), s32[]{:S(2)}) async-start(), calls=%async_computation.2 | async-start | bytes 589824 | tf_op jit(solution)/shard_map/reduce_scatter | solution.py:113
  168.7 1.6 copy-start.10
  168.7 1.6 copy-start.12
  168.7 1.6 copy-start.14
  168.7 1.6 copy-start.20
  170.0 1.0 copy-start.25
  171.0 2.8 copy-start.31
  176.1 0.8 copy-start.1
  176.9 195.6 %all-reduce.2.cloned.1.call-start = ((), (), s32[]{:S(2)}) async-start(), calls=%async_computation.4 | async-start | bytes 16777216 | tf_op jit(solution)/shard_map/psum | solution.py:111
  177.4 5.9 %copy-start.29 = (s32[256,1]{0,1:T(1,128)S(1)}, s32[256,1]{0,1:T(1,128)}, u32[]{:S(2)}) copy-start(s32[256,1]{0,1:T(1,128)} %copy-done.28) | copy-start | bytes 3076
  243.0 66.8 %collective-permute-start.1 = (f32[32,400]{1,0:T(8,128)}, f32[32,400]{1,0:T(8,128)S(1)}, u32[]{:S(2)}, u32[]{:S(2)}) collective-permute-start(f32[32,400]{1,0:T(8,128)} %reduce-scatter.5.cloned.1.call-done), channel_id=1, source_target_pairs={{0,16},{16,0},{8,24},{24,8},{1,17},{17,1},{9,25},{25,9},{2,18},{18... | collective-permute-start | bytes 153608 | tf_op jit(solution)/shard_map/ppermute | solution.py:14
Sparse Core Ops, SparseCore 0:
  168.7 74.1 reduce-scatter.4
  247.3 62.5 reduce-scatter.2
Sparse Core Ops, SparseCore 1:
  192.1 180.4 all-reduce.1
where the time goes:
time: 395 us; the launch traced here: 389 us
  waiting for transfers between devices  178 us (45%)
  blocking collectives  63.3 us (16%)
  local copies, waits for them, and re-layouts  50.2 us (13%)
  other arithmetic  49.2 us (12%)
  matrix products  27.3 us (7%)
  between operations  16.5 us (4%)
  starting transfers between devices  4.64 us (1%)
    reduce_scatter x1, waiting for transfers between devices, body(): lax.psum_scatter(source_total, 'block', scatter_dimension=0, tiled=True)  65.3 us
    psum x1, waiting for transfers between devices, body(): relation_grad = lax.psum(relation_total, ('dom', 'block'))  61.3 us
    reduce_scatter x1, waiting for transfers between devices, body(): lax.psum_scatter(target_total, 'block', scatter_dimension=0, tiled=True)  50.9 us
    all_gather x1, blocking collectives, body(): lax.all_gather(entities, 'block', axis=0, tiled=True)  32.1 us
    all_gather x1, blocking collectives, body(): lax.all_gather(partner_slice, 'block', axis=0, tiled=True)  31.2 us
    unnamed x86, local copies, waits for them, and re-layouts  21.2 us
    scatter-add x4, other arithmetic, body(): target_total.at[target_ids].add(grad_target).at[negative_ids]  19.7 us
    scatter-add x2, other arithmetic, body(): relation_total = relation_total.at[relation_ids].add(grad_factor)  14.6 us
  transfers between devices with their start and end apart: 5, of which 3 were waited for; matrix products, arithmetic and copies ran while one was open for 13% of the time, Pallas kernels for 0%

commit v1 on v0

v1 whole, which is shorter than its diff:
```python
import functools

import jax
import jax.numpy as jnp
from jax import lax
from jax.experimental import pallas as pl
from jax.experimental.pallas import tpu as pltpu
from jax.sharding import PartitionSpec as P

LANES = 128
CHUNK = 128
LANE_TILES = 4
VMEM_BYTES = 58 * 1024 * 1024


def swap(x, axis, bit):
    count = lax.axis_size(axis)
    return lax.ppermute(x, axis, [(i, i ^ (1 << bit)) for i in range(count)])


def gather_all(x, stages):
    for axis, bit in stages:
        x = jnp.concatenate([x, swap(x, axis, bit)], axis=0)
    return x


def table_kernel(half, rel_ref, out_ref):
    width = LANE_TILES // 2 * LANES
    count = rel_ref.shape[1]
    for part in range(2):
        rows = rel_ref[part * half : (part + 1) * half, :]
        rows = jnp.concatenate([rows, jnp.zeros((width - half, count), jnp.float32)], axis=0)
        rows = rows.T
        for j in range(LANE_TILES // 2):
            out_ref[:, part * (LANE_TILES // 2) + j, :] = rows[:, j * LANES : (j + 1) * LANES]


def relation_table(relations):
    count, dim = relations.shape
    step = 512
    return pl.pallas_call(
        functools.partial(table_kernel, dim // 2),
        grid=(count // step,),
        in_specs=[pl.BlockSpec((dim, step), lambda i: (0, i))],
        out_specs=pl.BlockSpec((step, LANE_TILES, LANES), lambda i: (i, 0, 0)),
        out_shape=jax.ShapeDtypeStruct((count, LANE_TILES, LANES), jnp.float32),
        name="relation_table",
    )(relations.T)


def high_low(x):
    high = x.astype(jnp.bfloat16)
    return high, (x - high.astype(jnp.float32)).astype(jnp.bfloat16)


def dot(a, b):
    return jnp.dot(a, b, preferred_element_type=jnp.float32)


def spread(j, places):
    out = 0
    for bit, place in enumerate(places):
        out = out | (((j >> bit) & 1) << place)
    return out


def main_kernel(
    spec,
    rel_ids,
    live,
    where,
    table,
    first,
    second,
    counts_of,
    out_ref,
    ent_ref,
    *scratch,
):
    (half, rows, shards, blocks, edges, places_a, places_b, place_a, place_b) = spec
    accs = scratch[:-7]
    ent, both, high_t, low_t, factor, grads, mine = scratch[-7:]
    width = LANE_TILES // 2 * LANES
    part_rows = rows * shards
    me, side = where[0], where[1]

    def clear(i, carry):
        at = pl.ds(i * 8, 8)
        for acc in accs:
            acc[at] = jnp.zeros((8,) + acc.shape[1:], jnp.float32)
        return carry

    lax.fori_loop(0, accs[0].shape[0] // 8, clear, 0)
    mine[...] = jnp.zeros_like(mine)

    for x in range(2):
        for j in range(shards):
            ka = spread(j, places_a) | (x << place_a)
            kb = spread(j, places_b) | (x << place_b)
            at = pl.ds(pl.multiple_of((j ^ me) * rows, 8), rows)
            ent[x, at, :width] = first[ka, :rows, :]
            ent[x, at, width:] = second[kb, :rows, :]
        whole = ent[x]
        high, low = high_low(whole)
        both[x, :, : 2 * width] = high
        both[x, :, 2 * width :] = low
        high, low = high_low(whole.T)
        high_t[x] = high
        low_t[x] = low

    own = me * rows

    def block(t, carry):
        bucket, rest = t // (shards * blocks), t % (shards * blocks)
        shard, slot = rest // blocks, rest % blocks
        x = bucket ^ side
        j = shard ^ me
        ka = spread(j, places_a) | (x << place_a)
        kb = spread(j, places_b) | (x << place_b)
        count = live[kb * blocks + slot]

        def chunk(s, carry):
            base = s * CHUNK
            id_base = (ka * blocks + slot) * edges + base

            def fetch(g, carry):
                for u in range(8):
                    e = g * 8 + u
                    factor[e] = table[rel_ids[id_base + e]]
                return carry

            lax.fori_loop(0, CHUNK // 8, fetch, 0)

            at = pl.ds(pl.multiple_of(base, CHUNK), CHUNK)
            tile = first[ka, pl.ds(rows, 4 * blocks), at]

            def chosen(k):
                row = tile[k * blocks : k * blocks + 1]
                for i in range(1, blocks):
                    row = jnp.where(slot == i, tile[k * blocks + i : k * blocks + i + 1], row)
                return row

            infos = [chosen(0), chosen(1), chosen(3)]
            source_row = infos[0].astype(jnp.int32)
            columns = jnp.concatenate(infos + [jnp.zeros((5, CHUNK), jnp.float32)], axis=0).T
            source_col = columns[:, 0:1].astype(jnp.int32)
            target_col = columns[:, 1:2].astype(jnp.int32)
            weight_col = columns[:, 2:3]

            lane = lax.broadcasted_iota(jnp.int32, (CHUNK, part_rows), 1)
            pick = jnp.where(source_col == lane, 1.0, 0.0).astype(jnp.bfloat16)
            sources = dot(pick, both[x])
            sources = sources[:, : 2 * width] + sources[:, 2 * width :]
            s_re, s_im = sources[:, :width], sources[:, width:]
            w = [factor[:, q, :] for q in range(LANE_TILES)]
            w_re, w_im = jnp.concatenate(w[:2], axis=1), jnp.concatenate(w[2:], axis=1)
            queries = jnp.concatenate([s_re * w_re - s_im * w_im, s_re * w_im + s_im * w_re], axis=1)
            q_high, q_low = high_low(queries)
            scores = dot(q_high, high_t[1 - x]) + (dot(q_high, low_t[1 - x]) + dot(q_low, high_t[1 - x]))

            small = jnp.exp(-jnp.abs(scores))
            near = 1.0 / (1.0 + small)
            far = small * near
            up = scores >= 0.0
            sig = jnp.where(up, near, far)
            sig_neg = jnp.where(up, far, near)
            g = sig * counts_of[kb * blocks + slot] - jnp.where(target_col == lane, sig_neg, 0.0)
            g = g * weight_col
            g_high, g_low = high_low(g)
            gq = dot(g_high, both[1 - x])
            gq = gq[:, : 2 * width] + (gq[:, 2 * width :] + dot(g_low, both[1 - x, :, : 2 * width]))
            g_re, g_im = gq[:, :width], gq[:, width:]
            gw = [g_re * s_re + g_im * s_im, g_im * s_re - g_re * s_im]
            for q in range(LANE_TILES):
                grads[:, q, :] = gw[q // 2][:, (q % 2) * LANES : (q % 2 + 1) * LANES]

            @pl.when(x == 0)
            def _():
                gs = jnp.concatenate([g_re * w_re + g_im * w_im, g_im * w_re - g_re * w_im], axis=1)
                sub = lax.broadcasted_iota(jnp.int32, (rows, CHUNK), 0)
                back = jnp.where(source_row - own == sub, 1.0, 0.0).astype(jnp.bfloat16)
                s_high, s_low = high_low(gs)
                mine[...] += dot(back, s_high) + dot(back, s_low)

            @pl.when(x == 1)
            def _():
                flipped = scratch_rows(g, own)
                f_high, f_low = high_low(flipped)
                mine[...] += dot(f_high, q_high) + (dot(f_high, q_low) + dot(f_low, q_high))

            groups = (jnp.minimum(count - base, CHUNK) + 7) // 8

            def push(n, carry):
                for u in range(8):
                    e = n * 8 + u
                    r = rel_ids[id_base + e]
                    acc = accs[u % len(accs)]
                    acc[r] = acc[r] + grads[e]
                return carry

            lax.fori_loop(0, groups, push, 0)
            return carry

        def scratch_rows(g, own):
            select = jnp.where(
                lax.broadcasted_iota(jnp.int32, (part_rows, LANES), 0)
                == own + lax.broadcasted_iota(jnp.int32, (part_rows, LANES), 1),
                1.0,
                0.0,
            ).astype(jnp.bfloat16)
            high, low = high_low(g)
            picked = dot(high, select) + dot(low, select)
            return picked.T[:rows]

        return lax.fori_loop(0, (count + CHUNK - 1) // CHUNK, chunk, carry)

    lax.fori_loop(0, 2 * shards * blocks, block, 0)

    ent_ref[:, :half] = mine[:, :half]
    ent_ref[:, half:] = mine[:, width : width + half]

    def finish(i, carry):
        at = pl.ds(pl.multiple_of(i * LANES, LANES), LANES)
        for q in range(LANE_TILES):
            total = accs[0][at, q, :]
            for acc in accs[1:]:
                total = total + acc[at, q, :]
            low = (q // 2) * half + (q % 2) * LANES
            size = min(LANES, half - (q % 2) * LANES)
            out_ref[low : low + size, at] = total.T[:size]
        return carry

    lax.fori_loop(0, out_ref.shape[1] // LANES, finish, 0)


def body(entities, relations, src_index, dst_index, rel_index, neg_index, counts, edge_weight):
    rows, dim = entities.shape
    half = dim // 2
    width = LANE_TILES // 2 * LANES
    relation_count = relations.shape[0]
    blocks, edges = src_index.shape[1:]
    dom_count, shards = lax.axis_size("dom"), lax.axis_size("block")
    part_rows = rows * shards
    partner_bit = dom_count.bit_length() - 2
    block_bits = shards.bit_length() - 1
    other_bits = [bit for bit in range(dom_count.bit_length() - 1) if bit != partner_bit]

    table = relation_table(relations)

    real = jnp.pad(entities[:, :half], ((0, 0), (0, width - half)))
    imag = jnp.pad(entities[:, half:], ((0, 0), (0, width - half)))
    alive = jnp.arange(edges, dtype=jnp.int32)[None, :] < counts[0][:, None]
    weight = edge_weight[0] * alive.astype(jnp.float32)
    entity_ids = jnp.arange(part_rows, dtype=jnp.int32)
    times = jnp.sum((neg_index[0][:, :, None] == entity_ids).astype(jnp.float32), axis=1)
    times = times / neg_index.shape[2]
    ids = jnp.concatenate([src_index[0], dst_index[0], rel_index[0]], axis=0).astype(jnp.float32)
    info_a = jnp.concatenate([ids, weight], axis=0).reshape(-1, width)
    live_row = jnp.pad(counts[0].astype(jnp.float32)[None, :], ((0, 0), (0, width - blocks)))
    times_rows = blocks * part_rows // width
    info_b = jnp.concatenate([times.reshape(-1, width), live_row], axis=0)
    info_b = jnp.pad(info_b, ((0, -info_b.shape[0] % 8), (0, 0)))

    upper = [("block", bit) for bit in reversed(range(1, block_bits))]
    stages_a = upper + [("dom", partner_bit), ("block", 0)]
    stages_b = upper + [("block", 0), ("dom", partner_bit)]
    first = gather_all(jnp.concatenate([real, info_a], axis=0)[None], stages_a)
    second = gather_all(jnp.concatenate([imag, info_b], axis=0)[None], stages_b)
    places_a = tuple(stages_a.index(("block", bit)) for bit in range(block_bits))
    places_b = tuple(stages_b.index(("block", bit)) for bit in range(block_bits))
    place_a, place_b = stages_a.index(("dom", partner_bit)), stages_b.index(("dom", partner_bit))

    id_rows = blocks * edges // width
    rel_ids = first[:, rows + 2 * id_rows : rows + 3 * id_rows, :].astype(jnp.int32).reshape(-1)
    live = second[:, rows + times_rows, :blocks].astype(jnp.int32).reshape(-1)
    times_all = second[:, rows : rows + times_rows, :].reshape(-1, 1, part_rows)
    where = jnp.stack([lax.axis_index("block"), (lax.axis_index("dom") >> partner_bit) & 1]).astype(jnp.int32)

    sums = 4 if part_rows <= 256 else 2
    spec = (half, rows, shards, blocks, edges, places_a, places_b, place_a, place_b)
    smem = pl.BlockSpec(memory_space=pltpu.SMEM)
    vmem = pl.BlockSpec(memory_space=pltpu.VMEM)
    relation_part, entity_grad = pl.pallas_call(
        functools.partial(main_kernel, spec),
        in_specs=[smem, smem, smem, vmem, vmem, vmem, vmem],
        out_specs=(vmem, vmem),
        out_shape=(
            jax.ShapeDtypeStruct((dim, relation_count), jnp.float32),
            jax.ShapeDtypeStruct((rows, dim), jnp.float32),
        ),
        scratch_shapes=[pltpu.VMEM((relation_count, LANE_TILES, LANES), jnp.float32)] * sums
        + [
            pltpu.VMEM((2, part_rows, 2 * width), jnp.float32),
            pltpu.VMEM((2, part_rows, 4 * width), jnp.bfloat16),
            pltpu.VMEM((2, 2 * width, part_rows), jnp.bfloat16),
            pltpu.VMEM((2, 2 * width, part_rows), jnp.bfloat16),
            pltpu.VMEM((CHUNK, LANE_TILES, LANES), jnp.float32),
            pltpu.VMEM((CHUNK, LANE_TILES, LANES), jnp.float32),
            pltpu.VMEM((rows, 2 * width), jnp.float32),
        ],
        compiler_params=pltpu.CompilerParams(vmem_limit_bytes=VMEM_BYTES),
        name="gradients",
    )(rel_ids, live, where, table, first, second, times_all)

    for bit in other_bits:
        relation_part = relation_part + swap(relation_part, "dom", bit)
    return entity_grad, relation_part.T


def solution(mesh):
    placed = (
        P(("dom", "block"), None),
        P(),
        P("dom", "block", None),
        P("dom", "block", None),
        P("dom", "block", None),
        P("dom", "block", None),
        P("dom", "block"),
        P("dom", "block", None),
    )
    return jax.shard_map(
        body,
        mesh=mesh,
        in_specs=placed,
        out_specs=(P(("dom", "block"), None), P()),
        check_vma=False,
    )
```

time: 395 us -> 175 us (0.44); the launches traced: 389 us -> 174 us
  waiting for transfers between devices: 178 us -> 22.7 us
  Pallas kernels: 0 us -> 124 us
  blocking collectives: 63.3 us -> 0 us
  local copies, waits for them, and re-layouts: 50.2 us -> 3.16 us
  other arithmetic: 49.2 us -> 11.5 us
  matrix products: 27.3 us -> 0 us
  between operations: 16.5 us -> 0.77 us
  starting transfers between devices: 4.64 us -> 12.1 us
    pallas_call x0 -> x2, Pallas kernels: none -> 124 us  [the longest x1 114 us: body(): pl.pallas_call(functools.partial(main_kernel, spec), in_specs=[smem, smem...]
    reduce_scatter x2 -> x0, waiting for transfers between devices: 116 us -> none  [the longest x1 65.3 us: body(): lax.psum_scatter(source_total, 'block', scatter_dimension=0, tiled=True)]
    all_gather x2 -> x0, blocking collectives: 63.3 us -> none  [the longest x1 32.1 us: body(): lax.all_gather(entities, 'block', axis=0, tiled=True)]
    psum x1 -> x0, waiting for transfers between devices: 61.3 us -> none  [body(): relation_grad = lax.psum(relation_total, ('dom', 'block'))]
    scatter-add x8 -> x0, other arithmetic: 39 us -> none  [the longest x4 19.7 us: body(): target_total.at[target_ids].add(grad_target).at[negative_ids]]
    dot_general x6 -> x0, matrix products: 27.3 us -> none  [the longest x2 10.2 us: block_gradients(): jnp.dot(queries, negatives.T, precision=lax.Precision.HIGHEST, preferred_...]
    ppermute x2 -> x9, waiting for transfers between devices: 0.01 us -> 22.7 us  [swap(): return lax.ppermute(x, axis, [(i, i ^ 1 << bit) for i in range(count)])]
    gather x10 -> x0, local copies, waits for them, and re-layouts: 21.9 us -> none  [the longest x2 9.18 us: block_gradients(): factors = relations[relation_ids]]
  transfers between devices with their start and end apart: 5 -> 9, of which waited for: 3 -> 6; matrix products, arithmetic and copies ran while one was open for 13% -> 3% of each run, Pallas kernels for 0% -> 6%
where the time goes in v1:
time: 175 us; the launch traced here: 174 us
  Pallas kernels  124 us (71%)
  waiting for transfers between devices  22.7 us (13%)
  starting transfers between devices  12.1 us (7%)
  other arithmetic  11.5 us (7%)
  local copies, waits for them, and re-layouts  3.16 us (2%)
    pallas_call x1, Pallas kernels, body(): pl.pallas_call(functools.partial(main_kernel, spec), in_specs=[smem, smem...  114 us
    ppermute x9, waiting for transfers between devices, swap(): return lax.ppermute(x, axis, [(i, i ^ 1 << bit) for i in range(count)])  22.7 us
    ppermute x9, starting transfers between devices, swap(): return lax.ppermute(x, axis, [(i, i ^ 1 << bit) for i in range(count)])  12.1 us
    pallas_call x1, Pallas kernels, relation_table(): pl.pallas_call(functools.partial(table_kernel, dim // 2), grid=(count //...  10.1 us
    transpose x1, other arithmetic, body(): return (entity_grad, relation_part.T)  6.68 us
  transfers between devices with their start and end apart: 9, of which 6 were waited for; matrix products, arithmetic and copies ran while one was open for 3% of the time, Pallas kernels for 6%

profile of v1, /device:TPU:0, one launch (start us, length us, event | category | flops | bytes accessed | tf_op | source)
XLA Modules:
  0.0 174.2 jit_solution(3146753721958789128)
XLA Ops:
  0.6 0.7 convert_element_type.31
  1.3 1.0 convert_reduce_fusion
  2.3 0.9 slice.18
  3.3 4.1 %collective-permute-start.4 = (f32[1,40,256]{2,1,0:T(8,128)S(1)}, f32[1,40,256]{2,1,0:T(8,128)S(1)}, u32[]{:S(2)}, u32[]{:S(2)}) collective-permute-start(f32[1,40,256]{2,1,0:T(8,128)S(1)} %fusion), channel_id=1, source_target_pairs={{0,4},{1,5},{2,6},{3,7},{4,0},{5,1},{6,2},{7,3},{8,12},{9,13},{10,... | collective-permute-start | bytes 122888 | tf_op jit(solution)/shard_map/ppermute | solution.py:18
  7.4 0.8 slice_select_fusion
  8.1 0.8 compare_select_fusion
  8.9 0.7 add_convert_fusion
  9.6 0.1 collective-permute-start
  9.7 0.7 pad_add_fusion.where
  10.4 10.1 %relation_table.1.table = f32[4096,4,128]{2,1,0:T(4,128)} custom-call(f32[400,4096]{1,0:T(8,128)} %bitcast.22), custom_call_target="tpu_custom_call" | custom-call | tf_op jit(solution)/shard_map/relation_table/pallas_call | solution.py:41
  20.5 0.0 collective-permute-done.4
  20.5 1.9 %collective-permute-start.5 = (f32[2,40,256]{2,1,0:T(8,128)S(1)}, f32[2,40,256]{2,1,0:T(8,128)S(1)}, u32[]{:S(2)}, u32[]{:S(2)}) collective-permute-start(f32[2,40,256]{2,1,0:T(8,128)S(1)} %pad_maximum_fusion.5), channel_id=1, source_target_pairs={{0,2},{1,3},{2,0},{3,1},{4,6},{5,7},{6,4},{7,5},{8,10},{9,11},{10,... | collective-permute-start | bytes 245768 | tf_op jit(solution)/shard_map/ppermute | solution.py:18
  22.4 0.0 collective-permute-done
  22.4 0.2 collective-permute-start.1
  22.7 3.2 %collective-permute-done.5 = f32[2,40,256]{2,1,0:T(8,128)S(1)} collective-permute-done((f32[2,40,256]{2,1,0:T(8,128)S(1)}, f32[2,40,256]{2,1,0:T(8,128)S(1)}, u32[]{:S(2)}, u32[]{:S(2)}) %collective-permute-start.5) | collective-permute-done | bytes 81952 | tf_op jit(solution)/shard_map/ppermute | solution.py:18
  25.9 1.6 collective-permute-start.6
  27.4 0.0 collective-permute-done.1
  27.5 1.6 collective-permute-start.2
  29.0 2.2 %collective-permute-done.6 = f32[4,40,256]{2,1,0:T(8,128)S(1)} collective-permute-done((f32[4,40,256]{2,1,0:T(8,128)S(1)}, f32[4,40,256]{2,1,0:T(8,128)S(1)}, u32[]{:S(2)}, u32[]{:S(2)}) %collective-permute-start.6) | collective-permute-done | bytes 163872 | tf_op jit(solution)/shard_map/ppermute | solution.py:18
  31.3 1.6 collective-permute-start.7
  32.8 1.8 %collective-permute-done.2 = f32[4,40,256]{2,1,0:T(8,128)S(1)} collective-permute-done((f32[4,40,256]{2,1,0:T(8,128)S(1)}, f32[4,40,256]{2,1,0:T(8,128)S(1)}, u32[]{:S(2)}, u32[]{:S(2)}) %collective-permute-start.2) | collective-permute-done | bytes 163872 | tf_op jit(solution)/shard_map/ppermute | solution.py:18
  34.7 1.0 collective-permute-start.3
  35.7 3.4 %collective-permute-done.7 = f32[8,40,256]{2,1,0:T(8,128)S(1)} collective-permute-done((f32[8,40,256]{2,1,0:T(8,128)S(1)}, f32[8,40,256]{2,1,0:T(8,128)S(1)}, u32[]{:S(2)}, u32[]{:S(2)}) %collective-permute-start.7) | collective-permute-done | bytes 327712 | tf_op jit(solution)/shard_map/ppermute | solution.py:18
  39.2 0.0 copy-start
  39.2 0.7 convert_element_type.33.live
  39.9 0.7 reshape.16.counts_of
  40.6 1.3 collective-permute-done.3
  41.9 0.0 copy-start.1
  41.9 0.8 copy.10
  42.7 0.0 copy-done
  42.7 0.1 copy-done.1
  42.8 114.0 %gradients.1 = (f32[400,4096]{1,0:T(8,128)}, f32[32,400]{1,0:T(8,128)}) custom-call(s32[8192]{0:T(1024)} %bitcast.23, s32[32]{0:T(128)} %convert_element_type.33.live, s32[2]{0:T(128)} %pad_add_fusion.where, f32[4096,4,128]{2,1,0:T(4,128)} %relation_table.1.table, f32[16,40,256]{2,1,0:T(8,128)} %copy-done.1, f32[16,40,256]{2,1,0:T(8,128)} %copy-done, ...), custom_call_target="tpu_custom_call" | custom-call | tf_op jit(solution)/shard_map/gradients/pallas_call | solution.py:283
  156.7 0.0 collective-permute-start.8
  156.7 10.7 %collective-permute-done.8 = f32[400,4096]{1,0:T(8,128)S(1)} collective-permute-done((f32[400,4096]{1,0:T(8,128)}, f32[400,4096]{1,0:T(8,128)S(1)}, u32[]{:S(2)}, u32[]{:S(2)}) %collective-permute-start.8) | collective-permute-done | bytes 6553632 | tf_op jit(solution)/shard_map/ppermute | solution.py:18
  167.5 6.7 %add_bitcast_fusion = f32[4096,400]{0,1:T(8,128)} fusion(f32[400,4096]{1,0:T(8,128)} %get-tuple-element.5, f32[400,4096]{1,0:T(8,128)S(1)} %collective-permute-done.8), kind=kLoop, calls=%fused_computation | loop fusion | flops 1638400 | bytes 19660800 | tf_op jit(solution)/shard_map/transpose | solution.py:307
  (22 shorter events, 0.3 us)
Async XLA Ops:
  3.3 17.2 %collective-permute-start.4 = (f32[1,40,256]{2,1,0:T(8,128)S(1)}, f32[1,40,256]{2,1,0:T(8,128)S(1)}, u32[]{:S(2)}, u32[]{:S(2)}) collective-permute-start(f32[1,40,256]{2,1,0:T(8,128)S(1)} %fusion), channel_id=1, source_target_pairs={{0,4},{1,5},{2,6},{3,7},{4,0},{5,1},{6,2},{7,3},{8,12},{9,13},{10,... | collective-permute-start | bytes 122888 | tf_op jit(solution)/shard_map/ppermute | solution.py:18
  9.6 12.8 %collective-permute-start = (f32[1,40,256]{2,1,0:T(8,128)S(1)}, f32[1,40,256]{2,1,0:T(8,128)S(1)}, u32[]{:S(2)}, u32[]{:S(2)}) collective-permute-start(f32[1,40,256]{2,1,0:T(8,128)S(1)} %get-tuple-element.7), channel_id=1, source_target_pairs={{0,4},{1,5},{2,6},{3,7},{4,0},{5,1},{6,2},{7,3},{8,12},{9,13},{10,... | collective-permute-start | bytes 122888 | tf_op jit(solution)/shard_map/ppermute | solution.py:18
  20.5 5.4 %collective-permute-start.5 = (f32[2,40,256]{2,1,0:T(8,128)S(1)}, f32[2,40,256]{2,1,0:T(8,128)S(1)}, u32[]{:S(2)}, u32[]{:S(2)}) collective-permute-start(f32[2,40,256]{2,1,0:T(8,128)S(1)} %pad_maximum_fusion.5), channel_id=1, source_target_pairs={{0,2},{1,3},{2,0},{3,1},{4,6},{5,7},{6,4},{7,5},{8,10},{9,11},{10,... | collective-permute-start | bytes 245768 | tf_op jit(solution)/shard_map/ppermute | solution.py:18
  22.4 5.0 %collective-permute-start.1 = (f32[2,40,256]{2,1,0:T(8,128)S(1)}, f32[2,40,256]{2,1,0:T(8,128)S(1)}, u32[]{:S(2)}, u32[]{:S(2)}) collective-permute-start(f32[2,40,256]{2,1,0:T(8,128)S(1)} %pad_maximum_fusion.4), channel_id=1, source_target_pairs={{0,2},{1,3},{2,0},{3,1},{4,6},{5,7},{6,4},{7,5},{8,10},{9,11},{10,... | collective-permute-start | bytes 245768 | tf_op jit(solution)/shard_map/ppermute | solution.py:18
  25.9 5.4 %collective-permute-start.6 = (f32[4,40,256]{2,1,0:T(8,128)S(1)}, f32[4,40,256]{2,1,0:T(8,128)S(1)}, u32[]{:S(2)}, u32[]{:S(2)}) collective-permute-start(f32[4,40,256]{2,1,0:T(8,128)S(1)} %pad_maximum_fusion.3), channel_id=1, source_target_pairs={{0,1},{1,0},{2,3},{3,2},{4,5},{5,4},{6,7},{7,6},{8,9},{9,8},{10,11... | collective-permute-start | bytes 491528 | tf_op jit(solution)/shard_map/ppermute | solution.py:18
  27.5 7.2 %collective-permute-start.2 = (f32[4,40,256]{2,1,0:T(8,128)S(1)}, f32[4,40,256]{2,1,0:T(8,128)S(1)}, u32[]{:S(2)}, u32[]{:S(2)}) collective-permute-start(f32[4,40,256]{2,1,0:T(8,128)S(1)} %pad_maximum_fusion.2), channel_id=1, source_target_pairs={{0,16},{8,24},{16,0},{24,8},{1,17},{9,25},{17,1},{25,9},{2,18},{10... | collective-permute-start | bytes 491528 | tf_op jit(solution)/shard_map/ppermute | solution.py:18
  31.3 7.9 %collective-permute-start.7 = (f32[8,40,256]{2,1,0:T(8,128)S(1)}, f32[8,40,256]{2,1,0:T(8,128)S(1)}, u32[]{:S(2)}, u32[]{:S(2)}) collective-permute-start(f32[8,40,256]{2,1,0:T(8,128)S(1)} %pad_maximum_fusion.1), channel_id=1, source_target_pairs={{0,16},{8,24},{16,0},{24,8},{1,17},{9,25},{17,1},{25,9},{2,18},{10... | collective-permute-start | bytes 983048 | tf_op jit(solution)/shard_map/ppermute | solution.py:18
  34.7 7.1 %collective-permute-start.3 = (f32[8,40,256]{2,1,0:T(8,128)S(1)}, f32[8,40,256]{2,1,0:T(8,128)S(1)}, u32[]{:S(2)}, u32[]{:S(2)}) collective-permute-start(f32[8,40,256]{2,1,0:T(8,128)S(1)} %pad_maximum_fusion), channel_id=1, source_target_pairs={{0,1},{1,0},{2,3},{3,2},{4,5},{5,4},{6,7},{7,6},{8,9},{9,8},{10,11... | collective-permute-start | bytes 983048 | tf_op jit(solution)/shard_map/ppermute | solution.py:18
  39.2 3.5 %copy-start = (f32[16,40,256]{2,1,0:T(8,128)}, f32[16,40,256]{2,1,0:T(8,128)S(1)}, u32[]{:S(2)}) copy-start(f32[16,40,256]{2,1,0:T(8,128)S(1)} %constant_dynamic-update-slice_fusion.5.second) | copy-start | bytes 1966084
  41.9 0.9 copy-start.1
  156.7 10.7 %collective-permute-start.8 = (f32[400,4096]{1,0:T(8,128)}, f32[400,4096]{1,0:T(8,128)S(1)}, u32[]{:S(2)}, u32[]{:S(2)}) collective-permute-start(f32[400,4096]{1,0:T(8,128)} %get-tuple-element.5), channel_id=1, source_target_pairs={{0,8},{8,0},{16,24},{24,16},{1,9},{9,1},{17,25},{25,17},{2,10},{10... | collective-permute-start | bytes 19660808 | tf_op jit(solution)/shard_map/ppermute | solution.py:18

commit v2 on v1

v2 whole, which is shorter than its diff:
```python
import functools

import jax
import jax.numpy as jnp
from jax import lax
from jax.experimental import pallas as pl
from jax.experimental.pallas import tpu as pltpu
from jax.sharding import PartitionSpec as P

LANES = 128
CHUNK = 256
LANE_TILES = 4
VMEM_BYTES = 58 * 1024 * 1024


def swap(x, axis, bit):
    count = lax.axis_size(axis)
    return lax.ppermute(x, axis, [(i, i ^ (1 << bit)) for i in range(count)])


def gather_all(x, stages):
    for axis, bit in stages:
        x = jnp.concatenate([x, swap(x, axis, bit)], axis=0)
    return x


def table_kernel(half, rel_ref, out_ref):
    width = LANE_TILES // 2 * LANES
    count = rel_ref.shape[1]
    flat = out_ref.reshape(count * LANE_TILES, LANES)
    for part in range(2):
        rows = rel_ref[part * half : (part + 1) * half, :]
        rows = jnp.concatenate([rows, jnp.zeros((width - half, count), jnp.float32)], axis=0)
        rows = rows.T
        for j in range(LANE_TILES // 2):
            at = pl.ds(part * (LANE_TILES // 2) + j, count, stride=LANE_TILES)
            flat[at, :] = rows[:, j * LANES : (j + 1) * LANES]


def relation_table(relations):
    count, dim = relations.shape
    step = 512
    return pl.pallas_call(
        functools.partial(table_kernel, dim // 2),
        grid=(count // step,),
        in_specs=[pl.BlockSpec((dim, step), lambda i: (0, i))],
        out_specs=pl.BlockSpec((step, LANE_TILES, LANES), lambda i: (i, 0, 0)),
        out_shape=jax.ShapeDtypeStruct((count, LANE_TILES, LANES), jnp.float32),
        name="relation_table",
    )(relations.T)


def high_low(x):
    high = x.astype(jnp.bfloat16)
    return high, (x - high.astype(jnp.float32)).astype(jnp.bfloat16)


def dot(a, b):
    return jnp.dot(a, b, preferred_element_type=jnp.float32)


def spread(j, places):
    out = 0
    for bit, place in enumerate(places):
        out = out | (((j >> bit) & 1) << place)
    return out


def tiles(ref, low, count, q):
    flat = ref.reshape(ref.shape[0] * ref.shape[1], LANES)
    return flat[pl.ds(low * LANE_TILES + q, count, stride=LANE_TILES), :]


def main_kernel(
    spec,
    live,
    where,
    table,
    first,
    second,
    counts_of,
    out_ref,
    ent_ref,
    *scratch,
):
    (half, rows, shards, blocks, edges, places_a, places_b, place_a, place_b) = spec
    accs = scratch[:-12]
    (ent, stack, stack_t, times, info, ids_v, ids, factor, grads, flip, mine, seg) = scratch[-12:]
    width = LANE_TILES // 2 * LANES
    part_rows = rows * shards
    group = shards * blocks
    total = group * edges // 2
    relation_count = out_ref.shape[1]
    me, side = where[0], where[1]
    own = me * rows

    def clear(i, carry):
        at = pl.ds(i * 8, 8)
        for acc in accs:
            acc[at] = jnp.zeros((8,) + acc.shape[1:], jnp.float32)
        return carry

    lax.fori_loop(0, relation_count // 8, clear, 0)
    mine[...] = jnp.zeros_like(mine)
    info[...] = jnp.zeros_like(info)

    for x in range(2):
        for j in range(shards):
            ka = spread(j, places_a) | (x << place_a)
            kb = spread(j, places_b) | (x << place_b)
            at = pl.ds(pl.multiple_of((j ^ me) * rows, 8), rows)
            ent[at, :width] = first[ka, :rows, :]
            ent[at, width:] = second[kb, :rows, :]
        whole = ent[...]
        high, low = high_low(whole)
        stack[x] = jnp.concatenate([high, low, high], axis=0)
        high, low = high_low(whole.T)
        stack_t[x] = jnp.concatenate([high, low, high], axis=0)

    def place(n, x):
        j = (n // blocks) ^ me
        ka = spread(j, places_a) | (x << place_a)
        kb = spread(j, places_b) | (x << place_b)
        return ka, kb, n % blocks

    for x in range(2):
        rows_of = []
        for n in range(group):
            ka, kb, slot = place(n, x)
            rows_of.append(counts_of[kb * blocks + slot])
        high, low = high_low(jnp.concatenate(rows_of, axis=0))
        times[x] = jnp.concatenate([high, low], axis=0)

        def lay(n, offset):
            ka, kb, slot = place(n, x)
            count = live[kb * blocks + slot]
            tile = first[ka, pl.ds(rows, 4 * blocks), :]

            def chosen(k):
                row = tile[k * blocks : k * blocks + 1]
                for i in range(1, blocks):
                    row = jnp.where(slot == i, tile[k * blocks + i : k * blocks + i + 1], row)
                return row

            number = jnp.zeros((1, edges), jnp.float32) + n.astype(jnp.float32)
            data = [chosen(k) for k in range(4)] + [number, jnp.zeros((3, edges), jnp.float32)]
            data = jnp.concatenate(data, axis=0)
            data = jnp.where(lax.broadcasted_iota(jnp.int32, data.shape, 1) < count, data, 0.0)
            data = jnp.concatenate([data, jnp.zeros((8, LANES), jnp.float32)], axis=1)
            data = pltpu.roll(data, offset % LANES, 1)
            at = pl.ds(pl.multiple_of((offset // LANES) * LANES, LANES), edges + LANES)
            info[x, :, at] = info[x, :, at] + data
            return offset + count

        lax.fori_loop(0, group, lay, jnp.int32(0))
        for i in range(total // LANES):
            ids_v[x, i : i + 1, :] = info[x, 2:3, i * LANES : (i + 1) * LANES].astype(jnp.int32)

    move = pltpu.make_async_copy(ids_v, ids, seg)
    move.start()
    move.wait()

    def row_id(x, at):
        return ids[x, at // LANES, at % LANES]

    def compute(x, start):
        at = pl.ds(pl.multiple_of(start, CHUNK), CHUNK)
        data = info[x, :, at]
        columns = data.T
        source_row = data[0:1].astype(jnp.int32)
        source_col = columns[:, 0:1].astype(jnp.int32)
        target_col = columns[:, 1:2].astype(jnp.int32)
        weight_col = columns[:, 3:4]
        block_col = columns[:, 4:5].astype(jnp.int32)

        lane = lax.broadcasted_iota(jnp.int32, (CHUNK, part_rows), 1)
        pick = jnp.where(source_col == lane, 1.0, 0.0).astype(jnp.bfloat16)
        sources = dot(jnp.concatenate([pick, pick], axis=1), stack[x, : 2 * part_rows])
        s_re, s_im = sources[:, :width], sources[:, width:]
        w = [tiles(factor, x * CHUNK, CHUNK, q) for q in range(LANE_TILES)]
        w_re, w_im = jnp.concatenate(w[:2], axis=1), jnp.concatenate(w[2:], axis=1)
        queries = jnp.concatenate([s_re * w_re - s_im * w_im, s_re * w_im + s_im * w_re], axis=1)
        q_high, q_low = high_low(queries)
        scores = dot(jnp.concatenate([q_high, q_high, q_low], axis=1), stack_t[1 - x])

        which = jnp.where(
            block_col == lax.broadcasted_iota(jnp.int32, (CHUNK, 2 * group), 1) % group, 1.0, 0.0
        ).astype(jnp.bfloat16)
        often = dot(which, times[x])

        small = jnp.exp(-jnp.abs(scores))
        near = 1.0 / (1.0 + small)
        far = small * near
        up = scores >= 0.0
        sig = jnp.where(up, near, far)
        sig_neg = jnp.where(up, far, near)
        g = sig * often - jnp.where(target_col == lane, sig_neg, 0.0)
        g = g * weight_col
        g_high, g_low = high_low(g)
        gq = dot(jnp.concatenate([g_high, g_high, g_low], axis=1), stack[1 - x])
        g_re, g_im = gq[:, :width], gq[:, width:]
        gw = [g_re * s_re + g_im * s_im, g_im * s_re - g_re * s_im]
        for q in range(LANE_TILES):
            flat = grads.reshape(2 * CHUNK * LANE_TILES, LANES)
            flat[pl.ds(x * CHUNK * LANE_TILES + q, CHUNK, stride=LANE_TILES), :] = gw[q // 2][
                :, (q % 2) * LANES : (q % 2 + 1) * LANES
            ]

        if x == 0:
            gs = jnp.concatenate([g_re * w_re + g_im * w_im, g_im * w_re - g_re * w_im], axis=1)
            sub = lax.broadcasted_iota(jnp.int32, (rows, CHUNK), 0)
            back = jnp.where(source_row - own == sub, 1.0, 0.0).astype(jnp.bfloat16)
            s_high, s_low = high_low(gs)
            mine[...] += dot(jnp.concatenate([back, back], axis=1), jnp.concatenate([s_high, s_low], axis=0))
        else:
            flip[...] = g.T
            turned = flip[pl.ds(pl.multiple_of(own, 8), rows), :]
            f_high, f_low = high_low(turned)
            mine[...] += dot(
                jnp.concatenate([f_high, f_high, f_low], axis=1),
                jnp.concatenate([q_high, q_low, q_high], axis=0),
            )

    def chunk(c, carry):
        start = c * CHUNK

        per = CHUNK // LANES
        row = c * per

        def fetch(k, carry):
            for x in range(2):
                for u in range(LANES):
                    factor[x * CHUNK + k * LANES + u] = table[ids[x, row + k, u]]
            return carry

        lax.fori_loop(0, per, fetch, 0)
        for x in range(2):
            compute(x, start)

        def push(k, carry):
            x = (k // per) ^ side
            k = k % per
            for e in range(0, LANES, 4):
                at = [ids[x, row + k, e + u] for u in range(4)]
                old = [accs[0][r] for r in at]
                for u in range(4):
                    value = old[u]
                    for v in range(u):
                        value = jnp.where(at[u] == at[v], old[v], value)
                    old[u] = value + grads[x * CHUNK + k * LANES + e + u]
                for u in range(4):
                    accs[0][at[u]] = old[u]
            return carry

        lax.fori_loop(0, 2 * per, push, 0)
        return carry

    lax.fori_loop(0, total // CHUNK, chunk, 0)

    ent_ref[:, :half] = mine[:, :half]
    ent_ref[:, half:] = mine[:, width : width + half]

    def finish(i, carry):
        at = pl.ds(pl.multiple_of(i * LANES, LANES), LANES)
        for q in range(LANE_TILES):
            sums = tiles(accs[0], i * LANES, LANES, q)
            for acc in accs[1:]:
                sums = sums + tiles(acc, i * LANES, LANES, q)
            low = (q // 2) * half + (q % 2) * LANES
            size = min(LANES, half - (q % 2) * LANES)
            out_ref[low : low + size, at] = sums.T[:size]
        return carry

    lax.fori_loop(0, relation_count // LANES, finish, 0)


def gradients(spec, sums, relation_count, *operands):
    half, rows, shards, blocks, edges = spec[:5]
    dim, part_rows, width = 2 * half, rows * shards, LANE_TILES // 2 * LANES
    group = shards * blocks
    total = group * edges // 2
    smem = pl.BlockSpec(memory_space=pltpu.SMEM)
    vmem = pl.BlockSpec(memory_space=pltpu.VMEM)
    return pl.pallas_call(
        functools.partial(main_kernel, spec),
        in_specs=[smem, smem, vmem, vmem, vmem, vmem],
        out_specs=(vmem, vmem),
        out_shape=(
            jax.ShapeDtypeStruct((dim, relation_count), jnp.float32),
            jax.ShapeDtypeStruct((rows, dim), jnp.float32),
        ),
        scratch_shapes=[pltpu.VMEM((relation_count, LANE_TILES, LANES), jnp.float32)] * sums
        + [
            pltpu.VMEM((part_rows, 2 * width), jnp.float32),
            pltpu.VMEM((2, 3 * part_rows, 2 * width), jnp.bfloat16),
            pltpu.VMEM((2, 6 * width, part_rows), jnp.bfloat16),
            pltpu.VMEM((2, 2 * group, part_rows), jnp.bfloat16),
            pltpu.VMEM((2, 8, total + edges + LANES), jnp.float32),
            pltpu.VMEM((2, total // LANES, LANES), jnp.int32),
            pltpu.SMEM((2, total // LANES, LANES), jnp.int32),
            pltpu.VMEM((2 * CHUNK, LANE_TILES, LANES), jnp.float32),
            pltpu.VMEM((2 * CHUNK, LANE_TILES, LANES), jnp.float32),
            pltpu.VMEM((part_rows, CHUNK), jnp.float32),
            pltpu.VMEM((rows, 2 * width), jnp.float32),
            pltpu.SemaphoreType.DMA,
        ],
        compiler_params=pltpu.CompilerParams(vmem_limit_bytes=VMEM_BYTES),
        name="gradients",
    )(*operands)


def body(entities, relations, src_index, dst_index, rel_index, neg_index, counts, edge_weight):
    rows, dim = entities.shape
    half = dim // 2
    width = LANE_TILES // 2 * LANES
    relation_count = relations.shape[0]
    blocks, edges = src_index.shape[1:]
    dom_count, shards = lax.axis_size("dom"), lax.axis_size("block")
    part_rows = rows * shards
    partner_bit = dom_count.bit_length() - 2
    block_bits = shards.bit_length() - 1
    other_bits = [bit for bit in range(dom_count.bit_length() - 1) if bit != partner_bit]

    table = relation_table(relations)

    real = jnp.pad(entities[:, :half], ((0, 0), (0, width - half)))
    imag = jnp.pad(entities[:, half:], ((0, 0), (0, width - half)))
    alive = jnp.arange(edges, dtype=jnp.int32)[None, :] < counts[0][:, None]
    weight = edge_weight[0] * alive.astype(jnp.float32)
    entity_ids = jnp.arange(part_rows, dtype=jnp.int32)
    times = jnp.sum((neg_index[0][:, :, None] == entity_ids).astype(jnp.float32), axis=1)
    times = times / neg_index.shape[2]
    ids = jnp.concatenate([src_index[0], dst_index[0], rel_index[0]], axis=0).astype(jnp.float32)
    info_a = jnp.concatenate([ids, weight], axis=0).reshape(-1, width)
    live_row = jnp.pad(counts[0].astype(jnp.float32)[None, :], ((0, 0), (0, width - blocks)))
    times_rows = blocks * part_rows // width
    info_b = jnp.concatenate([times.reshape(-1, width), live_row], axis=0)
    info_b = jnp.pad(info_b, ((0, -info_b.shape[0] % 8), (0, 0)))

    upper = [("block", bit) for bit in reversed(range(1, block_bits))]
    stages_a = upper + [("dom", partner_bit), ("block", 0)]
    stages_b = upper + [("block", 0), ("dom", partner_bit)]
    first = gather_all(jnp.concatenate([real, info_a], axis=0)[None], stages_a)
    second = gather_all(jnp.concatenate([imag, info_b], axis=0)[None], stages_b)
    places_a = tuple(stages_a.index(("block", bit)) for bit in range(block_bits))
    places_b = tuple(stages_b.index(("block", bit)) for bit in range(block_bits))
    place_a, place_b = stages_a.index(("dom", partner_bit)), stages_b.index(("dom", partner_bit))

    live = second[:, rows + times_rows, :blocks].astype(jnp.int32).reshape(-1)
    times_all = second[:, rows : rows + times_rows, :].reshape(-1, 1, part_rows)
    where = jnp.stack([lax.axis_index("block"), (lax.axis_index("dom") >> partner_bit) & 1]).astype(jnp.int32)

    sums = 1
    spec = (half, rows, shards, blocks, edges, places_a, places_b, place_a, place_b)
    relation_part, entity_grad = gradients(
        spec, sums, relation_count, live, where, table, first, second, times_all
    )

    for bit in other_bits:
        relation_part = relation_part + swap(relation_part, "dom", bit)
    return entity_grad, relation_part.T


def solution(mesh):
    placed = (
        P(("dom", "block"), None),
        P(),
        P("dom", "block", None),
        P("dom", "block", None),
        P("dom", "block", None),
        P("dom", "block", None),
        P("dom", "block"),
        P("dom", "block", None),
    )
    return jax.shard_map(
        body,
        mesh=mesh,
        in_specs=placed,
        out_specs=(P(("dom", "block"), None), P()),
        check_vma=False,
    )
```

time: 175 us -> 119 us (0.68)
  Pallas kernels: 124 us -> 68 us
    pallas_call x1, Pallas kernels: 114 us -> 58.8 us  [gradients(): pl.pallas_call(functools.partial(main_kernel, spec), in_specs=[smem, smem...]
  transfers between devices with their start and end apart: 9 -> 9, of which waited for: 6 -> 6; matrix products, arithmetic and copies ran while one was open for 3% -> 4% of each run, Pallas kernels for 6% -> 8%
where the time goes in v2:
time: 119 us; the launch traced here: 118 us
  Pallas kernels  68 us (57%)
  waiting for transfers between devices  22.6 us (19%)
  starting transfers between devices  12.1 us (10%)
  other arithmetic  11.4 us (10%)
  local copies, waits for them, and re-layouts  3.23 us (3%)
    pallas_call x1, Pallas kernels, gradients(): pl.pallas_call(functools.partial(main_kernel, spec), in_specs=[smem, smem...  58.8 us
    ppermute x9, waiting for transfers between devices, swap(): return lax.ppermute(x, axis, [(i, i ^ 1 << bit) for i in range(count)])  22.6 us
    ppermute x9, starting transfers between devices, swap(): return lax.ppermute(x, axis, [(i, i ^ 1 << bit) for i in range(count)])  12.1 us
    pallas_call x1, Pallas kernels, relation_table(): pl.pallas_call(functools.partial(table_kernel, dim // 2), grid=(count //...  9.22 us
    transpose x1, other arithmetic, body(): return (entity_grad, relation_part.T)  6.68 us
  transfers between devices with their start and end apart: 9, of which 6 were waited for; matrix products, arithmetic and copies ran while one was open for 4% of the time, Pallas kernels for 8%

profile of v2, /device:TPU:0, one launch (start us, length us, event | category | flops | bytes accessed | tf_op | source)
XLA Modules:
  0.0 118.2 jit_solution(841396063808076955)
XLA Ops:
  0.6 0.7 convert_element_type.26
  1.3 1.0 convert_reduce_fusion
  2.3 0.9 slice.13
  3.3 4.1 %collective-permute-start = (f32[1,40,256]{2,1,0:T(8,128)S(1)}, f32[1,40,256]{2,1,0:T(8,128)S(1)}, u32[]{:S(2)}, u32[]{:S(2)}) collective-permute-start(f32[1,40,256]{2,1,0:T(8,128)S(1)} %fusion), channel_id=1, source_target_pairs={{0,4},{1,5},{2,6},{3,7},{4,0},{5,1},{6,2},{7,3},{8,12},{9,13},{10,... | collective-permute-start | bytes 122888 | tf_op jit(solution)/shard_map/ppermute | solution.py:18
  7.4 0.8 slice_select_fusion
  8.1 0.8 compare_select_fusion
  8.9 0.7 add_convert_fusion
  9.6 0.1 collective-permute-start.4
  9.7 0.7 pad_add_fusion.where
  10.4 9.2 %relation_table.1.table = f32[4096,4,128]{2,1,0:T(4,128)} custom-call(f32[400,4096]{1,0:T(8,128)} %bitcast.19), custom_call_target="tpu_custom_call" | custom-call | tf_op jit(solution)/shard_map/relation_table/pallas_call | solution.py:43
  19.6 0.0 collective-permute-done
  19.6 1.9 %collective-permute-start.1 = (f32[2,40,256]{2,1,0:T(8,128)S(1)}, f32[2,40,256]{2,1,0:T(8,128)S(1)}, u32[]{:S(2)}, u32[]{:S(2)}) collective-permute-start(f32[2,40,256]{2,1,0:T(8,128)S(1)} %pad_maximum_fusion.4), channel_id=1, source_target_pairs={{0,2},{1,3},{2,0},{3,1},{4,6},{5,7},{6,4},{7,5},{8,10},{9,11},{10,... | collective-permute-start | bytes 245768 | tf_op jit(solution)/shard_map/ppermute | solution.py:18
  21.6 0.0 collective-permute-done.4
  21.6 0.2 collective-permute-start.5
  21.8 3.2 %collective-permute-done.1 = f32[2,40,256]{2,1,0:T(8,128)S(1)} collective-permute-done((f32[2,40,256]{2,1,0:T(8,128)S(1)}, f32[2,40,256]{2,1,0:T(8,128)S(1)}, u32[]{:S(2)}, u32[]{:S(2)}) %collective-permute-start.1) | collective-permute-done | bytes 81952 | tf_op jit(solution)/shard_map/ppermute | solution.py:18
  25.0 1.6 %collective-permute-start.2 = (f32[4,40,256]{2,1,0:T(8,128)S(1)}, f32[4,40,256]{2,1,0:T(8,128)S(1)}, u32[]{:S(2)}, u32[]{:S(2)}) collective-permute-start(f32[4,40,256]{2,1,0:T(8,128)S(1)} %pad_maximum_fusion.2), channel_id=1, source_target_pairs={{0,1},{1,0},{2,3},{3,2},{4,5},{5,4},{6,7},{7,6},{8,9},{9,8},{10,11... | collective-permute-start | bytes 491528 | tf_op jit(solution)/shard_map/ppermute | solution.py:18
  26.6 0.0 collective-permute-done.5
  26.6 1.6 %collective-permute-start.6 = (f32[4,40,256]{2,1,0:T(8,128)S(1)}, f32[4,40,256]{2,1,0:T(8,128)S(1)}, u32[]{:S(2)}, u32[]{:S(2)}) collective-permute-start(f32[4,40,256]{2,1,0:T(8,128)S(1)} %pad_maximum_fusion.3), channel_id=1, source_target_pairs={{0,16},{8,24},{16,0},{24,8},{1,17},{9,25},{17,1},{25,9},{2,18},{10... | collective-permute-start | bytes 491528 | tf_op jit(solution)/shard_map/ppermute | solution.py:18
  28.2 2.2 %collective-permute-done.2 = f32[4,40,256]{2,1,0:T(8,128)S(1)} collective-permute-done((f32[4,40,256]{2,1,0:T(8,128)S(1)}, f32[4,40,256]{2,1,0:T(8,128)S(1)}, u32[]{:S(2)}, u32[]{:S(2)}) %collective-permute-start.2) | collective-permute-done | bytes 163872 | tf_op jit(solution)/shard_map/ppermute | solution.py:18
  30.4 1.6 %collective-permute-start.3 = (f32[8,40,256]{2,1,0:T(8,128)S(1)}, f32[8,40,256]{2,1,0:T(8,128)S(1)}, u32[]{:S(2)}, u32[]{:S(2)}) collective-permute-start(f32[8,40,256]{2,1,0:T(8,128)S(1)} %pad_maximum_fusion), channel_id=1, source_target_pairs={{0,16},{8,24},{16,0},{24,8},{1,17},{9,25},{17,1},{25,9},{2,18},{10... | collective-permute-start | bytes 983048 | tf_op jit(solution)/shard_map/ppermute | solution.py:18
  32.0 1.8 %collective-permute-done.6 = f32[4,40,256]{2,1,0:T(8,128)S(1)} collective-permute-done((f32[4,40,256]{2,1,0:T(8,128)S(1)}, f32[4,40,256]{2,1,0:T(8,128)S(1)}, u32[]{:S(2)}, u32[]{:S(2)}) %collective-permute-start.6) | collective-permute-done | bytes 163872 | tf_op jit(solution)/shard_map/ppermute | solution.py:18
  33.8 1.0 collective-permute-start.7
  34.9 3.4 %collective-permute-done.3 = f32[8,40,256]{2,1,0:T(8,128)S(1)} collective-permute-done((f32[8,40,256]{2,1,0:T(8,128)S(1)}, f32[8,40,256]{2,1,0:T(8,128)S(1)}, u32[]{:S(2)}, u32[]{:S(2)}) %collective-permute-start.3) | collective-permute-done | bytes 327712 | tf_op jit(solution)/shard_map/ppermute | solution.py:18
  38.3 0.0 copy-start
  38.4 0.7 convert_element_type.28.live
  39.1 0.7 reshape.12.counts_of
  39.7 1.2 %collective-permute-done.7 = f32[8,40,256]{2,1,0:T(8,128)S(1)} collective-permute-done((f32[8,40,256]{2,1,0:T(8,128)S(1)}, f32[8,40,256]{2,1,0:T(8,128)S(1)}, u32[]{:S(2)}, u32[]{:S(2)}) %collective-permute-start.7) | collective-permute-done | bytes 327712 | tf_op jit(solution)/shard_map/ppermute | solution.py:18
  41.0 0.0 copy-done
  41.0 0.0 copy-start.1
  41.0 0.9 copy-done.1
  41.9 58.8 %gradients.1 = (f32[400,4096]{1,0:T(8,128)}, f32[32,400]{1,0:T(8,128)}) custom-call(s32[32]{0:T(128)} %convert_element_type.28.live, s32[2]{0:T(128)} %pad_add_fusion.where, f32[4096,4,128]{2,1,0:T(4,128)} %relation_table.1.table, f32[16,40,256]{2,1,0:T(8,128)} %copy-done.1, f32[16,40,256]{2,1,0:T(8,128)} %copy-done, f32[32,1,256]{2,1,0:T(1,128)} %reshape.12.counts_of), custom_call_target="tpu_custom_call" | custom-call | tf_op jit(solution)/shard_map/gradients/pallas_call | solution.py:284
  100.7 0.1 collective-permute-start.8
  100.7 10.7 %collective-permute-done.8 = f32[400,4096]{1,0:T(8,128)S(1)} collective-permute-done((f32[400,4096]{1,0:T(8,128)}, f32[400,4096]{1,0:T(8,128)S(1)}, u32[]{:S(2)}, u32[]{:S(2)}) %collective-permute-start.8) | collective-permute-done | bytes 6553632 | tf_op jit(solution)/shard_map/ppermute | solution.py:18
  111.5 6.7 %add_bitcast_fusion = f32[4096,400]{0,1:T(8,128)} fusion(f32[400,4096]{1,0:T(8,128)} %get-tuple-element.5, f32[400,4096]{1,0:T(8,128)S(1)} %collective-permute-done.8), kind=kLoop, calls=%fused_computation | loop fusion | flops 1638400 | bytes 19660800 | tf_op jit(solution)/shard_map/transpose | solution.py:361
  (21 shorter events, 0.3 us)
Async XLA Ops:
  3.3 16.3 %collective-permute-start = (f32[1,40,256]{2,1,0:T(8,128)S(1)}, f32[1,40,256]{2,1,0:T(8,128)S(1)}, u32[]{:S(2)}, u32[]{:S(2)}) collective-permute-start(f32[1,40,256]{2,1,0:T(8,128)S(1)} %fusion), channel_id=1, source_target_pairs={{0,4},{1,5},{2,6},{3,7},{4,0},{5,1},{6,2},{7,3},{8,12},{9,13},{10,... | collective-permute-start | bytes 122888 | tf_op jit(solution)/shard_map/ppermute | solution.py:18
  9.6 11.9 %collective-permute-start.4 = (f32[1,40,256]{2,1,0:T(8,128)S(1)}, f32[1,40,256]{2,1,0:T(8,128)S(1)}, u32[]{:S(2)}, u32[]{:S(2)}) collective-permute-start(f32[1,40,256]{2,1,0:T(8,128)S(1)} %get-tuple-element.7), channel_id=1, source_target_pairs={{0,4},{1,5},{2,6},{3,7},{4,0},{5,1},{6,2},{7,3},{8,12},{9,13},{10,... | collective-permute-start | bytes 122888 | tf_op jit(solution)/shard_map/ppermute | solution.py:18
  19.6 5.4 %collective-permute-start.1 = (f32[2,40,256]{2,1,0:T(8,128)S(1)}, f32[2,40,256]{2,1,0:T(8,128)S(1)}, u32[]{:S(2)}, u32[]{:S(2)}) collective-permute-start(f32[2,40,256]{2,1,0:T(8,128)S(1)} %pad_maximum_fusion.4), channel_id=1, source_target_pairs={{0,2},{1,3},{2,0},{3,1},{4,6},{5,7},{6,4},{7,5},{8,10},{9,11},{10,... | collective-permute-start | bytes 245768 | tf_op jit(solution)/shard_map/ppermute | solution.py:18
  21.6 5.0 %collective-permute-start.5 = (f32[2,40,256]{2,1,0:T(8,128)S(1)}, f32[2,40,256]{2,1,0:T(8,128)S(1)}, u32[]{:S(2)}, u32[]{:S(2)}) collective-permute-start(f32[2,40,256]{2,1,0:T(8,128)S(1)} %pad_maximum_fusion.5), channel_id=1, source_target_pairs={{0,2},{1,3},{2,0},{3,1},{4,6},{5,7},{6,4},{7,5},{8,10},{9,11},{10,... | collective-permute-start | bytes 245768 | tf_op jit(solution)/shard_map/ppermute | solution.py:18
  25.0 5.4 %collective-permute-start.2 = (f32[4,40,256]{2,1,0:T(8,128)S(1)}, f32[4,40,256]{2,1,0:T(8,128)S(1)}, u32[]{:S(2)}, u32[]{:S(2)}) collective-permute-start(f32[4,40,256]{2,1,0:T(8,128)S(1)} %pad_maximum_fusion.2), channel_id=1, source_target_pairs={{0,1},{1,0},{2,3},{3,2},{4,5},{5,4},{6,7},{7,6},{8,9},{9,8},{10,11... | collective-permute-start | bytes 491528 | tf_op jit(solution)/shard_map/ppermute | solution.py:18
  26.6 7.2 %collective-permute-start.6 = (f32[4,40,256]{2,1,0:T(8,128)S(1)}, f32[4,40,256]{2,1,0:T(8,128)S(1)}, u32[]{:S(2)}, u32[]{:S(2)}) collective-permute-start(f32[4,40,256]{2,1,0:T(8,128)S(1)} %pad_maximum_fusion.3), channel_id=1, source_target_pairs={{0,16},{8,24},{16,0},{24,8},{1,17},{9,25},{17,1},{25,9},{2,18},{10... | collective-permute-start | bytes 491528 | tf_op jit(solution)/shard_map/ppermute | solution.py:18
  30.4 7.9 %collective-permute-start.3 = (f32[8,40,256]{2,1,0:T(8,128)S(1)}, f32[8,40,256]{2,1,0:T(8,128)S(1)}, u32[]{:S(2)}, u32[]{:S(2)}) collective-permute-start(f32[8,40,256]{2,1,0:T(8,128)S(1)} %pad_maximum_fusion), channel_id=1, source_target_pairs={{0,16},{8,24},{16,0},{24,8},{1,17},{9,25},{17,1},{25,9},{2,18},{10... | collective-permute-start | bytes 983048 | tf_op jit(solution)/shard_map/ppermute | solution.py:18
  33.8 7.1 %collective-permute-start.7 = (f32[8,40,256]{2,1,0:T(8,128)S(1)}, f32[8,40,256]{2,1,0:T(8,128)S(1)}, u32[]{:S(2)}, u32[]{:S(2)}) collective-permute-start(f32[8,40,256]{2,1,0:T(8,128)S(1)} %pad_maximum_fusion.1), channel_id=1, source_target_pairs={{0,1},{1,0},{2,3},{3,2},{4,5},{5,4},{6,7},{7,6},{8,9},{9,8},{10,11... | collective-permute-start | bytes 983048 | tf_op jit(solution)/shard_map/ppermute | solution.py:18
  38.3 2.7 %copy-start = (f32[16,40,256]{2,1,0:T(8,128)}, f32[16,40,256]{2,1,0:T(8,128)S(1)}, u32[]{:S(2)}) copy-start(f32[16,40,256]{2,1,0:T(8,128)S(1)} %constant_dynamic-update-slice_fusion.second) | copy-start | bytes 1966084
  41.0 0.9 copy-start.1
  100.7 10.8 %collective-permute-start.8 = (f32[400,4096]{1,0:T(8,128)}, f32[400,4096]{1,0:T(8,128)S(1)}, u32[]{:S(2)}, u32[]{:S(2)}) collective-permute-start(f32[400,4096]{1,0:T(8,128)} %get-tuple-element.5), channel_id=1, source_target_pairs={{0,8},{8,0},{16,24},{24,16},{1,9},{9,1},{17,25},{25,17},{2,10},{10... | collective-permute-start | bytes 19660808 | tf_op jit(solution)/shard_map/ppermute | solution.py:18

commit v3 on v2

v3 whole, which is shorter than its diff:
```python
import functools

import jax
import jax.numpy as jnp
from jax import lax
from jax.experimental import pallas as pl
from jax.experimental.pallas import tpu as pltpu
from jax.sharding import PartitionSpec as P

LANES = 128
CHUNK = 256
GROUP = 8
STEP = 512
PARTS = 4
LANE_TILES = 4
SMALL_BYTES = 16 * 1024 * 1024


def swap(x, axis, bit):
    count = lax.axis_size(axis)
    return lax.ppermute(x, axis, [(i, i ^ (1 << bit)) for i in range(count)])


def gather_all(x, upper, lower):
    for axis, bit in upper:
        x = jnp.concatenate([x, swap(x, axis, bit)], axis=0)
    halves = list(jnp.split(x, 2))
    for k in range(2):
        others = [swap(halves[0], *lower[k]), swap(halves[1], *lower[1 - k])]
        halves = [jnp.concatenate(both, axis=0) for both in zip(halves, others)]
    return jnp.concatenate(halves, axis=0)


def block_index(j, x, bits):
    depth = bits - 1
    out = 0
    for stage in range(depth - 1):
        out = out | (((j >> (bits - 1 - stage)) & 1) << stage)
    half, low = (j >> 1) & 1, j & 1
    straight = (x << (depth - 1)) | (low << depth)
    crossed = (low << (depth - 1)) | (x << depth)
    return out | (half << (depth + 1)) | (straight + half * (crossed - straight))


def high_low(x):
    high = x.astype(jnp.bfloat16)
    return high, (x - high.astype(jnp.float32)).astype(jnp.bfloat16)


def dot(a, b):
    return jnp.dot(a, b, preferred_element_type=jnp.float32)


def pack_kernel(half, part_rows, counts, entities, src, dst, rel, neg, weight, out_ref):
    rows = entities.shape[0]
    blocks, edges = src.shape[1:]
    width = out_ref.shape[2]
    draws = neg.shape[2]
    base = rows + 4 * blocks
    gap = jnp.zeros((rows, width - half), jnp.float32)
    out = out_ref.at[0]
    out[:rows, :] = jnp.concatenate([entities[:, :half], gap], axis=1)
    out[base : base + rows, :] = jnp.concatenate([entities[:, half:], gap], axis=1)
    for k, ids in enumerate((src, dst, rel)):
        out[rows + k * blocks : rows + (k + 1) * blocks, :] = ids[0].astype(jnp.float32)
    slot = lax.broadcasted_iota(jnp.int32, (1, edges), 1)
    for i in range(blocks):
        row = rows + 3 * blocks + i
        out[row : row + 1, :] = jnp.where(slot < counts[0, i], weight[0, i : i + 1, :], 0.0)
    top = base + rows
    drawn = jnp.concatenate([neg[0], jnp.zeros((8 - blocks, draws), jnp.int32)], axis=0).astype(jnp.float32)
    drawn = drawn.T.astype(jnp.int32)
    lane = lax.broadcasted_iota(jnp.int32, (draws, part_rows), 1)
    for i in range(blocks):
        hits = jnp.where(drawn[:, i : i + 1] == lane, 1.0, 0.0).astype(jnp.bfloat16)
        times = dot(jnp.ones((8, draws), jnp.bfloat16), hits)[:1] / draws
        for part in range(part_rows // width):
            row = top + i * (part_rows // width) + part
            out[row : row + 1, :] = times[:, part * width : (part + 1) * width]
    top += blocks * (part_rows // width)
    spare = out_ref.shape[1] - top
    lane = lax.broadcasted_iota(jnp.int32, (spare, width), 1)
    last = jnp.zeros((spare, width), jnp.float32)
    for i in range(blocks):
        last = jnp.where(lane == i, counts[0, i].astype(jnp.float32), last)
    out[top:, :] = last


def packed(entities, counts, src, dst, rel, neg, weight, part_rows):
    rows, dim = entities.shape
    blocks = src.shape[1]
    width = LANE_TILES // 2 * LANES
    height = 2 * rows + 4 * blocks + blocks * (part_rows // width) + 1
    vmem = pl.BlockSpec(memory_space=pltpu.VMEM)
    return pl.pallas_call(
        functools.partial(pack_kernel, dim // 2, part_rows),
        in_specs=[pl.BlockSpec(memory_space=pltpu.SMEM)] + [vmem] * 6,
        out_specs=vmem,
        out_shape=jax.ShapeDtypeStruct((1, -(-height // 8) * 8, width), jnp.float32),
        compiler_params=pltpu.CompilerParams(vmem_limit_bytes=SMALL_BYTES),
        name="pack",
    )(counts, *[in_hbm(x) for x in (entities, src, dst, rel, neg, weight)])


def in_vmem(x):
    return pltpu.with_memory_space_constraint(x, pltpu.VMEM)


def in_hbm(x):
    return pltpu.with_memory_space_constraint(x, pltpu.HBM)


def finish_kernel(half, low, acc_ref, out_ref):
    for i in range(out_ref.shape[1] // LANES):
        for q in range(LANE_TILES):
            rows = tiles(acc_ref, low + i * LANES, LANES, q).T
            top = (q // 2) * half + (q % 2) * LANES
            size = min(LANES, half - (q % 2) * LANES)
            out_ref[top : top + size, i * LANES : (i + 1) * LANES] = rows[:size]


def add_kernel(one_ref, other_ref, *refs):
    refs[-1][...] = one_ref[...] + other_ref[...]


def summed(acc, dim, bits):
    count = acc.shape[0]
    size = count // PARTS
    parts = []
    for k in range(PARTS):
        part = pl.pallas_call(
            functools.partial(finish_kernel, dim // 2, k * size),
            in_specs=[pl.BlockSpec(memory_space=pltpu.VMEM)],
            out_specs=pl.BlockSpec(memory_space=pltpu.VMEM),
            out_shape=pltpu.VMEM((dim, size), jnp.float32),
            cost_estimate=pl.CostEstimate(flops=0, bytes_accessed=size * dim * 8, transcendentals=0),
            compiler_params=pltpu.CompilerParams(vmem_limit_bytes=SMALL_BYTES),
            name="turn",
        )(in_vmem(acc))
        for bit in bits[:-1]:
            part = part + swap(part, "dom", bit)
        parts.append((part, swap(part, "dom", bits[-1])))
    total = None
    for k, (part, other) in enumerate(parts):
        block = pl.BlockSpec((dim, size), lambda i: (0, 0))
        total = pl.pallas_call(
            add_kernel,
            grid=(1,),
            in_specs=[block, block] + ([] if total is None else [pl.BlockSpec(memory_space=pl.ANY)]),
            out_specs=pl.BlockSpec((dim, size), lambda i, k=k: (0, k)),
            out_shape=jax.ShapeDtypeStruct((dim, count), jnp.float32),
            input_output_aliases={} if total is None else {2: 0},
            cost_estimate=pl.CostEstimate(flops=size * dim, bytes_accessed=size * dim * 12, transcendentals=0),
            compiler_params=pltpu.CompilerParams(vmem_limit_bytes=SMALL_BYTES),
            name="add_part",
        )(part, other, *([] if total is None else [total]))
    return total


def tiles(ref, low, count, q):
    flat = ref.reshape(ref.shape[0] * ref.shape[1], LANES)
    return flat[pl.ds(low * LANE_TILES + q, count, stride=LANE_TILES), :]


STAGES = 5


def in_turn(parts, *sides):
    for stage in range(STAGES):
        for part in parts:
            next(part, None)
            for side, steps in sides:
                for _ in range(-(-steps // (STAGES * len(parts)))):
                    next(side, None)


def main_kernel(spec, live, where, relations, blocks_of, acc, ent_ref, *scratch):
    (half, rows, shards, blocks, edges) = spec
    (columns_of, table, ent, stack, stack_t, times, info, ids_v, ids, factor, grads, flip, mine, band, seg, come) = scratch
    width = LANE_TILES // 2 * LANES
    part_rows = rows * shards
    group = shards * blocks
    total = group * edges // 2
    bits = shards.bit_length() - 1
    base = rows + 4 * blocks
    top = base + rows
    me, side = where[0], where[1]
    own = me * rows

    steps = acc.shape[0] // STEP
    arrivals = []
    for k in range(steps):
        at = pl.ds(k * STEP, STEP)
        arrivals.append(pltpu.make_async_copy(relations.at[:, at], columns_of.at[:, at], come.at[k]))
        arrivals[-1].start()

    mine[...] = jnp.zeros_like(mine)
    info[...] = jnp.zeros_like(info)
    down = lax.broadcasted_iota(jnp.int32, band.shape, 0)
    across = lax.broadcasted_iota(jnp.int32, band.shape, 1)
    band[...] = jnp.where((across <= down) & (across // GROUP == down // GROUP), 1.0, 0.0)

    for x in range(2):
        for j in range(shards):
            k = block_index(j, x, bits)
            at = pl.ds(pl.multiple_of((j ^ me) * rows, 8), rows)
            ent[at, :width] = blocks_of[k, :rows, :]
            ent[at, width:] = blocks_of[k, base : base + rows, :]
        whole = ent[...]
        high, low = high_low(whole)
        stack[x] = jnp.concatenate([high, low, high], axis=0)
        high, low = high_low(whole.T)
        stack_t[x] = jnp.concatenate([high, low, high], axis=0)

    for x in range(2):
        rows_of = []
        for n in range(group):
            k = block_index((n // blocks) ^ me, x, bits)
            low = top + (n % blocks) * (part_rows // width)
            pieces = [blocks_of[k, low + i : low + i + 1, :] for i in range(part_rows // width)]
            rows_of.append(jnp.concatenate(pieces, axis=1))
        high, low = high_low(jnp.concatenate(rows_of, axis=0))
        times[x] = jnp.concatenate([high, low], axis=0)

        def lay(n, offset):
            k, slot = block_index((n // blocks) ^ me, x, bits), n % blocks
            count = live[k * blocks + slot]
            tile = blocks_of[k, rows : rows + 4 * blocks, :]

            def chosen(k):
                row = tile[k * blocks : k * blocks + 1]
                for i in range(1, blocks):
                    row = jnp.where(slot == i, tile[k * blocks + i : k * blocks + i + 1], row)
                return row

            number = jnp.zeros((1, edges), jnp.float32) + n.astype(jnp.float32)
            data = [chosen(k) for k in range(4)] + [number, jnp.zeros((3, edges), jnp.float32)]
            data = jnp.concatenate(data, axis=0)
            data = jnp.where(lax.broadcasted_iota(jnp.int32, data.shape, 1) < count, data, 0.0)
            data = jnp.concatenate([data, jnp.zeros((8, LANES), jnp.float32)], axis=1)
            data = pltpu.roll(data, offset % LANES, 1)
            at = pl.ds(pl.multiple_of((offset // LANES) * LANES, LANES), edges + LANES)
            info[x, :, at] = info[x, :, at] + data
            return offset + count

        lax.fori_loop(0, group, lay, jnp.int32(0))
        for i in range(total // LANES):
            ids_v[x, i : i + 1, :] = info[x, 2:3, i * LANES : (i + 1) * LANES].astype(jnp.int32)

    move = pltpu.make_async_copy(ids_v, ids, seg)
    move.start()

    def turn(k, carry):
        low = k * STEP
        at = pl.ds(pl.multiple_of(low, STEP), STEP)
        pltpu.make_async_copy(relations.at[:, at], columns_of.at[:, at], come.at[k]).wait()
        flat = table.reshape(table.shape[0] * LANE_TILES, LANES)
        for part in range(2):
            square = columns_of[part * half : (part + 1) * half, at]
            square = jnp.concatenate([square, jnp.zeros((width - half, STEP), jnp.float32)], axis=0).T
            for j in range(LANE_TILES // 2):
                to = pl.ds(low * LANE_TILES + part * (LANE_TILES // 2) + j, STEP, stride=LANE_TILES)
                flat[to, :] = square[:, j * LANES : (j + 1) * LANES]
        flat = acc.reshape(acc.shape[0] * LANE_TILES, LANES)
        to = pl.ds(pl.multiple_of(low * LANE_TILES, 8), STEP * LANE_TILES)
        flat[to, :] = jnp.zeros((STEP * LANE_TILES, LANES), jnp.float32)
        return carry

    lax.fori_loop(0, steps, turn, 0)
    move.wait()

    def row_id(x, at):
        return ids[x, at // LANES, at % LANES]

    def compute(x, start, slot):
        at = pl.ds(pl.multiple_of(start, CHUNK), CHUNK)
        data = info[x, :, at]
        columns = data.T
        source_row = data[0:1].astype(jnp.int32)
        source_col = columns[:, 0:1].astype(jnp.int32)
        target_col = columns[:, 1:2].astype(jnp.int32)
        weight_col = columns[:, 3:4]
        block_col = columns[:, 4:5].astype(jnp.int32)

        lane = lax.broadcasted_iota(jnp.int32, (CHUNK, part_rows), 1)
        pick = jnp.where(source_col == lane, 1.0, 0.0).astype(jnp.bfloat16)
        sources = dot(jnp.concatenate([pick, pick], axis=1), stack[x, : 2 * part_rows])
        yield
        s_re, s_im = sources[:, :width], sources[:, width:]
        w = [tiles(factor, (slot * 2 + x) * CHUNK, CHUNK, q) for q in range(LANE_TILES)]
        w_re, w_im = jnp.concatenate(w[:2], axis=1), jnp.concatenate(w[2:], axis=1)
        queries = jnp.concatenate([s_re * w_re - s_im * w_im, s_re * w_im + s_im * w_re], axis=1)
        q_high, q_low = high_low(queries)
        scores = dot(jnp.concatenate([q_high, q_high, q_low], axis=1), stack_t[1 - x])
        yield

        which = jnp.where(
            block_col == lax.broadcasted_iota(jnp.int32, (CHUNK, 2 * group), 1) % group, 1.0, 0.0
        ).astype(jnp.bfloat16)
        often = dot(which, times[x])

        small = jnp.exp(-jnp.abs(scores))
        near = 1.0 / (1.0 + small)
        far = small * near
        up = scores >= 0.0
        sig = jnp.where(up, near, far)
        sig_neg = jnp.where(up, far, near)
        g = sig * often - jnp.where(target_col == lane, sig_neg, 0.0)
        g = g * weight_col
        g_high, g_low = high_low(g)
        gq = dot(jnp.concatenate([g_high, g_high, g_low], axis=1), stack[1 - x])
        yield
        g_re, g_im = gq[:, :width], gq[:, width:]
        gw = jnp.concatenate([g_re * s_re + g_im * s_im, g_im * s_re - g_re * s_im], axis=1)
        same = jnp.where(columns[:, 2:3] == data[2:3], band[...], 0.0).astype(jnp.bfloat16)
        w_high, w_low = high_low(gw)
        gw = dot(jnp.concatenate([same, same], axis=1), jnp.concatenate([w_high, w_low], axis=0))
        yield
        flat = grads.reshape(4 * CHUNK * LANE_TILES, LANES)
        for q in range(LANE_TILES):
            at = pl.ds((slot * 2 + x) * CHUNK * LANE_TILES + q, CHUNK, stride=LANE_TILES)
            flat[at, :] = gw[:, q * LANES : (q + 1) * LANES]

        if x == 0:
            gs = jnp.concatenate([g_re * w_re + g_im * w_im, g_im * w_re - g_re * w_im], axis=1)
            sub = lax.broadcasted_iota(jnp.int32, (rows, CHUNK), 0)
            back = jnp.where(source_row - own == sub, 1.0, 0.0).astype(jnp.bfloat16)
            s_high, s_low = high_low(gs)
            mine[...] += dot(jnp.concatenate([back, back], axis=1), jnp.concatenate([s_high, s_low], axis=0))
        else:
            flip[...] = g.T
            turned = flip[pl.ds(pl.multiple_of(own, 8), rows), :]
            f_high, f_low = high_low(turned)
            mine[...] += dot(
                jnp.concatenate([f_high, f_high, f_low], axis=1),
                jnp.concatenate([q_high, q_low, q_high], axis=0),
            )

    per = CHUNK // LANES
    last = total // CHUNK - 1

    def fetch(c, slot):
        for e in range(0, CHUNK, 8):
            for x in range(2):
                for u in range(8):
                    row = table[ids[x, c * per + e // LANES, e % LANES + u]]
                    factor[(slot * 2 + x) * CHUNK + e + u] = row
            yield

    def push(c, slot):
        for turn in range(2):
            x = turn ^ side
            for e in range(0, CHUNK, GROUP):
                at = [ids[x, c * per + e // LANES, e % LANES + u] for u in range(GROUP)]
                new = [acc[r] + grads[(slot * 2 + x) * CHUNK + e + u] for u, r in enumerate(at)]
                for r, value in zip(at, new):
                    acc[r] = value
                yield

    def drain(steps):
        for _ in steps:
            pass

    def chunk(c, carry):
        slot = c & 1
        in_turn(
            [compute(x, c * CHUNK, slot) for x in range(2)],
            (fetch(jnp.minimum(c + 1, last), 1 - slot), CHUNK // 8),
            (push(jnp.maximum(c - 1, 0), 1 - slot), 2 * CHUNK // GROUP),
        )
        return carry

    def empty(i, carry):
        grads[pl.ds(2 * CHUNK + i * 8, 8)] = jnp.zeros((8, LANE_TILES, LANES), jnp.float32)
        return carry

    lax.fori_loop(0, 2 * CHUNK // 8, empty, 0)
    drain(fetch(0, 0))
    lax.fori_loop(0, last + 1, chunk, 0)
    drain(push(last, last % 2))

    ent_ref[:, :half] = mine[:, :half]
    ent_ref[:, half:] = mine[:, width : width + half]


def gradients(spec, relations, live, where, blocks_of):
    half, rows, shards, blocks, edges = spec
    dim, part_rows, width = 2 * half, rows * shards, LANE_TILES // 2 * LANES
    relation_count = relations.shape[0]
    group = shards * blocks
    total = group * edges // 2
    smem = pl.BlockSpec(memory_space=pltpu.SMEM)
    vmem = pl.BlockSpec(memory_space=pltpu.VMEM)
    return pl.pallas_call(
        functools.partial(main_kernel, spec),
        in_specs=[smem, smem, pl.BlockSpec(memory_space=pl.ANY), vmem],
        out_specs=(vmem, vmem),
        out_shape=(
            pltpu.VMEM((relation_count, LANE_TILES, LANES), jnp.float32),
            jax.ShapeDtypeStruct((rows, dim), jnp.float32),
        ),
        scratch_shapes=[
            pltpu.VMEM((dim, relation_count), jnp.float32),
            pltpu.VMEM((relation_count, LANE_TILES, LANES), jnp.float32),
            pltpu.VMEM((part_rows, 2 * width), jnp.float32),
            pltpu.VMEM((2, 3 * part_rows, 2 * width), jnp.bfloat16),
            pltpu.VMEM((2, 6 * width, part_rows), jnp.bfloat16),
            pltpu.VMEM((2, 2 * group, part_rows), jnp.bfloat16),
            pltpu.VMEM((2, 8, total + edges + LANES), jnp.float32),
            pltpu.VMEM((2, total // LANES, LANES), jnp.int32),
            pltpu.SMEM((2, total // LANES, LANES), jnp.int32),
            pltpu.VMEM((4 * CHUNK, LANE_TILES, LANES), jnp.float32),
            pltpu.VMEM((4 * CHUNK, LANE_TILES, LANES), jnp.float32),
            pltpu.VMEM((part_rows, CHUNK), jnp.float32),
            pltpu.VMEM((rows, 2 * width), jnp.float32),
            pltpu.VMEM((CHUNK, CHUNK), jnp.float32),
            pltpu.SemaphoreType.DMA,
            pltpu.SemaphoreType.DMA((relation_count // STEP,)),
        ],
        compiler_params=pltpu.CompilerParams(vmem_limit_bytes=(40 if part_rows <= 256 else 54) * 1024 * 1024),
        name="gradients",
    )(live, where, in_hbm(relations.T), blocks_of)


def body(entities, relations, src_index, dst_index, rel_index, neg_index, counts, edge_weight):
    rows, dim = entities.shape
    width = LANE_TILES // 2 * LANES
    blocks, edges = src_index.shape[1:]
    dom_count, shards = lax.axis_size("dom"), lax.axis_size("block")
    part_rows = rows * shards
    partner_bit = dom_count.bit_length() - 2
    block_bits = shards.bit_length() - 1
    other_bits = [bit for bit in range(dom_count.bit_length() - 1) if bit != partner_bit]

    block = packed(entities, counts, src_index, dst_index, rel_index, neg_index, edge_weight, part_rows)
    upper = [("block", bit) for bit in reversed(range(1, block_bits))]
    blocks_of = gather_all(block, upper, [("dom", partner_bit), ("block", 0)])
    last = 2 * rows + 4 * blocks + blocks * (part_rows // width)
    live = blocks_of[:, last, :blocks].astype(jnp.int32).reshape(-1)
    where = jnp.stack([lax.axis_index("block"), (lax.axis_index("dom") >> partner_bit) & 1]).astype(jnp.int32)

    spec = (dim // 2, rows, shards, blocks, edges)
    acc, entity_grad = gradients(spec, relations, live, where, blocks_of)
    return entity_grad, summed(acc, dim, other_bits).T


def solution(mesh):
    placed = (
        P(("dom", "block"), None),
        P(),
        P("dom", "block", None),
        P("dom", "block", None),
        P("dom", "block", None),
        P("dom", "block", None),
        P("dom", "block"),
        P("dom", "block", None),
    )
    return jax.shard_map(
        body,
        mesh=mesh,
        in_specs=placed,
        out_specs=(P(("dom", "block"), None), P()),
        check_vma=False,
    )
```

time: 119 us -> 84.2 us (0.71)
  the two profiles are of different devices: /device:TPU:0 before, /device:TPU:29 now
where the time goes in v3:
time: 84.2 us; the launch traced here: 84.1 us
  Pallas kernels  44.7 us (53%)
  waiting for transfers between devices  29.9 us (36%)
  starting transfers between devices  7.75 us (9%)
    pallas_call x1, Pallas kernels, gradients(): pl.pallas_call(functools.partial(main_kernel, spec), in_specs=[smem, smem...  35.4 us
    ppermute x10, waiting for transfers between devices, swap(): return lax.ppermute(x, axis, [(i, i ^ 1 << bit) for i in range(count)])  29.9 us
    ppermute x10, starting transfers between devices, swap(): return lax.ppermute(x, axis, [(i, i ^ 1 << bit) for i in range(count)])  7.75 us
    pallas_call x4, Pallas kernels, summed(): pl.pallas_call(add_kernel, grid=(1,), in_specs=[block, block] + ([] if to...  5.32 us
    pallas_call x4, Pallas kernels, summed(): pl.pallas_call(functools.partial(finish_kernel, dim // 2, k * size), in_s...  2.37 us
  transfers between devices with their start and end apart: 10, of which 9 were waited for; matrix products, arithmetic and copies ran while one was open for 0% of the time, Pallas kernels for 7%

profile of v3, /device:TPU:29, one launch (start us, length us, event | category | flops | bytes accessed | tf_op | source)
XLA Modules:
  0.0 84.1 jit_solution(13912230350360140219)
XLA Ops:
  0.6 0.0 copy-start
  0.6 0.6 copy-done
  1.3 1.5 %pack.1 = f32[1,80,256]{2,1,0:T(8,128)S(1)} custom-call(s32[1,2]{1,0:T(1,128)S(1)} %copy-done, f32[32,400]{1,0:T(8,128)} %entities.1, s32[1,2,256]{2,1,0:T(2,128)} %src.1, s32[1,2,256]{2,1,0:T(2,128)} %dst.1, s32[1,2,256]{2,1,0:T(2,128)} %rel.1, s32[1,2,1024]{2,1,0:T(2,128)} %neg.1, f32[1,2,256]{2,1,0:T(2,128)} %weight.1), custom_call_target="tpu_custom_call" | custom-call | tf_op jit(solution)/shard_map/pack/pallas_call | solution.py:95
  2.8 0.1 collective-permute-start
  3.0 6.7 %collective-permute-done = f32[1,80,256]{2,1,0:T(8,128)S(1)} collective-permute-done((f32[1,80,256]{2,1,0:T(8,128)S(1)}, f32[1,80,256]{2,1,0:T(8,128)S(1)}, u32[]{:S(2)}, u32[]{:S(2)}) %collective-permute-start) | collective-permute-done | bytes 81952 | tf_op jit(solution)/shard_map/ppermute | solution.py:21
  9.7 1.3 %collective-permute-start.1 = (f32[2,80,256]{2,1,0:T(8,128)S(1)}, f32[2,80,256]{2,1,0:T(8,128)S(1)}, u32[]{:S(2)}, u32[]{:S(2)}) collective-permute-start(f32[2,80,256]{2,1,0:T(8,128)S(1)} %pad_maximum_fusion.2), channel_id=1, source_target_pairs={{0,16},{8,24},{16,0},{24,8},{1,17},{9,25},{17,1},{25,9},{2,18},{10... | collective-permute-start | bytes 491528 | tf_op jit(solution)/shard_map/ppermute | solution.py:21
  11.0 0.0 collective-permute-start.3
  11.0 0.1 pad_add_fusion.where
  11.0 3.8 %collective-permute-done.1 = f32[2,80,256]{2,1,0:T(8,128)S(1)} collective-permute-done((f32[2,80,256]{2,1,0:T(8,128)S(1)}, f32[2,80,256]{2,1,0:T(8,128)S(1)}, u32[]{:S(2)}, u32[]{:S(2)}) %collective-permute-start.1) | collective-permute-done | bytes 163872 | tf_op jit(solution)/shard_map/ppermute | solution.py:21
  14.9 0.3 collective-permute-start.2
  15.2 0.6 collective-permute-done.3
  15.7 0.7 collective-permute-start.4
  16.4 9.7 %collective-permute-done.4 = f32[2,80,256]{2,1,0:T(8,128)S(1)} collective-permute-done((f32[2,80,256]{2,1,0:T(8,128)S(1)}, f32[2,80,256]{2,1,0:T(8,128)S(1)}, u32[]{:S(2)}, u32[]{:S(2)}) %collective-permute-start.4) | collective-permute-done | bytes 163872 | tf_op jit(solution)/shard_map/ppermute | solution.py:21
  26.1 1.3 %collective-permute-start.5 = (f32[4,80,256]{2,1,0:T(8,128)S(1)}, f32[4,80,256]{2,1,0:T(8,128)S(1)}, u32[]{:S(2)}, u32[]{:S(2)}) collective-permute-start(f32[4,80,256]{2,1,0:T(8,128)S(1)} %pad_maximum_fusion.1), channel_id=1, source_target_pairs={{0,16},{8,24},{16,0},{24,8},{1,17},{9,25},{17,1},{25,9},{2,18},{10... | collective-permute-start | bytes 983048 | tf_op jit(solution)/shard_map/ppermute | solution.py:21
  27.4 0.0 collective-permute-done.2
  27.5 5.5 %collective-permute-done.5 = f32[4,80,256]{2,1,0:T(8,128)S(1)} collective-permute-done((f32[4,80,256]{2,1,0:T(8,128)S(1)}, f32[4,80,256]{2,1,0:T(8,128)S(1)}, u32[]{:S(2)}, u32[]{:S(2)}) %collective-permute-start.5) | collective-permute-done | bytes 327712 | tf_op jit(solution)/shard_map/ppermute | solution.py:21
  33.0 0.1 convert_element_type.8.live
  33.1 35.4 %gradients.1 = (f32[4096,4,128]{2,1,0:T(4,128)S(1)}, f32[32,400]{1,0:T(8,128)}) custom-call(s32[32]{0:T(128)S(1)} %convert_element_type.8.live, s32[2]{0:T(128)S(1)} %pad_add_fusion.where, f32[400,4096]{1,0:T(8,128)} %bitcast.5, f32[16,80,256]{2,1,0:T(8,128)S(1)} %constant_dynamic-update-slice_fusion.blocks_of), custom_call_target="tpu_custom_call" | custom-call | tf_op jit(solution)/shard_map/gradients/pallas_call | solution.py:394
  68.6 0.6 turn.7.one_ref
  69.2 3.4 %collective-permute-start.9 = (f32[400,1024]{1,0:T(8,128)S(1)}, f32[400,1024]{1,0:T(8,128)S(1)}, u32[]{:S(2)}, u32[]{:S(2)}) collective-permute-start(f32[400,1024]{1,0:T(8,128)S(1)} %turn.7.one_ref), channel_id=1, source_target_pairs={{0,8},{8,0},{16,24},{24,16},{1,9},{9,1},{17,25},{25,17},{2,10},{10... | collective-permute-start | bytes 4915208 | tf_op jit(solution)/shard_map/ppermute | solution.py:21
  72.6 0.6 turn.6.one_ref
  73.2 0.1 collective-permute-start.8
  73.2 0.6 turn.5.one_ref
  73.8 0.6 collective-permute-start.7
  74.4 0.6 turn.4.one_ref
  75.0 0.1 collective-permute-start.6
  75.1 0.6 collective-permute-done.9.other_ref
  75.7 1.3 %add_part.4.refs_0_ = f32[400,4096]{1,0:T(8,128)} custom-call(f32[400,1024]{1,0:T(8,128)S(1)} %turn.7.one_ref, f32[400,1024]{1,0:T(8,128)S(1)} %collective-permute-done.9.other_ref), custom_call_target="tpu_custom_call" | custom-call | flops 409600 | bytes 4915200 | tf_op jit(solution)/shard_map/add_part/pallas_call | solution.py:146
  77.0 1.0 %collective-permute-done.8.other_ref = f32[400,1024]{1,0:T(8,128)S(1)} collective-permute-done((f32[400,1024]{1,0:T(8,128)S(1)}, f32[400,1024]{1,0:T(8,128)S(1)}, u32[]{:S(2)}, u32[]{:S(2)}) %collective-permute-start.8) | collective-permute-done | bytes 1638432 | tf_op jit(solution)/shard_map/ppermute | solution.py:21
  78.0 1.3 %add_part.5.refs_0_ = f32[400,4096]{1,0:T(8,128)} custom-call(f32[400,1024]{1,0:T(8,128)S(1)} %turn.6.one_ref, f32[400,1024]{1,0:T(8,128)S(1)} %collective-permute-done.8.other_ref, f32[400,4096]{1,0:T(8,128)} %add_part.4.refs_0_), custom_call_target="tpu_custom_call", output_to_operand_aliasing={{}: (2, {})} | custom-call | flops 409600 | bytes 4915200 | tf_op jit(solution)/shard_map/add_part/pallas_call | solution.py:146
  79.4 1.0 %collective-permute-done.7.other_ref = f32[400,1024]{1,0:T(8,128)S(1)} collective-permute-done((f32[400,1024]{1,0:T(8,128)S(1)}, f32[400,1024]{1,0:T(8,128)S(1)}, u32[]{:S(2)}, u32[]{:S(2)}) %collective-permute-start.7) | collective-permute-done | bytes 1638432 | tf_op jit(solution)/shard_map/ppermute | solution.py:21
  80.4 1.3 %add_part.6.refs_0_ = f32[400,4096]{1,0:T(8,128)} custom-call(f32[400,1024]{1,0:T(8,128)S(1)} %turn.5.one_ref, f32[400,1024]{1,0:T(8,128)S(1)} %collective-permute-done.7.other_ref, f32[400,4096]{1,0:T(8,128)} %add_part.5.refs_0_), custom_call_target="tpu_custom_call", output_to_operand_aliasing={{}: (2, {})} | custom-call | flops 409600 | bytes 4915200 | tf_op jit(solution)/shard_map/add_part/pallas_call | solution.py:146
  81.7 1.0 %collective-permute-done.6.other_ref = f32[400,1024]{1,0:T(8,128)S(1)} collective-permute-done((f32[400,1024]{1,0:T(8,128)S(1)}, f32[400,1024]{1,0:T(8,128)S(1)}, u32[]{:S(2)}, u32[]{:S(2)}) %collective-permute-start.6) | collective-permute-done | bytes 1638432 | tf_op jit(solution)/shard_map/ppermute | solution.py:21
  82.7 1.3 %add_part.7 = f32[400,4096]{1,0:T(8,128)} custom-call(f32[400,1024]{1,0:T(8,128)S(1)} %turn.4.one_ref, f32[400,1024]{1,0:T(8,128)S(1)} %collective-permute-done.6.other_ref, f32[400,4096]{1,0:T(8,128)} %add_part.6.refs_0_), custom_call_target="tpu_custom_call", output_to_operand_aliasing={{}: (2, {})} | custom-call | flops 409600 | bytes 4915200 | tf_op jit(solution)/shard_map/add_part/pallas_call | solution.py:146
  (11 shorter events, 0.2 us)
Async XLA Ops:
  0.6 0.7 copy-start
  2.8 6.8 %collective-permute-start = (f32[1,80,256]{2,1,0:T(8,128)S(1)}, f32[1,80,256]{2,1,0:T(8,128)S(1)}, u32[]{:S(2)}, u32[]{:S(2)}) collective-permute-start(f32[1,80,256]{2,1,0:T(8,128)S(1)} %pack.1), channel_id=1, source_target_pairs={{0,4},{1,5},{2,6},{3,7},{4,0},{5,1},{6,2},{7,3},{8,12},{9,13},{10,... | collective-permute-start | bytes 245768 | tf_op jit(solution)/shard_map/ppermute | solution.py:21
  9.7 5.2 %collective-permute-start.1 = (f32[2,80,256]{2,1,0:T(8,128)S(1)}, f32[2,80,256]{2,1,0:T(8,128)S(1)}, u32[]{:S(2)}, u32[]{:S(2)}) collective-permute-start(f32[2,80,256]{2,1,0:T(8,128)S(1)} %pad_maximum_fusion.2), channel_id=1, source_target_pairs={{0,16},{8,24},{16,0},{24,8},{1,17},{9,25},{17,1},{25,9},{2,18},{10... | collective-permute-start | bytes 491528 | tf_op jit(solution)/shard_map/ppermute | solution.py:21
  11.0 4.8 %collective-permute-start.3 = (f32[2,80,256]{2,1,0:T(8,128)S(1)}, f32[2,80,256]{2,1,0:T(8,128)S(1)}, u32[]{:S(2)}, u32[]{:S(2)}) collective-permute-start(f32[2,80,256]{2,1,0:T(8,128)S(1)} %pad_maximum_fusion.2), channel_id=1, source_target_pairs={{0,2},{1,3},{2,0},{3,1},{4,6},{5,7},{6,4},{7,5},{8,10},{9,11},{10,... | collective-permute-start | bytes 491528 | tf_op jit(solution)/shard_map/ppermute | solution.py:21
  14.9 12.6 %collective-permute-start.2 = (f32[4,80,256]{2,1,0:T(8,128)S(1)}, f32[4,80,256]{2,1,0:T(8,128)S(1)}, u32[]{:S(2)}, u32[]{:S(2)}) collective-permute-start(f32[4,80,256]{2,1,0:T(8,128)S(1)} %pad_maximum_fusion), channel_id=1, source_target_pairs={{0,1},{1,0},{2,3},{3,2},{4,5},{5,4},{6,7},{7,6},{8,9},{9,8},{10,11... | collective-permute-start | bytes 983048 | tf_op jit(solution)/shard_map/ppermute | solution.py:21
  15.7 10.4 %collective-permute-start.4 = (f32[2,80,256]{2,1,0:T(8,128)S(1)}, f32[2,80,256]{2,1,0:T(8,128)S(1)}, u32[]{:S(2)}, u32[]{:S(2)}) collective-permute-start(f32[2,80,256]{2,1,0:T(8,128)S(1)} %collective-permute-done.3), channel_id=1, source_target_pairs={{0,1},{1,0},{2,3},{3,2},{4,5},{5,4},{6,7},{7,6},{8,9},{9,8},{10,11... | collective-permute-start | bytes 491528 | tf_op jit(solution)/shard_map/ppermute | solution.py:21
  26.1 6.8 %collective-permute-start.5 = (f32[4,80,256]{2,1,0:T(8,128)S(1)}, f32[4,80,256]{2,1,0:T(8,128)S(1)}, u32[]{:S(2)}, u32[]{:S(2)}) collective-permute-start(f32[4,80,256]{2,1,0:T(8,128)S(1)} %pad_maximum_fusion.1), channel_id=1, source_target_pairs={{0,16},{8,24},{16,0},{24,8},{1,17},{9,25},{17,1},{25,9},{2,18},{10... | collective-permute-start | bytes 983048 | tf_op jit(solution)/shard_map/ppermute | solution.py:21
  69.2 6.5 %collective-permute-start.9 = (f32[400,1024]{1,0:T(8,128)S(1)}, f32[400,1024]{1,0:T(8,128)S(1)}, u32[]{:S(2)}, u32[]{:S(2)}) collective-permute-start(f32[400,1024]{1,0:T(8,128)S(1)} %turn.7.one_ref), channel_id=1, source_target_pairs={{0,8},{8,0},{16,24},{24,16},{1,9},{9,1},{17,25},{25,17},{2,10},{10... | collective-permute-start | bytes 4915208 | tf_op jit(solution)/shard_map/ppermute | solution.py:21
  73.2 4.9 %collective-permute-start.8 = (f32[400,1024]{1,0:T(8,128)S(1)}, f32[400,1024]{1,0:T(8,128)S(1)}, u32[]{:S(2)}, u32[]{:S(2)}) collective-permute-start(f32[400,1024]{1,0:T(8,128)S(1)} %turn.6.one_ref), channel_id=1, source_target_pairs={{0,8},{8,0},{16,24},{24,16},{1,9},{9,1},{17,25},{25,17},{2,10},{10... | collective-permute-start | bytes 4915208 | tf_op jit(solution)/shard_map/ppermute | solution.py:21
  73.8 6.5 %collective-permute-start.7 = (f32[400,1024]{1,0:T(8,128)S(1)}, f32[400,1024]{1,0:T(8,128)S(1)}, u32[]{:S(2)}, u32[]{:S(2)}) collective-permute-start(f32[400,1024]{1,0:T(8,128)S(1)} %turn.5.one_ref), channel_id=1, source_target_pairs={{0,8},{8,0},{16,24},{24,16},{1,9},{9,1},{17,25},{25,17},{2,10},{10... | collective-permute-start | bytes 4915208 | tf_op jit(solution)/shard_map/ppermute | solution.py:21
  75.0 7.7 %collective-permute-start.6 = (f32[400,1024]{1,0:T(8,128)S(1)}, f32[400,1024]{1,0:T(8,128)S(1)}, u32[]{:S(2)}, u32[]{:S(2)}) collective-permute-start(f32[400,1024]{1,0:T(8,128)S(1)} %turn.4.one_ref), channel_id=1, source_target_pairs={{0,8},{8,0},{16,24},{24,16},{1,9},{9,1},{17,25},{25,17},{2,10},{10... | collective-permute-start | bytes 4915208 | tf_op jit(solution)/shard_map/ppermute | solution.py:21

commit v4 on v3

--- a/solution.py
+++ b/solution.py
@@ -51,52 +51,56 @@
     return jnp.dot(a, b, preferred_element_type=jnp.float32)
 
 
+def packing(half, rows, blocks, part_rows):
+    width = LANE_TILES // 2 * LANES
+    count = 4 * blocks + blocks * (part_rows // width) + 1
+    room = width - half
+    pieces = -(-width // room)
+    return count, room, pieces, max(2 * rows, -(-pieces * count // 8) * 8)
+
+
 def pack_kernel(half, part_rows, counts, entities, src, dst, rel, neg, weight, out_ref):
     rows = entities.shape[0]
     blocks, edges = src.shape[1:]
-    width = out_ref.shape[2]
+    width, height = out_ref.shape[2], out_ref.shape[1]
     draws = neg.shape[2]
-    base = rows + 4 * blocks
-    gap = jnp.zeros((rows, width - half), jnp.float32)
-    out = out_ref.at[0]
-    out[:rows, :] = jnp.concatenate([entities[:, :half], gap], axis=1)
-    out[base : base + rows, :] = jnp.concatenate([entities[:, half:], gap], axis=1)
-    for k, ids in enumerate((src, dst, rel)):
-        out[rows + k * blocks : rows + (k + 1) * blocks, :] = ids[0].astype(jnp.float32)
+    data = [ids[0].astype(jnp.float32) for ids in (src, dst, rel)]
     slot = lax.broadcasted_iota(jnp.int32, (1, edges), 1)
     for i in range(blocks):
-        row = rows + 3 * blocks + i
-        out[row : row + 1, :] = jnp.where(slot < counts[0, i], weight[0, i : i + 1, :], 0.0)
-    top = base + rows
+        data.append(jnp.where(slot < counts[0, i], weight[0, i : i + 1, :], 0.0))
     drawn = jnp.concatenate([neg[0], jnp.zeros((8 - blocks, draws), jnp.int32)], axis=0).astype(jnp.float32)
     drawn = drawn.T.astype(jnp.int32)
     lane = lax.broadcasted_iota(jnp.int32, (draws, part_rows), 1)
     for i in range(blocks):
         hits = jnp.where(drawn[:, i : i + 1] == lane, 1.0, 0.0).astype(jnp.bfloat16)
         times = dot(jnp.ones((8, draws), jnp.bfloat16), hits)[:1] / draws
-        for part in range(part_rows // width):
-            row = top + i * (part_rows // width) + part
-            out[row : row + 1, :] = times[:, part * width : (part + 1) * width]
-    top += blocks * (part_rows // width)
-    spare = out_ref.shape[1] - top
-    lane = lax.broadcasted_iota(jnp.int32, (spare, width), 1)
-    last = jnp.zeros((spare, width), jnp.float32)
+        data += [times[:, low : low + width] for low in range(0, part_rows, width)]
+    last = jnp.zeros((1, width), jnp.float32)
     for i in range(blocks):
-        last = jnp.where(lane == i, counts[0, i].astype(jnp.float32), last)
-    out[top:, :] = last
+        last = jnp.where(slot == i, counts[0, i].astype(jnp.float32), last)
+    data = jnp.concatenate(data + [last], axis=0)
+    count, room, pieces, _ = packing(half, rows, blocks, part_rows)
+    cut = [pltpu.roll(data, (half - room * piece) % width, 1) for piece in range(pieces)]
+    cut.append(jnp.zeros((height - pieces * count, width), jnp.float32))
+    beside = jnp.concatenate(cut, axis=0)
+    gap = jnp.zeros((2 * rows, width - half), jnp.float32)
+    held = jnp.concatenate([entities[:, :half], entities[:, half:]], axis=0)
+    held = jnp.concatenate([held, gap], axis=1)
+    if height > 2 * rows:
+        held = jnp.concatenate([held, jnp.zeros((height - 2 * rows, width), jnp.float32)], axis=0)
+    out_ref[0] = jnp.where(lax.broadcasted_iota(jnp.int32, held.shape, 1) < half, held, beside)
 
 
 def packed(entities, counts, src, dst, rel, neg, weight, part_rows):
     rows, dim = entities.shape
-    blocks = src.shape[1]
     width = LANE_TILES // 2 * LANES
-    height = 2 * rows + 4 * blocks + blocks * (part_rows // width) + 1
+    height = packing(dim // 2, rows, src.shape[1], part_rows)[3]
     vmem = pl.BlockSpec(memory_space=pltpu.VMEM)
     return pl.pallas_call(
         functools.partial(pack_kernel, dim // 2, part_rows),
         in_specs=[pl.BlockSpec(memory_space=pltpu.SMEM)] + [vmem] * 6,
         out_specs=vmem,
-        out_shape=jax.ShapeDtypeStruct((1, -(-height // 8) * 8, width), jnp.float32),
+        out_shape=jax.ShapeDtypeStruct((1, height, width), jnp.float32),
         compiler_params=pltpu.CompilerParams(vmem_limit_bytes=SMALL_BYTES),
         name="pack",
     )(counts, *[in_hbm(x) for x in (entities, src, dst, rel, neg, weight)])
@@ -110,10 +114,11 @@
     return pltpu.with_memory_space_constraint(x, pltpu.HBM)
 
 
-def finish_kernel(half, low, acc_ref, out_ref):
+def finish_kernel(half, low, *refs):
+    accs, out_ref = refs[:-1], refs[-1]
     for i in range(out_ref.shape[1] // LANES):
         for q in range(LANE_TILES):
-            rows = tiles(acc_ref, low + i * LANES, LANES, q).T
+            rows = sum(tiles(acc, low + i * LANES, LANES, q) for acc in accs).T
             top = (q // 2) * half + (q % 2) * LANES
             size = min(LANES, half - (q % 2) * LANES)
             out_ref[top : top + size, i * LANES : (i + 1) * LANES] = rows[:size]
@@ -123,20 +128,20 @@
     refs[-1][...] = one_ref[...] + other_ref[...]
 
 
-def summed(acc, dim, bits):
-    count = acc.shape[0]
+def summed(accs, dim, bits):
+    count = accs[0].shape[0]
     size = count // PARTS
     parts = []
     for k in range(PARTS):
         part = pl.pallas_call(
             functools.partial(finish_kernel, dim // 2, k * size),
-            in_specs=[pl.BlockSpec(memory_space=pltpu.VMEM)],
+            in_specs=[pl.BlockSpec(memory_space=pltpu.VMEM)] * len(accs),
             out_specs=pl.BlockSpec(memory_space=pltpu.VMEM),
             out_shape=pltpu.VMEM((dim, size), jnp.float32),
             cost_estimate=pl.CostEstimate(flops=0, bytes_accessed=size * dim * 8, transcendentals=0),
             compiler_params=pltpu.CompilerParams(vmem_limit_bytes=SMALL_BYTES),
             name="turn",
-        )(in_vmem(acc))
+        )(*[in_vmem(acc) for acc in accs])
         for bit in bits[:-1]:
             part = part + swap(part, "dom", bit)
         parts.append((part, swap(part, "dom", bits[-1])))
@@ -162,7 +167,8 @@
     return flat[pl.ds(low * LANE_TILES + q, count, stride=LANE_TILES), :]
 
 
-STAGES = 5
+STAGES = 4
+SCRATCH = 16
 
 
 def in_turn(parts, *sides):
@@ -174,20 +180,20 @@
                     next(side, None)
 
 
-def main_kernel(spec, live, where, relations, blocks_of, acc, ent_ref, *scratch):
+def main_kernel(spec, live, where, relations, blocks_of, *refs):
+    accs, ent_ref, scratch = refs[:-SCRATCH][:-1], refs[:-SCRATCH][-1], refs[-SCRATCH:]
     (half, rows, shards, blocks, edges) = spec
-    (columns_of, table, ent, stack, stack_t, times, info, ids_v, ids, factor, grads, flip, mine, band, seg, come) = scratch
+    (data_rows, columns_of, table, ent, stack, stack_t, times, info, ids_v, ids, factor, grads, flip, mine, seg, come) = scratch
     width = LANE_TILES // 2 * LANES
     part_rows = rows * shards
     group = shards * blocks
     total = group * edges // 2
     bits = shards.bit_length() - 1
-    base = rows + 4 * blocks
-    top = base + rows
+    count, room, pieces, _ = packing(half, rows, blocks, part_rows)
     me, side = where[0], where[1]
     own = me * rows
 
-    steps = acc.shape[0] // STEP
+    steps = accs[0].shape[0] // STEP
     arrivals = []
     for k in range(steps):
         at = pl.ds(k * STEP, STEP)
@@ -196,16 +202,23 @@
 
     mine[...] = jnp.zeros_like(mine)
     info[...] = jnp.zeros_like(info)
-    down = lax.broadcasted_iota(jnp.int32, band.shape, 0)
-    across = lax.broadcasted_iota(jnp.int32, band.shape, 1)
-    band[...] = jnp.where((across <= down) & (across // GROUP == down // GROUP), 1.0, 0.0)
 
     for x in range(2):
         for j in range(shards):
             k = block_index(j, x, bits)
             at = pl.ds(pl.multiple_of((j ^ me) * rows, 8), rows)
-            ent[at, :width] = blocks_of[k, :rows, :]
-            ent[at, width:] = blocks_of[k, base : base + rows, :]
+            lane = lax.broadcasted_iota(jnp.int32, (rows, width), 1)
+            for part in range(2):
+                square = blocks_of[k, part * rows : (part + 1) * rows, :]
+                ent[at, part * width : (part + 1) * width] = jnp.where(lane < half, square, 0.0)
+            lane = lax.broadcasted_iota(jnp.int32, (count, width), 1)
+            raw = jnp.zeros((count, width), jnp.float32)
+            for piece in range(pieces):
+                square = pltpu.roll(
+                    blocks_of[k, piece * count : (piece + 1) * count, :], (room * piece - half) % width, 1
+                )
+                raw = jnp.where((lane >= room * piece) & (lane < room * (piece + 1)), square, raw)
+            data_rows[k, :count, :] = raw
         whole = ent[...]
         high, low = high_low(whole)
         stack[x] = jnp.concatenate([high, low, high], axis=0)
@@ -216,16 +229,16 @@
         rows_of = []
         for n in range(group):
             k = block_index((n // blocks) ^ me, x, bits)
-            low = top + (n % blocks) * (part_rows // width)
-            pieces = [blocks_of[k, low + i : low + i + 1, :] for i in range(part_rows // width)]
-            rows_of.append(jnp.concatenate(pieces, axis=1))
+            low = 4 * blocks + (n % blocks) * (part_rows // width)
+            whole = [data_rows[k, low + i : low + i + 1, :] for i in range(part_rows // width)]
+            rows_of.append(jnp.concatenate(whole, axis=1))
         high, low = high_low(jnp.concatenate(rows_of, axis=0))
         times[x] = jnp.concatenate([high, low], axis=0)
 
         def lay(n, offset):
             k, slot = block_index((n // blocks) ^ me, x, bits), n % blocks
-            count = live[k * blocks + slot]
-            tile = blocks_of[k, rows : rows + 4 * blocks, :]
+            alive = live[k * blocks + slot]
+            tile = data_rows[k, : 4 * blocks, :]
 
             def chosen(k):
                 row = tile[k * blocks : k * blocks + 1]
@@ -236,12 +249,12 @@
             number = jnp.zeros((1, edges), jnp.float32) + n.astype(jnp.float32)
             data = [chosen(k) for k in range(4)] + [number, jnp.zeros((3, edges), jnp.float32)]
             data = jnp.concatenate(data, axis=0)
-            data = jnp.where(lax.broadcasted_iota(jnp.int32, data.shape, 1) < count, data, 0.0)
+            data = jnp.where(lax.broadcasted_iota(jnp.int32, data.shape, 1) < alive, data, 0.0)
             data = jnp.concatenate([data, jnp.zeros((8, LANES), jnp.float32)], axis=1)
             data = pltpu.roll(data, offset % LANES, 1)
             at = pl.ds(pl.multiple_of((offset // LANES) * LANES, LANES), edges + LANES)
             info[x, :, at] = info[x, :, at] + data
-            return offset + count
+            return offset + alive
 
         lax.fori_loop(0, group, lay, jnp.int32(0))
         for i in range(total // LANES):
@@ -261,9 +274,10 @@
             for j in range(LANE_TILES // 2):
                 to = pl.ds(low * LANE_TILES + part * (LANE_TILES // 2) + j, STEP, stride=LANE_TILES)
                 flat[to, :] = square[:, j * LANES : (j + 1) * LANES]
-        flat = acc.reshape(acc.shape[0] * LANE_TILES, LANES)
         to = pl.ds(pl.multiple_of(low * LANE_TILES, 8), STEP * LANE_TILES)
-        flat[to, :] = jnp.zeros((STEP * LANE_TILES, LANES), jnp.float32)
+        for acc in accs:
+            flat = acc.reshape(acc.shape[0] * LANE_TILES, LANES)
+            flat[to, :] = jnp.zeros((STEP * LANE_TILES, LANES), jnp.float32)
         return carry
 
     lax.fori_loop(0, steps, turn, 0)
@@ -299,12 +313,8 @@
         ).astype(jnp.bfloat16)
         often = dot(which, times[x])
 
-        small = jnp.exp(-jnp.abs(scores))
-        near = 1.0 / (1.0 + small)
-        far = small * near
-        up = scores >= 0.0
-        sig = jnp.where(up, near, far)
-        sig_neg = jnp.where(up, far, near)
+        sig = 1.0 / (1.0 + jnp.exp(-scores))
+        sig_neg = 1.0 / (1.0 + jnp.exp(scores))
         g = sig * often - jnp.where(target_col == lane, sig_neg, 0.0)
         g = g * weight_col
         g_high, g_low = high_low(g)
@@ -312,10 +322,6 @@
         yield
         g_re, g_im = gq[:, :width], gq[:, width:]
         gw = jnp.concatenate([g_re * s_re + g_im * s_im, g_im * s_re - g_re * s_im], axis=1)
-        same = jnp.where(columns[:, 2:3] == data[2:3], band[...], 0.0).astype(jnp.bfloat16)
-        w_high, w_low = high_low(gw)
-        gw = dot(jnp.concatenate([same, same], axis=1), jnp.concatenate([w_high, w_low], axis=0))
-        yield
         flat = grads.reshape(4 * CHUNK * LANE_TILES, LANES)
         for q in range(LANE_TILES):
             at = pl.ds((slot * 2 + x) * CHUNK * LANE_TILES + q, CHUNK, stride=LANE_TILES)
@@ -348,14 +354,14 @@
             yield
 
     def push(c, slot):
-        for turn in range(2):
-            x = turn ^ side
-            for e in range(0, CHUNK, GROUP):
-                at = [ids[x, c * per + e // LANES, e % LANES + u] for u in range(GROUP)]
-                new = [acc[r] + grads[(slot * 2 + x) * CHUNK + e + u] for u, r in enumerate(at)]
-                for r, value in zip(at, new):
-                    acc[r] = value
-                yield
+        for e in range(0, CHUNK, GROUP):
+            for u in range(GROUP):
+                for order in range(2):
+                    acc = accs[order % len(accs)]
+                    x = order ^ side
+                    r = ids[x, c * per + e // LANES, e % LANES + u]
+                    acc[r] = acc[r] + grads[(slot * 2 + x) * CHUNK + e + u]
+            yield
 
     def drain(steps):
         for _ in steps:
@@ -366,7 +372,7 @@
         in_turn(
             [compute(x, c * CHUNK, slot) for x in range(2)],
             (fetch(jnp.minimum(c + 1, last), 1 - slot), CHUNK // 8),
-            (push(jnp.maximum(c - 1, 0), 1 - slot), 2 * CHUNK // GROUP),
+            (push(jnp.maximum(c - 1, 0), 1 - slot), CHUNK // GROUP),
         )
         return carry
 
@@ -389,17 +395,19 @@
     relation_count = relations.shape[0]
     group = shards * blocks
     total = group * edges // 2
+    totals = 2 if part_rows <= 256 else 1
     smem = pl.BlockSpec(memory_space=pltpu.SMEM)
     vmem = pl.BlockSpec(memory_space=pltpu.VMEM)
     return pl.pallas_call(
         functools.partial(main_kernel, spec),
         in_specs=[smem, smem, pl.BlockSpec(memory_space=pl.ANY), vmem],
-        out_specs=(vmem, vmem),
+        out_specs=(vmem,) * (totals + 1),
         out_shape=(
-            pltpu.VMEM((relation_count, LANE_TILES, LANES), jnp.float32),
+            *[pltpu.VMEM((relation_count, LANE_TILES, LANES), jnp.float32)] * totals,
             jax.ShapeDtypeStruct((rows, dim), jnp.float32),
         ),
         scratch_shapes=[
+            pltpu.VMEM((2 * shards, -(-packing(half, rows, blocks, part_rows)[0] // 8) * 8, width), jnp.float32),
             pltpu.VMEM((dim, relation_count), jnp.float32),
             pltpu.VMEM((relation_count, LANE_TILES, LANES), jnp.float32),
             pltpu.VMEM((part_rows, 2 * width), jnp.float32),
@@ -413,7 +421,6 @@
             pltpu.VMEM((4 * CHUNK, LANE_TILES, LANES), jnp.float32),
             pltpu.VMEM((part_rows, CHUNK), jnp.float32),
             pltpu.VMEM((rows, 2 * width), jnp.float32),
-            pltpu.VMEM((CHUNK, CHUNK), jnp.float32),
             pltpu.SemaphoreType.DMA,
             pltpu.SemaphoreType.DMA((relation_count // STEP,)),
         ],
@@ -424,7 +431,6 @@
 
 def body(entities, relations, src_index, dst_index, rel_index, neg_index, counts, edge_weight):
     rows, dim = entities.shape
-    width = LANE_TILES // 2 * LANES
     blocks, edges = src_index.shape[1:]
     dom_count, shards = lax.axis_size("dom"), lax.axis_size("block")
     part_rows = rows * shards
@@ -435,13 +441,13 @@
     block = packed(entities, counts, src_index, dst_index, rel_index, neg_index, edge_weight, part_rows)
     upper = [("block", bit) for bit in reversed(range(1, block_bits))]
     blocks_of = gather_all(block, upper, [("dom", partner_bit), ("block", 0)])
-    last = 2 * rows + 4 * blocks + blocks * (part_rows // width)
-    live = blocks_of[:, last, :blocks].astype(jnp.int32).reshape(-1)
+    last = packing(dim // 2, rows, blocks, part_rows)[0] - 1
+    live = blocks_of[:, last, dim // 2 : dim // 2 + blocks].astype(jnp.int32).reshape(-1)
     where = jnp.stack([lax.axis_index("block"), (lax.axis_index("dom") >> partner_bit) & 1]).astype(jnp.int32)
 
     spec = (dim // 2, rows, shards, blocks, edges)
-    acc, entity_grad = gradients(spec, relations, live, where, blocks_of)
-    return entity_grad, summed(acc, dim, other_bits).T
+    *accs, entity_grad = gradients(spec, relations, live, where, blocks_of)
+    return entity_grad, summed(accs, dim, other_bits).T
 
 
 def solution(mesh):

time: 84.2 us -> 78.2 us (0.929)
  the two profiles are of different devices: /device:TPU:29 before, /device:TPU:0 now
where the time goes in v4:
time: 78.2 us; the launch traced here: 77.3 us
  Pallas kernels  43 us (55%)
  waiting for transfers between devices  18.7 us (24%)
  starting transfers between devices  12.5 us (16%)
  local copies, waits for them, and re-layouts  1.59 us (2%)
  other arithmetic  0.79 us (1%)
    pallas_call x1, Pallas kernels, gradients(): pl.pallas_call(functools.partial(main_kernel, spec), in_specs=[smem, smem...  33.7 us
    ppermute x10, waiting for transfers between devices, swap(): return lax.ppermute(x, axis, [(i, i ^ 1 << bit) for i in range(count)])  18.7 us
    ppermute x10, starting transfers between devices, swap(): return lax.ppermute(x, axis, [(i, i ^ 1 << bit) for i in range(count)])  12.5 us
    pallas_call x4, Pallas kernels, summed(): pl.pallas_call(add_kernel, grid=(1,), in_specs=[block, block] + ([] if to...  5.32 us
    pallas_call x4, Pallas kernels, summed(): pl.pallas_call(functools.partial(finish_kernel, dim // 2, k * size), in_s...  2.38 us
    pallas_call x1, Pallas kernels, packed(): pl.pallas_call(functools.partial(pack_kernel, dim // 2, part_rows), in_sp...  1.63 us
  transfers between devices with their start and end apart: 10, of which 8 were waited for; matrix products, arithmetic and copies ran while one was open for 1% of the time, Pallas kernels for 7%

profile of v4, /device:TPU:0, one launch (start us, length us, event | category | flops | bytes accessed | tf_op | source)
XLA Modules:
  0.0 77.3 jit_solution(10824764844591477610)
XLA Ops:
  0.6 0.0 copy-start
  0.6 0.6 copy-done
  1.3 1.6 %pack.1 = f32[1,64,256]{2,1,0:T(8,128)S(1)} custom-call(s32[1,2]{1,0:T(1,128)S(1)} %copy-done, f32[32,400]{1,0:T(8,128)} %entities.1, s32[1,2,256]{2,1,0:T(2,128)} %src.1, s32[1,2,256]{2,1,0:T(2,128)} %dst.1, s32[1,2,256]{2,1,0:T(2,128)} %rel.1, s32[1,2,1024]{2,1,0:T(2,128)} %neg.1, f32[1,2,256]{2,1,0:T(2,128)} %weight.1), custom_call_target="tpu_custom_call" | custom-call | tf_op jit(solution)/shard_map/pack/pallas_call | solution.py:99
  2.9 4.1 %collective-permute-start = (f32[1,64,256]{2,1,0:T(8,128)S(1)}, f32[1,64,256]{2,1,0:T(8,128)S(1)}, u32[]{:S(2)}, u32[]{:S(2)}) collective-permute-start(f32[1,64,256]{2,1,0:T(8,128)S(1)} %pack.1), channel_id=1, source_target_pairs={{0,4},{1,5},{2,6},{3,7},{4,0},{5,1},{6,2},{7,3},{8,12},{9,13},{10,... | collective-permute-start | bytes 196616 | tf_op jit(solution)/shard_map/ppermute | solution.py:21
  7.0 3.6 %collective-permute-done = f32[1,64,256]{2,1,0:T(8,128)S(1)} collective-permute-done((f32[1,64,256]{2,1,0:T(8,128)S(1)}, f32[1,64,256]{2,1,0:T(8,128)S(1)}, u32[]{:S(2)}, u32[]{:S(2)}) %collective-permute-start) | collective-permute-done | bytes 65568 | tf_op jit(solution)/shard_map/ppermute | solution.py:21
  10.7 1.8 %collective-permute-start.1 = (f32[2,64,256]{2,1,0:T(8,128)S(1)}, f32[2,64,256]{2,1,0:T(8,128)S(1)}, u32[]{:S(2)}, u32[]{:S(2)}) collective-permute-start(f32[2,64,256]{2,1,0:T(8,128)S(1)} %pad_maximum_fusion.2), channel_id=1, source_target_pairs={{0,16},{8,24},{16,0},{24,8},{1,17},{9,25},{17,1},{25,9},{2,18},{10... | collective-permute-start | bytes 393224 | tf_op jit(solution)/shard_map/ppermute | solution.py:21
  12.5 0.4 collective-permute-start.3
  12.8 0.6 pad_add_fusion.where
  13.5 2.3 %collective-permute-done.1 = f32[2,64,256]{2,1,0:T(8,128)S(1)} collective-permute-done((f32[2,64,256]{2,1,0:T(8,128)S(1)}, f32[2,64,256]{2,1,0:T(8,128)S(1)}, u32[]{:S(2)}, u32[]{:S(2)}) %collective-permute-start.1) | collective-permute-done | bytes 131104 | tf_op jit(solution)/shard_map/ppermute | solution.py:21
  15.8 1.8 %collective-permute-start.2 = (f32[4,64,256]{2,1,0:T(8,128)S(1)}, f32[4,64,256]{2,1,0:T(8,128)S(1)}, u32[]{:S(2)}, u32[]{:S(2)}) collective-permute-start(f32[4,64,256]{2,1,0:T(8,128)S(1)} %pad_maximum_fusion), channel_id=1, source_target_pairs={{0,1},{1,0},{2,3},{3,2},{4,5},{5,4},{6,7},{7,6},{8,9},{9,8},{10,11... | collective-permute-start | bytes 786440 | tf_op jit(solution)/shard_map/ppermute | solution.py:21
  17.5 0.0 collective-permute-done.3
  17.5 1.4 %collective-permute-start.4 = (f32[2,64,256]{2,1,0:T(8,128)S(1)}, f32[2,64,256]{2,1,0:T(8,128)S(1)}, u32[]{:S(2)}, u32[]{:S(2)}) collective-permute-start(f32[2,64,256]{2,1,0:T(8,128)S(1)} %collective-permute-done.3), channel_id=1, source_target_pairs={{0,1},{1,0},{2,3},{3,2},{4,5},{5,4},{6,7},{7,6},{8,9},{9,8},{10,11... | collective-permute-start | bytes 393224 | tf_op jit(solution)/shard_map/ppermute | solution.py:21
  19.0 4.6 %collective-permute-done.4 = f32[2,64,256]{2,1,0:T(8,128)S(1)} collective-permute-done((f32[2,64,256]{2,1,0:T(8,128)S(1)}, f32[2,64,256]{2,1,0:T(8,128)S(1)}, u32[]{:S(2)}, u32[]{:S(2)}) %collective-permute-start.4) | collective-permute-done | bytes 131104 | tf_op jit(solution)/shard_map/ppermute | solution.py:21
  23.6 1.8 %collective-permute-start.5 = (f32[4,64,256]{2,1,0:T(8,128)S(1)}, f32[4,64,256]{2,1,0:T(8,128)S(1)}, u32[]{:S(2)}, u32[]{:S(2)}) collective-permute-start(f32[4,64,256]{2,1,0:T(8,128)S(1)} %pad_maximum_fusion.1), channel_id=1, source_target_pairs={{0,16},{8,24},{16,0},{24,8},{1,17},{9,25},{17,1},{25,9},{2,18},{10... | collective-permute-start | bytes 786440 | tf_op jit(solution)/shard_map/ppermute | solution.py:21
  25.4 0.0 collective-permute-done.2
  25.4 4.6 %collective-permute-done.5 = f32[4,64,256]{2,1,0:T(8,128)S(1)} collective-permute-done((f32[4,64,256]{2,1,0:T(8,128)S(1)}, f32[4,64,256]{2,1,0:T(8,128)S(1)}, u32[]{:S(2)}, u32[]{:S(2)}) %collective-permute-start.5) | collective-permute-done | bytes 262176 | tf_op jit(solution)/shard_map/ppermute | solution.py:21
  30.1 0.0 copy-start.1
  30.1 0.1 fusion
  30.2 0.8 convert_element_type.8.live
  31.0 0.1 copy-done.1
  31.0 33.7 %gradients.1 = (f32[4096,4,128]{2,1,0:T(4,128)S(1)}, f32[4096,4,128]{2,1,0:T(4,128)S(1)}, f32[32,400]{1,0:T(8,128)}) custom-call(s32[32]{0:T(128)} %convert_element_type.8.live, s32[2]{0:T(128)} %pad_add_fusion.where, f32[400,4096]{1,0:T(8,128)} %bitcast.5, f32[16,64,256]{2,1,0:T(8,128)} %copy-done.1), custom_call_target="tpu_custom_call" | custom-call | tf_op jit(solution)/shard_map/gradients/pallas_call | solution.py:401
  64.8 0.6 turn.7.one_ref
  65.4 0.1 collective-permute-start.9
  65.4 0.6 turn.6.one_ref
  66.0 0.6 collective-permute-start.8
  66.6 0.6 turn.5.one_ref
  67.2 0.1 collective-permute-start.7
  67.3 0.6 turn.4.one_ref
  67.9 0.6 collective-permute-start.6
  68.5 0.5 collective-permute-done.9.other_ref
  68.9 1.3 %add_part.4.refs_0_ = f32[400,4096]{1,0:T(8,128)} custom-call(f32[400,1024]{1,0:T(8,128)S(1)} %turn.7.one_ref, f32[400,1024]{1,0:T(8,128)S(1)} %collective-permute-done.9.other_ref), custom_call_target="tpu_custom_call" | custom-call | flops 409600 | bytes 4915200 | tf_op jit(solution)/shard_map/add_part/pallas_call | solution.py:151
  70.3 1.0 %collective-permute-done.8.other_ref = f32[400,1024]{1,0:T(8,128)S(1)} collective-permute-done((f32[400,1024]{1,0:T(8,128)S(1)}, f32[400,1024]{1,0:T(8,128)S(1)}, u32[]{:S(2)}, u32[]{:S(2)}) %collective-permute-start.8) | collective-permute-done | bytes 1638432 | tf_op jit(solution)/shard_map/ppermute | solution.py:21
  71.3 1.3 %add_part.5.refs_0_ = f32[400,4096]{1,0:T(8,128)} custom-call(f32[400,1024]{1,0:T(8,128)S(1)} %turn.6.one_ref, f32[400,1024]{1,0:T(8,128)S(1)} %collective-permute-done.8.other_ref, f32[400,4096]{1,0:T(8,128)} %add_part.4.refs_0_), custom_call_target="tpu_custom_call", output_to_operand_aliasing={{}: (2, {})} | custom-call | flops 409600 | bytes 4915200 | tf_op jit(solution)/shard_map/add_part/pallas_call | solution.py:151
  72.6 1.0 %collective-permute-done.7.other_ref = f32[400,1024]{1,0:T(8,128)S(1)} collective-permute-done((f32[400,1024]{1,0:T(8,128)S(1)}, f32[400,1024]{1,0:T(8,128)S(1)}, u32[]{:S(2)}, u32[]{:S(2)}) %collective-permute-start.7) | collective-permute-done | bytes 1638432 | tf_op jit(solution)/shard_map/ppermute | solution.py:21
  73.6 1.3 %add_part.6.refs_0_ = f32[400,4096]{1,0:T(8,128)} custom-call(f32[400,1024]{1,0:T(8,128)S(1)} %turn.5.one_ref, f32[400,1024]{1,0:T(8,128)S(1)} %collective-permute-done.7.other_ref, f32[400,4096]{1,0:T(8,128)} %add_part.5.refs_0_), custom_call_target="tpu_custom_call", output_to_operand_aliasing={{}: (2, {})} | custom-call | flops 409600 | bytes 4915200 | tf_op jit(solution)/shard_map/add_part/pallas_call | solution.py:151
  75.0 1.0 %collective-permute-done.6.other_ref = f32[400,1024]{1,0:T(8,128)S(1)} collective-permute-done((f32[400,1024]{1,0:T(8,128)S(1)}, f32[400,1024]{1,0:T(8,128)S(1)}, u32[]{:S(2)}, u32[]{:S(2)}) %collective-permute-start.6) | collective-permute-done | bytes 1638432 | tf_op jit(solution)/shard_map/ppermute | solution.py:21
  76.0 1.3 %add_part.7 = f32[400,4096]{1,0:T(8,128)} custom-call(f32[400,1024]{1,0:T(8,128)S(1)} %turn.4.one_ref, f32[400,1024]{1,0:T(8,128)S(1)} %collective-permute-done.6.other_ref, f32[400,4096]{1,0:T(8,128)} %add_part.6.refs_0_), custom_call_target="tpu_custom_call", output_to_operand_aliasing={{}: (2, {})} | custom-call | flops 409600 | bytes 4915200 | tf_op jit(solution)/shard_map/add_part/pallas_call | solution.py:151
  (10 shorter events, 0.1 us)
Async XLA Ops:
  0.6 0.7 copy-start
  2.9 7.8 %collective-permute-start = (f32[1,64,256]{2,1,0:T(8,128)S(1)}, f32[1,64,256]{2,1,0:T(8,128)S(1)}, u32[]{:S(2)}, u32[]{:S(2)}) collective-permute-start(f32[1,64,256]{2,1,0:T(8,128)S(1)} %pack.1), channel_id=1, source_target_pairs={{0,4},{1,5},{2,6},{3,7},{4,0},{5,1},{6,2},{7,3},{8,12},{9,13},{10,... | collective-permute-start | bytes 196616 | tf_op jit(solution)/shard_map/ppermute | solution.py:21
  10.7 5.0 %collective-permute-start.1 = (f32[2,64,256]{2,1,0:T(8,128)S(1)}, f32[2,64,256]{2,1,0:T(8,128)S(1)}, u32[]{:S(2)}, u32[]{:S(2)}) collective-permute-start(f32[2,64,256]{2,1,0:T(8,128)S(1)} %pad_maximum_fusion.2), channel_id=1, source_target_pairs={{0,16},{8,24},{16,0},{24,8},{1,17},{9,25},{17,1},{25,9},{2,18},{10... | collective-permute-start | bytes 393224 | tf_op jit(solution)/shard_map/ppermute | solution.py:21
  12.5 5.1 %collective-permute-start.3 = (f32[2,64,256]{2,1,0:T(8,128)S(1)}, f32[2,64,256]{2,1,0:T(8,128)S(1)}, u32[]{:S(2)}, u32[]{:S(2)}) collective-permute-start(f32[2,64,256]{2,1,0:T(8,128)S(1)} %pad_maximum_fusion.2), channel_id=1, source_target_pairs={{0,2},{1,3},{2,0},{3,1},{4,6},{5,7},{6,4},{7,5},{8,10},{9,11},{10,... | collective-permute-start | bytes 393224 | tf_op jit(solution)/shard_map/ppermute | solution.py:21
  15.8 9.6 %collective-permute-start.2 = (f32[4,64,256]{2,1,0:T(8,128)S(1)}, f32[4,64,256]{2,1,0:T(8,128)S(1)}, u32[]{:S(2)}, u32[]{:S(2)}) collective-permute-start(f32[4,64,256]{2,1,0:T(8,128)S(1)} %pad_maximum_fusion), channel_id=1, source_target_pairs={{0,1},{1,0},{2,3},{3,2},{4,5},{5,4},{6,7},{7,6},{8,9},{9,8},{10,11... | collective-permute-start | bytes 786440 | tf_op jit(solution)/shard_map/ppermute | solution.py:21
  17.5 6.0 %collective-permute-start.4 = (f32[2,64,256]{2,1,0:T(8,128)S(1)}, f32[2,64,256]{2,1,0:T(8,128)S(1)}, u32[]{:S(2)}, u32[]{:S(2)}) collective-permute-start(f32[2,64,256]{2,1,0:T(8,128)S(1)} %collective-permute-done.3), channel_id=1, source_target_pairs={{0,1},{1,0},{2,3},{3,2},{4,5},{5,4},{6,7},{7,6},{8,9},{9,8},{10,11... | collective-permute-start | bytes 393224 | tf_op jit(solution)/shard_map/ppermute | solution.py:21
  23.6 6.4 %collective-permute-start.5 = (f32[4,64,256]{2,1,0:T(8,128)S(1)}, f32[4,64,256]{2,1,0:T(8,128)S(1)}, u32[]{:S(2)}, u32[]{:S(2)}) collective-permute-start(f32[4,64,256]{2,1,0:T(8,128)S(1)} %pad_maximum_fusion.1), channel_id=1, source_target_pairs={{0,16},{8,24},{16,0},{24,8},{1,17},{9,25},{17,1},{25,9},{2,18},{10... | collective-permute-start | bytes 786440 | tf_op jit(solution)/shard_map/ppermute | solution.py:21
  30.1 1.0 %copy-start.1 = (f32[16,64,256]{2,1,0:T(8,128)}, f32[16,64,256]{2,1,0:T(8,128)S(1)}, u32[]{:S(2)}) copy-start(f32[16,64,256]{2,1,0:T(8,128)S(1)} %constant_dynamic-update-slice_fusion.blocks_of) | copy-start | bytes 3145732
  65.4 3.6 %collective-permute-start.9 = (f32[400,1024]{1,0:T(8,128)S(1)}, f32[400,1024]{1,0:T(8,128)S(1)}, u32[]{:S(2)}, u32[]{:S(2)}) collective-permute-start(f32[400,1024]{1,0:T(8,128)S(1)} %turn.7.one_ref), channel_id=1, source_target_pairs={{0,8},{8,0},{16,24},{24,16},{1,9},{9,1},{17,25},{25,17},{2,10},{10... | collective-permute-start | bytes 4915208 | tf_op jit(solution)/shard_map/ppermute | solution.py:21
  66.0 5.2 %collective-permute-start.8 = (f32[400,1024]{1,0:T(8,128)S(1)}, f32[400,1024]{1,0:T(8,128)S(1)}, u32[]{:S(2)}, u32[]{:S(2)}) collective-permute-start(f32[400,1024]{1,0:T(8,128)S(1)} %turn.6.one_ref), channel_id=1, source_target_pairs={{0,8},{8,0},{16,24},{24,16},{1,9},{9,1},{17,25},{25,17},{2,10},{10... | collective-permute-start | bytes 4915208 | tf_op jit(solution)/shard_map/ppermute | solution.py:21
  67.2 6.4 %collective-permute-start.7 = (f32[400,1024]{1,0:T(8,128)S(1)}, f32[400,1024]{1,0:T(8,128)S(1)}, u32[]{:S(2)}, u32[]{:S(2)}) collective-permute-start(f32[400,1024]{1,0:T(8,128)S(1)} %turn.5.one_ref), channel_id=1, source_target_pairs={{0,8},{8,0},{16,24},{24,16},{1,9},{9,1},{17,25},{25,17},{2,10},{10... | collective-permute-start | bytes 4915208 | tf_op jit(solution)/shard_map/ppermute | solution.py:21
  67.9 8.1 %collective-permute-start.6 = (f32[400,1024]{1,0:T(8,128)S(1)}, f32[400,1024]{1,0:T(8,128)S(1)}, u32[]{:S(2)}, u32[]{:S(2)}) collective-permute-start(f32[400,1024]{1,0:T(8,128)S(1)} %turn.4.one_ref), channel_id=1, source_target_pairs={{0,8},{8,0},{16,24},{24,16},{1,9},{9,1},{17,25},{25,17},{2,10},{10... | collective-permute-start | bytes 4915208 | tf_op jit(solution)/shard_map/ppermute | solution.py:21

commit v5 on v4

--- a/solution.py
+++ b/solution.py
@@ -22,8 +22,14 @@
 
 
 def gather_all(x, upper, lower):
-    for axis, bit in upper:
-        x = jnp.concatenate([x, swap(x, axis, bit)], axis=0)
+    while upper:
+        stage, upper = upper[:2], upper[2:]
+        others = [swap(x, *step) for step in stage]
+        if len(stage) == 2:
+            (axis, bit), (_, other) = stage
+            count = lax.axis_size(axis)
+            others.append(lax.ppermute(x, axis, [(i, i ^ (1 << bit) ^ (1 << other)) for i in range(count)]))
+        x = jnp.concatenate([x] + others, axis=0)
     halves = list(jnp.split(x, 2))
     for k in range(2):
         others = [swap(halves[0], *lower[k]), swap(halves[1], *lower[1 - k])]
@@ -103,7 +109,7 @@
         out_shape=jax.ShapeDtypeStruct((1, height, width), jnp.float32),
         compiler_params=pltpu.CompilerParams(vmem_limit_bytes=SMALL_BYTES),
         name="pack",
-    )(counts, *[in_hbm(x) for x in (entities, src, dst, rel, neg, weight)])
+    )(*[in_hbm(x) for x in (counts, entities, src, dst, rel, neg, weight)])
 
 
 def in_vmem(x):
@@ -168,22 +174,23 @@
 
 
 STAGES = 4
-SCRATCH = 16
+FIRST = 2
+SCRATCH = 19
 
 
 def in_turn(parts, *sides):
     for stage in range(STAGES):
         for part in parts:
             next(part, None)
-            for side, steps in sides:
-                for _ in range(-(-steps // (STAGES * len(parts)))):
+            for side, steps in sides if stage >= FIRST else []:
+                for _ in range(-(-steps // ((STAGES - FIRST) * len(parts)))):
                     next(side, None)
 
 
-def main_kernel(spec, live, where, relations, blocks_of, *refs):
+def main_kernel(spec, where, relations, blocks_of, *refs):
     accs, ent_ref, scratch = refs[:-SCRATCH][:-1], refs[:-SCRATCH][-1], refs[-SCRATCH:]
     (half, rows, shards, blocks, edges) = spec
-    (data_rows, columns_of, table, ent, stack, stack_t, times, info, ids_v, ids, factor, grads, flip, mine, seg, come) = scratch
+    (live_v, live, data_rows, columns_of, table, ent, stack, stack_t, times, info, ids_v, ids, factor, grads, flip, mine, seg, come, known) = scratch
     width = LANE_TILES // 2 * LANES
     part_rows = rows * shards
     group = shards * blocks
@@ -203,6 +210,18 @@
     mine[...] = jnp.zeros_like(mine)
     info[...] = jnp.zeros_like(info)
 
+    lane = lax.broadcasted_iota(jnp.int32, (count, width), 1)
+    for k in range(2 * shards):
+        raw = jnp.zeros((count, width), jnp.float32)
+        for piece in range(pieces):
+            square = blocks_of[k, piece * count : (piece + 1) * count, :]
+            square = pltpu.roll(square, (room * piece - half) % width, 1)
+            raw = jnp.where((lane >= room * piece) & (lane < room * (piece + 1)), square, raw)
+        data_rows[k, :count, :] = raw
+        live_v[k : k + 1, :] = raw[count - 1 :, :LANES].astype(jnp.int32)
+    tell = pltpu.make_async_copy(live_v, live, known)
+    tell.start()
+
     for x in range(2):
         for j in range(shards):
             k = block_index(j, x, bits)
@@ -211,19 +230,13 @@
             for part in range(2):
                 square = blocks_of[k, part * rows : (part + 1) * rows, :]
                 ent[at, part * width : (part + 1) * width] = jnp.where(lane < half, square, 0.0)
-            lane = lax.broadcasted_iota(jnp.int32, (count, width), 1)
-            raw = jnp.zeros((count, width), jnp.float32)
-            for piece in range(pieces):
-                square = pltpu.roll(
-                    blocks_of[k, piece * count : (piece + 1) * count, :], (room * piece - half) % width, 1
-                )
-                raw = jnp.where((lane >= room * piece) & (lane < room * (piece + 1)), square, raw)
-            data_rows[k, :count, :] = raw
         whole = ent[...]
         high, low = high_low(whole)
         stack[x] = jnp.concatenate([high, low, high], axis=0)
         high, low = high_low(whole.T)
         stack_t[x] = jnp.concatenate([high, low, high], axis=0)
+
+    tell.wait()
 
     for x in range(2):
         rows_of = []
@@ -237,7 +250,7 @@
 
         def lay(n, offset):
             k, slot = block_index((n // blocks) ^ me, x, bits), n % blocks
-            alive = live[k * blocks + slot]
+            alive = live[k, slot]
             tile = data_rows[k, : 4 * blocks, :]
 
             def chosen(k):
@@ -389,24 +402,27 @@
     ent_ref[:, half:] = mine[:, width : width + half]
 
 
-def gradients(spec, relations, live, where, blocks_of):
+def gradients(spec, relations, where, blocks_of):
     half, rows, shards, blocks, edges = spec
     dim, part_rows, width = 2 * half, rows * shards, LANE_TILES // 2 * LANES
     relation_count = relations.shape[0]
     group = shards * blocks
     total = group * edges // 2
-    totals = 2 if part_rows <= 256 else 1
+    small = part_rows <= 256
+    totals = 2 if small else 1
     smem = pl.BlockSpec(memory_space=pltpu.SMEM)
     vmem = pl.BlockSpec(memory_space=pltpu.VMEM)
     return pl.pallas_call(
         functools.partial(main_kernel, spec),
-        in_specs=[smem, smem, pl.BlockSpec(memory_space=pl.ANY), vmem],
+        in_specs=[smem, pl.BlockSpec(memory_space=pl.ANY), vmem],
         out_specs=(vmem,) * (totals + 1),
         out_shape=(
             *[pltpu.VMEM((relation_count, LANE_TILES, LANES), jnp.float32)] * totals,
             jax.ShapeDtypeStruct((rows, dim), jnp.float32),
         ),
         scratch_shapes=[
+            pltpu.VMEM((2 * shards, LANES), jnp.int32),
+            pltpu.SMEM((2 * shards, LANES), jnp.int32),
             pltpu.VMEM((2 * shards, -(-packing(half, rows, blocks, part_rows)[0] // 8) * 8, width), jnp.float32),
             pltpu.VMEM((dim, relation_count), jnp.float32),
             pltpu.VMEM((relation_count, LANE_TILES, LANES), jnp.float32),
@@ -423,10 +439,11 @@
             pltpu.VMEM((rows, 2 * width), jnp.float32),
             pltpu.SemaphoreType.DMA,
             pltpu.SemaphoreType.DMA((relation_count // STEP,)),
+            pltpu.SemaphoreType.DMA,
         ],
-        compiler_params=pltpu.CompilerParams(vmem_limit_bytes=(40 if part_rows <= 256 else 54) * 1024 * 1024),
+        compiler_params=pltpu.CompilerParams(vmem_limit_bytes=(40 if small else 54) * 1024 * 1024),
         name="gradients",
-    )(live, where, in_hbm(relations.T), blocks_of)
+    )(where, in_hbm(relations.T), in_vmem(blocks_of) if small else blocks_of)
 
 
 def body(entities, relations, src_index, dst_index, rel_index, neg_index, counts, edge_weight):
@@ -441,12 +458,10 @@
     block = packed(entities, counts, src_index, dst_index, rel_index, neg_index, edge_weight, part_rows)
     upper = [("block", bit) for bit in reversed(range(1, block_bits))]
     blocks_of = gather_all(block, upper, [("dom", partner_bit), ("block", 0)])
-    last = packing(dim // 2, rows, blocks, part_rows)[0] - 1
-    live = blocks_of[:, last, dim // 2 : dim // 2 + blocks].astype(jnp.int32).reshape(-1)
     where = jnp.stack([lax.axis_index("block"), (lax.axis_index("dom") >> partner_bit) & 1]).astype(jnp.int32)
 
     spec = (dim // 2, rows, shards, blocks, edges)
-    *accs, entity_grad = gradients(spec, relations, live, where, blocks_of)
+    *accs, entity_grad = gradients(spec, relations, where, blocks_of)
     return entity_grad, summed(accs, dim, other_bits).T
 
 

time: 78.2 us -> 73.5 us (0.940)
  local copies, waits for them, and re-layouts: 1.59 us -> 0.08 us
  Pallas kernels: 43 us -> 41.9 us
  waiting for transfers between devices: 18.7 us -> 17.6 us
    ppermute x10, starting transfers between devices: 12.5 us -> 7.2 us  [swap(): return lax.ppermute(x, axis, [(i, i ^ 1 << bit) for i in range(count)])]
    ppermute x0 -> x1, starting transfers between devices: none -> 5.11 us  [gather_all(): lax.ppermute(x, axis, [(i, i ^ 1 << bit ^ 1 << other) for i in range(coun...]
    pallas_call x1, Pallas kernels: 33.7 us -> 32.6 us  [gradients(): pl.pallas_call(functools.partial(main_kernel, spec), in_specs=[smem, pl.B...]
    ppermute x10, waiting for transfers between devices: 18.7 us -> 17.6 us  [swap(): return lax.ppermute(x, axis, [(i, i ^ 1 << bit) for i in range(count)])]
  transfers between devices with their start and end apart: 10 -> 11, of which waited for: 8 -> 9; matrix products, arithmetic and copies ran while one was open for 1% -> 1% of each run, Pallas kernels for 7% -> 8%
where the time goes in v5:
time: 73.5 us; the launch traced here: 73.3 us
  Pallas kernels  41.9 us (57%)
  waiting for transfers between devices  17.6 us (24%)
  starting transfers between devices  12.3 us (17%)
  between operations  0.75 us (1%)
    pallas_call x1, Pallas kernels, gradients(): pl.pallas_call(functools.partial(main_kernel, spec), in_specs=[smem, pl.B...  32.6 us
    ppermute x10, waiting for transfers between devices, swap(): return lax.ppermute(x, axis, [(i, i ^ 1 << bit) for i in range(count)])  17.6 us
    ppermute x10, starting transfers between devices, swap(): return lax.ppermute(x, axis, [(i, i ^ 1 << bit) for i in range(count)])  7.2 us
    pallas_call x4, Pallas kernels, summed(): pl.pallas_call(add_kernel, grid=(1,), in_specs=[block, block] + ([] if to...  5.32 us
    ppermute x1, starting transfers between devices, gather_all(): lax.ppermute(x, axis, [(i, i ^ 1 << bit ^ 1 << other) for i in range(coun...  5.11 us
    pallas_call x4, Pallas kernels, summed(): pl.pallas_call(functools.partial(finish_kernel, dim // 2, k * size), in_s...  2.38 us
    pallas_call x1, Pallas kernels, packed(): pl.pallas_call(functools.partial(pack_kernel, dim // 2, part_rows), in_sp...  1.64 us
  transfers between devices with their start and end apart: 11, of which 9 were waited for; matrix products, arithmetic and copies ran while one was open for 1% of the time, Pallas kernels for 8%

profile of v5, /device:TPU:0, one launch (start us, length us, event | category | flops | bytes accessed | tf_op | source)
XLA Modules:
  0.0 73.3 jit_solution(7902280696220636853)
XLA Ops:
  0.6 1.6 %pack.1 = f32[1,64,256]{2,1,0:T(8,128)S(1)} custom-call(s32[1,2]{1,0:T(1,128)} %counts.1, f32[32,400]{1,0:T(8,128)} %entities.1, s32[1,2,256]{2,1,0:T(2,128)} %src.1, s32[1,2,256]{2,1,0:T(2,128)} %dst.1, s32[1,2,256]{2,1,0:T(2,128)} %rel.1, s32[1,2,1024]{2,1,0:T(2,128)} %neg.1, f32[1,2,256]{2,1,0:T(2,128)} %weight.1), custom_call_target="tpu_custom_call" | custom-call | tf_op jit(solution)/shard_map/pack/pallas_call | solution.py:105
  2.3 5.1 %collective-permute-start.4 = (f32[1,64,256]{2,1,0:T(8,128)S(1)}, f32[1,64,256]{2,1,0:T(8,128)S(1)}, u32[]{:S(2)}, u32[]{:S(2)}) collective-permute-start(f32[1,64,256]{2,1,0:T(8,128)S(1)} %pack.1), channel_id=1, source_target_pairs={{0,6},{1,7},{2,4},{3,5},{4,2},{5,3},{6,0},{7,1},{8,14},{9,15},{10,... | collective-permute-start | bytes 196616 | tf_op jit(solution)/shard_map/ppermute | solution.py:31
  7.4 0.0 collective-permute-start.3
  7.4 0.6 collective-permute-start
  8.0 5.0 %collective-permute-done = f32[1,64,256]{2,1,0:T(8,128)S(1)} collective-permute-done((f32[1,64,256]{2,1,0:T(8,128)S(1)}, f32[1,64,256]{2,1,0:T(8,128)S(1)}, u32[]{:S(2)}, u32[]{:S(2)}) %collective-permute-start) | collective-permute-done | bytes 65568 | tf_op jit(solution)/shard_map/ppermute | solution.py:21
  13.0 1.6 %collective-permute-start.1 = (f32[2,64,256]{2,1,0:T(8,128)S(1)}, f32[2,64,256]{2,1,0:T(8,128)S(1)}, u32[]{:S(2)}, u32[]{:S(2)}) collective-permute-start(f32[2,64,256]{2,1,0:T(8,128)S(1)} %pad_maximum_fusion.2), channel_id=1, source_target_pairs={{0,16},{8,24},{16,0},{24,8},{1,17},{9,25},{17,1},{25,9},{2,18},{10... | collective-permute-start | bytes 393224 | tf_op jit(solution)/shard_map/ppermute | solution.py:21
  14.6 0.6 pad_add_fusion.where
  15.2 0.0 collective-permute-done.4
  15.2 0.0 collective-permute-done.3
  15.3 1.6 %collective-permute-start.5 = (f32[2,64,256]{2,1,0:T(8,128)S(1)}, f32[2,64,256]{2,1,0:T(8,128)S(1)}, u32[]{:S(2)}, u32[]{:S(2)}) collective-permute-start(f32[2,64,256]{2,1,0:T(8,128)S(1)} %pad_maximum_fusion.3), channel_id=1, source_target_pairs={{0,1},{1,0},{2,3},{3,2},{4,5},{5,4},{6,7},{7,6},{8,9},{9,8},{10,11... | collective-permute-start | bytes 393224 | tf_op jit(solution)/shard_map/ppermute | solution.py:21
  16.8 1.2 %collective-permute-done.1 = f32[2,64,256]{2,1,0:T(8,128)S(1)} collective-permute-done((f32[2,64,256]{2,1,0:T(8,128)S(1)}, f32[2,64,256]{2,1,0:T(8,128)S(1)}, u32[]{:S(2)}, u32[]{:S(2)}) %collective-permute-start.1) | collective-permute-done | bytes 131104 | tf_op jit(solution)/shard_map/ppermute | solution.py:21
  18.1 1.6 %collective-permute-start.2 = (f32[4,64,256]{2,1,0:T(8,128)S(1)}, f32[4,64,256]{2,1,0:T(8,128)S(1)}, u32[]{:S(2)}, u32[]{:S(2)}) collective-permute-start(f32[4,64,256]{2,1,0:T(8,128)S(1)} %pad_maximum_fusion), channel_id=1, source_target_pairs={{0,1},{1,0},{2,3},{3,2},{4,5},{5,4},{6,7},{7,6},{8,9},{9,8},{10,11... | collective-permute-start | bytes 786440 | tf_op jit(solution)/shard_map/ppermute | solution.py:21
  19.7 2.1 %collective-permute-done.5 = f32[2,64,256]{2,1,0:T(8,128)S(1)} collective-permute-done((f32[2,64,256]{2,1,0:T(8,128)S(1)}, f32[2,64,256]{2,1,0:T(8,128)S(1)}, u32[]{:S(2)}, u32[]{:S(2)}) %collective-permute-start.5) | collective-permute-done | bytes 131104 | tf_op jit(solution)/shard_map/ppermute | solution.py:21
  21.8 0.6 collective-permute-start.6
  22.3 2.3 %collective-permute-done.2 = f32[4,64,256]{2,1,0:T(8,128)S(1)} collective-permute-done((f32[4,64,256]{2,1,0:T(8,128)S(1)}, f32[4,64,256]{2,1,0:T(8,128)S(1)}, u32[]{:S(2)}, u32[]{:S(2)}) %collective-permute-start.2) | collective-permute-done | bytes 262176 | tf_op jit(solution)/shard_map/ppermute | solution.py:21
  24.7 3.5 %collective-permute-done.6 = f32[4,64,256]{2,1,0:T(8,128)S(1)} collective-permute-done((f32[4,64,256]{2,1,0:T(8,128)S(1)}, f32[4,64,256]{2,1,0:T(8,128)S(1)}, u32[]{:S(2)}, u32[]{:S(2)}) %collective-permute-start.6) | collective-permute-done | bytes 262176 | tf_op jit(solution)/shard_map/ppermute | solution.py:21
  28.2 32.6 %gradients.1 = (f32[4096,4,128]{2,1,0:T(4,128)S(1)}, f32[4096,4,128]{2,1,0:T(4,128)S(1)}, f32[32,400]{1,0:T(8,128)}) custom-call(s32[2]{0:T(128)} %pad_add_fusion.where, f32[400,4096]{1,0:T(8,128)} %bitcast.5, f32[16,64,256]{2,1,0:T(8,128)S(1)} %constant_dynamic-update-slice_fusion.blocks_of), custom_call_target="tpu_custom_call" | custom-call | tf_op jit(solution)/shard_map/gradients/pallas_call | solution.py:415
  60.8 0.6 turn.7.one_ref
  61.4 0.1 collective-permute-start.10
  61.5 0.6 turn.6.one_ref
  62.1 0.6 collective-permute-start.9
  62.7 0.6 turn.5.one_ref
  63.3 0.1 collective-permute-start.8
  63.3 0.6 turn.4.one_ref
  63.9 0.6 collective-permute-start.7
  64.5 0.5 collective-permute-done.10.other_ref
  65.0 1.3 %add_part.4.refs_0_ = f32[400,4096]{1,0:T(8,128)} custom-call(f32[400,1024]{1,0:T(8,128)S(1)} %turn.7.one_ref, f32[400,1024]{1,0:T(8,128)S(1)} %collective-permute-done.10.other_ref), custom_call_target="tpu_custom_call" | custom-call | flops 409600 | bytes 4915200 | tf_op jit(solution)/shard_map/add_part/pallas_call | solution.py:157
  66.3 1.0 %collective-permute-done.9.other_ref = f32[400,1024]{1,0:T(8,128)S(1)} collective-permute-done((f32[400,1024]{1,0:T(8,128)S(1)}, f32[400,1024]{1,0:T(8,128)S(1)}, u32[]{:S(2)}, u32[]{:S(2)}) %collective-permute-start.9) | collective-permute-done | bytes 1638432 | tf_op jit(solution)/shard_map/ppermute | solution.py:21
  67.3 1.3 %add_part.5.refs_0_ = f32[400,4096]{1,0:T(8,128)} custom-call(f32[400,1024]{1,0:T(8,128)S(1)} %turn.6.one_ref, f32[400,1024]{1,0:T(8,128)S(1)} %collective-permute-done.9.other_ref, f32[400,4096]{1,0:T(8,128)} %add_part.4.refs_0_), custom_call_target="tpu_custom_call", output_to_operand_aliasing={{}: (2, {})} | custom-call | flops 409600 | bytes 4915200 | tf_op jit(solution)/shard_map/add_part/pallas_call | solution.py:157
  68.7 1.0 %collective-permute-done.8.other_ref = f32[400,1024]{1,0:T(8,128)S(1)} collective-permute-done((f32[400,1024]{1,0:T(8,128)S(1)}, f32[400,1024]{1,0:T(8,128)S(1)}, u32[]{:S(2)}, u32[]{:S(2)}) %collective-permute-start.8) | collective-permute-done | bytes 1638432 | tf_op jit(solution)/shard_map/ppermute | solution.py:21
  69.7 1.3 %add_part.6.refs_0_ = f32[400,4096]{1,0:T(8,128)} custom-call(f32[400,1024]{1,0:T(8,128)S(1)} %turn.5.one_ref, f32[400,1024]{1,0:T(8,128)S(1)} %collective-permute-done.8.other_ref, f32[400,4096]{1,0:T(8,128)} %add_part.5.refs_0_), custom_call_target="tpu_custom_call", output_to_operand_aliasing={{}: (2, {})} | custom-call | flops 409600 | bytes 4915200 | tf_op jit(solution)/shard_map/add_part/pallas_call | solution.py:157
  71.0 1.0 %collective-permute-done.7.other_ref = f32[400,1024]{1,0:T(8,128)S(1)} collective-permute-done((f32[400,1024]{1,0:T(8,128)S(1)}, f32[400,1024]{1,0:T(8,128)S(1)}, u32[]{:S(2)}, u32[]{:S(2)}) %collective-permute-start.7) | collective-permute-done | bytes 1638432 | tf_op jit(solution)/shard_map/ppermute | solution.py:21
  72.0 1.3 %add_part.7 = f32[400,4096]{1,0:T(8,128)} custom-call(f32[400,1024]{1,0:T(8,128)S(1)} %turn.4.one_ref, f32[400,1024]{1,0:T(8,128)S(1)} %collective-permute-done.7.other_ref, f32[400,4096]{1,0:T(8,128)} %add_part.6.refs_0_), custom_call_target="tpu_custom_call", output_to_operand_aliasing={{}: (2, {})} | custom-call | flops 409600 | bytes 4915200 | tf_op jit(solution)/shard_map/add_part/pallas_call | solution.py:157
  (12 shorter events, 0.1 us)
Async XLA Ops:
  2.3 13.0 %collective-permute-start.4 = (f32[1,64,256]{2,1,0:T(8,128)S(1)}, f32[1,64,256]{2,1,0:T(8,128)S(1)}, u32[]{:S(2)}, u32[]{:S(2)}) collective-permute-start(f32[1,64,256]{2,1,0:T(8,128)S(1)} %pack.1), channel_id=1, source_target_pairs={{0,6},{1,7},{2,4},{3,5},{4,2},{5,3},{6,0},{7,1},{8,14},{9,15},{10,... | collective-permute-start | bytes 196616 | tf_op jit(solution)/shard_map/ppermute | solution.py:31
  7.4 7.9 %collective-permute-start.3 = (f32[1,64,256]{2,1,0:T(8,128)S(1)}, f32[1,64,256]{2,1,0:T(8,128)S(1)}, u32[]{:S(2)}, u32[]{:S(2)}) collective-permute-start(f32[1,64,256]{2,1,0:T(8,128)S(1)} %pack.1), channel_id=1, source_target_pairs={{0,2},{1,3},{2,0},{3,1},{4,6},{5,7},{6,4},{7,5},{8,10},{9,11},{10,... | collective-permute-start | bytes 196616 | tf_op jit(solution)/shard_map/ppermute | solution.py:21
  7.4 5.6 %collective-permute-start = (f32[1,64,256]{2,1,0:T(8,128)S(1)}, f32[1,64,256]{2,1,0:T(8,128)S(1)}, u32[]{:S(2)}, u32[]{:S(2)}) collective-permute-start(f32[1,64,256]{2,1,0:T(8,128)S(1)} %pack.1), channel_id=1, source_target_pairs={{0,4},{1,5},{2,6},{3,7},{4,0},{5,1},{6,2},{7,3},{8,12},{9,13},{10,... | collective-permute-start | bytes 196616 | tf_op jit(solution)/shard_map/ppermute | solution.py:21
  13.0 5.0 %collective-permute-start.1 = (f32[2,64,256]{2,1,0:T(8,128)S(1)}, f32[2,64,256]{2,1,0:T(8,128)S(1)}, u32[]{:S(2)}, u32[]{:S(2)}) collective-permute-start(f32[2,64,256]{2,1,0:T(8,128)S(1)} %pad_maximum_fusion.2), channel_id=1, source_target_pairs={{0,16},{8,24},{16,0},{24,8},{1,17},{9,25},{17,1},{25,9},{2,18},{10... | collective-permute-start | bytes 393224 | tf_op jit(solution)/shard_map/ppermute | solution.py:21
  15.3 6.5 %collective-permute-start.5 = (f32[2,64,256]{2,1,0:T(8,128)S(1)}, f32[2,64,256]{2,1,0:T(8,128)S(1)}, u32[]{:S(2)}, u32[]{:S(2)}) collective-permute-start(f32[2,64,256]{2,1,0:T(8,128)S(1)} %pad_maximum_fusion.3), channel_id=1, source_target_pairs={{0,1},{1,0},{2,3},{3,2},{4,5},{5,4},{6,7},{7,6},{8,9},{9,8},{10,11... | collective-permute-start | bytes 393224 | tf_op jit(solution)/shard_map/ppermute | solution.py:21
  18.1 6.5 %collective-permute-start.2 = (f32[4,64,256]{2,1,0:T(8,128)S(1)}, f32[4,64,256]{2,1,0:T(8,128)S(1)}, u32[]{:S(2)}, u32[]{:S(2)}) collective-permute-start(f32[4,64,256]{2,1,0:T(8,128)S(1)} %pad_maximum_fusion), channel_id=1, source_target_pairs={{0,1},{1,0},{2,3},{3,2},{4,5},{5,4},{6,7},{7,6},{8,9},{9,8},{10,11... | collective-permute-start | bytes 786440 | tf_op jit(solution)/shard_map/ppermute | solution.py:21
  21.8 6.4 %collective-permute-start.6 = (f32[4,64,256]{2,1,0:T(8,128)S(1)}, f32[4,64,256]{2,1,0:T(8,128)S(1)}, u32[]{:S(2)}, u32[]{:S(2)}) collective-permute-start(f32[4,64,256]{2,1,0:T(8,128)S(1)} %pad_maximum_fusion.1), channel_id=1, source_target_pairs={{0,16},{8,24},{16,0},{24,8},{1,17},{9,25},{17,1},{25,9},{2,18},{10... | collective-permute-start | bytes 786440 | tf_op jit(solution)/shard_map/ppermute | solution.py:21
  61.4 3.6 %collective-permute-start.10 = (f32[400,1024]{1,0:T(8,128)S(1)}, f32[400,1024]{1,0:T(8,128)S(1)}, u32[]{:S(2)}, u32[]{:S(2)}) collective-permute-start(f32[400,1024]{1,0:T(8,128)S(1)} %turn.7.one_ref), channel_id=1, source_target_pairs={{0,8},{8,0},{16,24},{24,16},{1,9},{9,1},{17,25},{25,17},{2,10},{10... | collective-permute-start | bytes 4915208 | tf_op jit(solution)/shard_map/ppermute | solution.py:21
  62.1 5.2 %collective-permute-start.9 = (f32[400,1024]{1,0:T(8,128)S(1)}, f32[400,1024]{1,0:T(8,128)S(1)}, u32[]{:S(2)}, u32[]{:S(2)}) collective-permute-start(f32[400,1024]{1,0:T(8,128)S(1)} %turn.6.one_ref), channel_id=1, source_target_pairs={{0,8},{8,0},{16,24},{24,16},{1,9},{9,1},{17,25},{25,17},{2,10},{10... | collective-permute-start | bytes 4915208 | tf_op jit(solution)/shard_map/ppermute | solution.py:21
  63.3 6.4 %collective-permute-start.8 = (f32[400,1024]{1,0:T(8,128)S(1)}, f32[400,1024]{1,0:T(8,128)S(1)}, u32[]{:S(2)}, u32[]{:S(2)}) collective-permute-start(f32[400,1024]{1,0:T(8,128)S(1)} %turn.5.one_ref), channel_id=1, source_target_pairs={{0,8},{8,0},{16,24},{24,16},{1,9},{9,1},{17,25},{25,17},{2,10},{10... | collective-permute-start | bytes 4915208 | tf_op jit(solution)/shard_map/ppermute | solution.py:21
  63.9 8.1 %collective-permute-start.7 = (f32[400,1024]{1,0:T(8,128)S(1)}, f32[400,1024]{1,0:T(8,128)S(1)}, u32[]{:S(2)}, u32[]{:S(2)}) collective-permute-start(f32[400,1024]{1,0:T(8,128)S(1)} %turn.4.one_ref), channel_id=1, source_target_pairs={{0,8},{8,0},{16,24},{24,16},{1,9},{9,1},{17,25},{25,17},{2,10},{10... | collective-permute-start | bytes 4915208 | tf_op jit(solution)/shard_map/ppermute | solution.py:21

commit v6 on v5

--- a/solution.py
+++ b/solution.py
@@ -187,9 +187,9 @@
                     next(side, None)
 
 
-def main_kernel(spec, where, relations, blocks_of, *refs):
+def main_kernel(spec, relations, blocks_of, *refs):
     accs, ent_ref, scratch = refs[:-SCRATCH][:-1], refs[:-SCRATCH][-1], refs[-SCRATCH:]
-    (half, rows, shards, blocks, edges) = spec
+    half, rows, shards, blocks, edges, partner_bit = spec
     (live_v, live, data_rows, columns_of, table, ent, stack, stack_t, times, info, ids_v, ids, factor, grads, flip, mine, seg, come, known) = scratch
     width = LANE_TILES // 2 * LANES
     part_rows = rows * shards
@@ -197,7 +197,7 @@
     total = group * edges // 2
     bits = shards.bit_length() - 1
     count, room, pieces, _ = packing(half, rows, blocks, part_rows)
-    me, side = where[0], where[1]
+    me, side = lax.axis_index("block"), (lax.axis_index("dom") >> partner_bit) & 1
     own = me * rows
 
     steps = accs[0].shape[0] // STEP
@@ -402,19 +402,18 @@
     ent_ref[:, half:] = mine[:, width : width + half]
 
 
-def gradients(spec, relations, where, blocks_of):
-    half, rows, shards, blocks, edges = spec
+def gradients(spec, relations, blocks_of):
+    half, rows, shards, blocks, edges = spec[:5]
     dim, part_rows, width = 2 * half, rows * shards, LANE_TILES // 2 * LANES
     relation_count = relations.shape[0]
     group = shards * blocks
     total = group * edges // 2
     small = part_rows <= 256
     totals = 2 if small else 1
-    smem = pl.BlockSpec(memory_space=pltpu.SMEM)
     vmem = pl.BlockSpec(memory_space=pltpu.VMEM)
     return pl.pallas_call(
         functools.partial(main_kernel, spec),
-        in_specs=[smem, pl.BlockSpec(memory_space=pl.ANY), vmem],
+        in_specs=[pl.BlockSpec(memory_space=pl.ANY), vmem],
         out_specs=(vmem,) * (totals + 1),
         out_shape=(
             *[pltpu.VMEM((relation_count, LANE_TILES, LANES), jnp.float32)] * totals,
@@ -443,7 +442,7 @@
         ],
         compiler_params=pltpu.CompilerParams(vmem_limit_bytes=(40 if small else 54) * 1024 * 1024),
         name="gradients",
-    )(where, in_hbm(relations.T), in_vmem(blocks_of) if small else blocks_of)
+    )(in_hbm(relations.T), in_vmem(blocks_of) if small else blocks_of)
 
 
 def body(entities, relations, src_index, dst_index, rel_index, neg_index, counts, edge_weight):
@@ -458,10 +457,9 @@
     block = packed(entities, counts, src_index, dst_index, rel_index, neg_index, edge_weight, part_rows)
     upper = [("block", bit) for bit in reversed(range(1, block_bits))]
     blocks_of = gather_all(block, upper, [("dom", partner_bit), ("block", 0)])
-    where = jnp.stack([lax.axis_index("block"), (lax.axis_index("dom") >> partner_bit) & 1]).astype(jnp.int32)
-
-    spec = (dim // 2, rows, shards, blocks, edges)
-    *accs, entity_grad = gradients(spec, relations, where, blocks_of)
+
+    spec = (dim // 2, rows, shards, blocks, edges, partner_bit)
+    *accs, entity_grad = gradients(spec, relations, blocks_of)
     return entity_grad, summed(accs, dim, other_bits).T
 
 

time: 73.5 us -> 70.5 us (0.959)
  waiting for transfers between devices: 17.6 us -> 13.2 us
  starting transfers between devices: 12.3 us -> 14.8 us
    ppermute x10, starting transfers between devices: 7.2 us -> 13.4 us  [swap(): return lax.ppermute(x, axis, [(i, i ^ 1 << bit) for i in range(count)])]
    ppermute x10, waiting for transfers between devices: 17.6 us -> 13.2 us  [swap(): return lax.ppermute(x, axis, [(i, i ^ 1 << bit) for i in range(count)])]
    ppermute x1, starting transfers between devices: 5.11 us -> 1.35 us  [gather_all(): lax.ppermute(x, axis, [(i, i ^ 1 << bit ^ 1 << other) for i in range(coun...]
  transfers between devices with their start and end apart: 11 -> 11, of which waited for: 9 -> 9; matrix products, arithmetic and copies ran while one was open for 1% -> 0% of each run, Pallas kernels for 8% -> 8%
where the time goes in v6:
time: 70.5 us; the launch traced here: 70.3 us
  Pallas kernels  41.4 us (59%)
  starting transfers between devices  14.8 us (21%)
  waiting for transfers between devices  13.2 us (19%)
  between operations  0.76 us (1%)
    pallas_call x1, Pallas kernels, gradients(): pl.pallas_call(functools.partial(main_kernel, spec), in_specs=[pl.BlockSp...  32.1 us
    ppermute x10, starting transfers between devices, swap(): return lax.ppermute(x, axis, [(i, i ^ 1 << bit) for i in range(count)])  13.4 us
    ppermute x10, waiting for transfers between devices, swap(): return lax.ppermute(x, axis, [(i, i ^ 1 << bit) for i in range(count)])  13.2 us
    pallas_call x4, Pallas kernels, summed(): pl.pallas_call(add_kernel, grid=(1,), in_specs=[block, block] + ([] if to...  5.32 us
    pallas_call x4, Pallas kernels, summed(): pl.pallas_call(functools.partial(finish_kernel, dim // 2, k * size), in_s...  2.38 us
    pallas_call x1, Pallas kernels, packed(): pl.pallas_call(functools.partial(pack_kernel, dim // 2, part_rows), in_sp...  1.64 us
  transfers between devices with their start and end apart: 11, of which 9 were waited for; matrix products, arithmetic and copies ran while one was open for 0% of the time, Pallas kernels for 8%

profile of v6, /device:TPU:0, one launch (start us, length us, event | category | flops | bytes accessed | tf_op | source)
XLA Modules:
  0.0 70.3 jit_solution(3823121085603372349)
XLA Ops:
  0.6 1.6 %pack.1 = f32[1,64,256]{2,1,0:T(8,128)S(1)} custom-call(s32[1,2]{1,0:T(1,128)} %counts.1, f32[32,400]{1,0:T(8,128)} %entities.1, s32[1,2,256]{2,1,0:T(2,128)} %src.1, s32[1,2,256]{2,1,0:T(2,128)} %dst.1, s32[1,2,256]{2,1,0:T(2,128)} %rel.1, s32[1,2,1024]{2,1,0:T(2,128)} %neg.1, f32[1,2,256]{2,1,0:T(2,128)} %weight.1), custom_call_target="tpu_custom_call" | custom-call | tf_op jit(solution)/shard_map/pack/pallas_call | solution.py:105
  2.3 4.1 %collective-permute-start = (f32[1,64,256]{2,1,0:T(8,128)S(1)}, f32[1,64,256]{2,1,0:T(8,128)S(1)}, u32[]{:S(2)}, u32[]{:S(2)}) collective-permute-start(f32[1,64,256]{2,1,0:T(8,128)S(1)} %pack.1), channel_id=1, source_target_pairs={{0,4},{1,5},{2,6},{3,7},{4,0},{5,1},{6,2},{7,3},{8,12},{9,13},{10,... | collective-permute-start | bytes 196616 | tf_op jit(solution)/shard_map/ppermute | solution.py:21
  6.4 1.3 %collective-permute-start.4 = (f32[1,64,256]{2,1,0:T(8,128)S(1)}, f32[1,64,256]{2,1,0:T(8,128)S(1)}, u32[]{:S(2)}, u32[]{:S(2)}) collective-permute-start(f32[1,64,256]{2,1,0:T(8,128)S(1)} %pack.1), channel_id=1, source_target_pairs={{0,6},{1,7},{2,4},{3,5},{4,2},{5,3},{6,0},{7,1},{8,14},{9,15},{10,... | collective-permute-start | bytes 196616 | tf_op jit(solution)/shard_map/ppermute | solution.py:31
  7.7 0.2 collective-permute-start.3
  8.0 2.2 %collective-permute-done = f32[1,64,256]{2,1,0:T(8,128)S(1)} collective-permute-done((f32[1,64,256]{2,1,0:T(8,128)S(1)}, f32[1,64,256]{2,1,0:T(8,128)S(1)}, u32[]{:S(2)}, u32[]{:S(2)}) %collective-permute-start) | collective-permute-done | bytes 65568 | tf_op jit(solution)/shard_map/ppermute | solution.py:21
  10.1 2.6 %collective-permute-start.1 = (f32[2,64,256]{2,1,0:T(8,128)S(1)}, f32[2,64,256]{2,1,0:T(8,128)S(1)}, u32[]{:S(2)}, u32[]{:S(2)}) collective-permute-start(f32[2,64,256]{2,1,0:T(8,128)S(1)} %pad_maximum_fusion.2), channel_id=1, source_target_pairs={{0,16},{8,24},{16,0},{24,8},{1,17},{9,25},{17,1},{25,9},{2,18},{10... | collective-permute-start | bytes 393224 | tf_op jit(solution)/shard_map/ppermute | solution.py:21
  12.7 0.0 collective-permute-done.4
  12.8 0.0 collective-permute-done.3
  12.8 1.6 %collective-permute-start.5 = (f32[2,64,256]{2,1,0:T(8,128)S(1)}, f32[2,64,256]{2,1,0:T(8,128)S(1)}, u32[]{:S(2)}, u32[]{:S(2)}) collective-permute-start(f32[2,64,256]{2,1,0:T(8,128)S(1)} %pad_maximum_fusion.3), channel_id=1, source_target_pairs={{0,1},{1,0},{2,3},{3,2},{4,5},{5,4},{6,7},{7,6},{8,9},{9,8},{10,11... | collective-permute-start | bytes 393224 | tf_op jit(solution)/shard_map/ppermute | solution.py:21
  14.4 1.3 %collective-permute-done.1 = f32[2,64,256]{2,1,0:T(8,128)S(1)} collective-permute-done((f32[2,64,256]{2,1,0:T(8,128)S(1)}, f32[2,64,256]{2,1,0:T(8,128)S(1)}, u32[]{:S(2)}, u32[]{:S(2)}) %collective-permute-start.1) | collective-permute-done | bytes 131104 | tf_op jit(solution)/shard_map/ppermute | solution.py:21
  15.7 2.1 %collective-permute-start.2 = (f32[4,64,256]{2,1,0:T(8,128)S(1)}, f32[4,64,256]{2,1,0:T(8,128)S(1)}, u32[]{:S(2)}, u32[]{:S(2)}) collective-permute-start(f32[4,64,256]{2,1,0:T(8,128)S(1)} %pad_maximum_fusion), channel_id=1, source_target_pairs={{0,1},{1,0},{2,3},{3,2},{4,5},{5,4},{6,7},{7,6},{8,9},{9,8},{10,11... | collective-permute-start | bytes 786440 | tf_op jit(solution)/shard_map/ppermute | solution.py:21
  17.8 1.4 %collective-permute-done.5 = f32[2,64,256]{2,1,0:T(8,128)S(1)} collective-permute-done((f32[2,64,256]{2,1,0:T(8,128)S(1)}, f32[2,64,256]{2,1,0:T(8,128)S(1)}, u32[]{:S(2)}, u32[]{:S(2)}) %collective-permute-start.5) | collective-permute-done | bytes 131104 | tf_op jit(solution)/shard_map/ppermute | solution.py:21
  19.3 1.5 %collective-permute-start.6 = (f32[4,64,256]{2,1,0:T(8,128)S(1)}, f32[4,64,256]{2,1,0:T(8,128)S(1)}, u32[]{:S(2)}, u32[]{:S(2)}) collective-permute-start(f32[4,64,256]{2,1,0:T(8,128)S(1)} %pad_maximum_fusion.1), channel_id=1, source_target_pairs={{0,16},{8,24},{16,0},{24,8},{1,17},{9,25},{17,1},{25,9},{2,18},{10... | collective-permute-start | bytes 786440 | tf_op jit(solution)/shard_map/ppermute | solution.py:21
  20.8 1.5 %collective-permute-done.2 = f32[4,64,256]{2,1,0:T(8,128)S(1)} collective-permute-done((f32[4,64,256]{2,1,0:T(8,128)S(1)}, f32[4,64,256]{2,1,0:T(8,128)S(1)}, u32[]{:S(2)}, u32[]{:S(2)}) %collective-permute-start.2) | collective-permute-done | bytes 262176 | tf_op jit(solution)/shard_map/ppermute | solution.py:21
  22.4 3.3 %collective-permute-done.6 = f32[4,64,256]{2,1,0:T(8,128)S(1)} collective-permute-done((f32[4,64,256]{2,1,0:T(8,128)S(1)}, f32[4,64,256]{2,1,0:T(8,128)S(1)}, u32[]{:S(2)}, u32[]{:S(2)}) %collective-permute-start.6) | collective-permute-done | bytes 262176 | tf_op jit(solution)/shard_map/ppermute | solution.py:21
  25.7 32.1 %gradients.1 = (f32[4096,4,128]{2,1,0:T(4,128)S(1)}, f32[4096,4,128]{2,1,0:T(4,128)S(1)}, f32[32,400]{1,0:T(8,128)}) custom-call(f32[400,4096]{1,0:T(8,128)} %bitcast.3, f32[16,64,256]{2,1,0:T(8,128)S(1)} %constant_dynamic-update-slice_fusion.blocks_of), custom_call_target="tpu_custom_call" | custom-call | tf_op jit(solution)/shard_map/gradients/pallas_call | solution.py:414
  57.8 0.6 turn.7.one_ref
  58.4 0.1 collective-permute-start.10
  58.5 0.6 turn.6.one_ref
  59.1 0.6 collective-permute-start.9
  59.7 0.6 turn.5.one_ref
  60.3 0.1 collective-permute-start.8
  60.3 0.6 turn.4.one_ref
  60.9 0.6 collective-permute-start.7
  61.5 0.5 collective-permute-done.10.other_ref
  62.0 1.3 %add_part.4.refs_0_ = f32[400,4096]{1,0:T(8,128)} custom-call(f32[400,1024]{1,0:T(8,128)S(1)} %turn.7.one_ref, f32[400,1024]{1,0:T(8,128)S(1)} %collective-permute-done.10.other_ref), custom_call_target="tpu_custom_call" | custom-call | flops 409600 | bytes 4915200 | tf_op jit(solution)/shard_map/add_part/pallas_call | solution.py:157
  63.3 1.0 %collective-permute-done.9.other_ref = f32[400,1024]{1,0:T(8,128)S(1)} collective-permute-done((f32[400,1024]{1,0:T(8,128)S(1)}, f32[400,1024]{1,0:T(8,128)S(1)}, u32[]{:S(2)}, u32[]{:S(2)}) %collective-permute-start.9) | collective-permute-done | bytes 1638432 | tf_op jit(solution)/shard_map/ppermute | solution.py:21
  64.3 1.3 %add_part.5.refs_0_ = f32[400,4096]{1,0:T(8,128)} custom-call(f32[400,1024]{1,0:T(8,128)S(1)} %turn.6.one_ref, f32[400,1024]{1,0:T(8,128)S(1)} %collective-permute-done.9.other_ref, f32[400,4096]{1,0:T(8,128)} %add_part.4.refs_0_), custom_call_target="tpu_custom_call", output_to_operand_aliasing={{}: (2, {})} | custom-call | flops 409600 | bytes 4915200 | tf_op jit(solution)/shard_map/add_part/pallas_call | solution.py:157
  65.7 1.0 %collective-permute-done.8.other_ref = f32[400,1024]{1,0:T(8,128)S(1)} collective-permute-done((f32[400,1024]{1,0:T(8,128)S(1)}, f32[400,1024]{1,0:T(8,128)S(1)}, u32[]{:S(2)}, u32[]{:S(2)}) %collective-permute-start.8) | collective-permute-done | bytes 1638432 | tf_op jit(solution)/shard_map/ppermute | solution.py:21
  66.7 1.3 %add_part.6.refs_0_ = f32[400,4096]{1,0:T(8,128)} custom-call(f32[400,1024]{1,0:T(8,128)S(1)} %turn.5.one_ref, f32[400,1024]{1,0:T(8,128)S(1)} %collective-permute-done.8.other_ref, f32[400,4096]{1,0:T(8,128)} %add_part.5.refs_0_), custom_call_target="tpu_custom_call", output_to_operand_aliasing={{}: (2, {})} | custom-call | flops 409600 | bytes 4915200 | tf_op jit(solution)/shard_map/add_part/pallas_call | solution.py:157
  68.0 1.0 %collective-permute-done.7.other_ref = f32[400,1024]{1,0:T(8,128)S(1)} collective-permute-done((f32[400,1024]{1,0:T(8,128)S(1)}, f32[400,1024]{1,0:T(8,128)S(1)}, u32[]{:S(2)}, u32[]{:S(2)}) %collective-permute-start.7) | collective-permute-done | bytes 1638432 | tf_op jit(solution)/shard_map/ppermute | solution.py:21
  69.0 1.3 %add_part.7 = f32[400,4096]{1,0:T(8,128)} custom-call(f32[400,1024]{1,0:T(8,128)S(1)} %turn.4.one_ref, f32[400,1024]{1,0:T(8,128)S(1)} %collective-permute-done.7.other_ref, f32[400,4096]{1,0:T(8,128)} %add_part.6.refs_0_), custom_call_target="tpu_custom_call", output_to_operand_aliasing={{}: (2, {})} | custom-call | flops 409600 | bytes 4915200 | tf_op jit(solution)/shard_map/add_part/pallas_call | solution.py:157
  (12 shorter events, 0.1 us)
Async XLA Ops:
  2.3 7.9 %collective-permute-start = (f32[1,64,256]{2,1,0:T(8,128)S(1)}, f32[1,64,256]{2,1,0:T(8,128)S(1)}, u32[]{:S(2)}, u32[]{:S(2)}) collective-permute-start(f32[1,64,256]{2,1,0:T(8,128)S(1)} %pack.1), channel_id=1, source_target_pairs={{0,4},{1,5},{2,6},{3,7},{4,0},{5,1},{6,2},{7,3},{8,12},{9,13},{10,... | collective-permute-start | bytes 196616 | tf_op jit(solution)/shard_map/ppermute | solution.py:21
  6.4 6.4 %collective-permute-start.4 = (f32[1,64,256]{2,1,0:T(8,128)S(1)}, f32[1,64,256]{2,1,0:T(8,128)S(1)}, u32[]{:S(2)}, u32[]{:S(2)}) collective-permute-start(f32[1,64,256]{2,1,0:T(8,128)S(1)} %pack.1), channel_id=1, source_target_pairs={{0,6},{1,7},{2,4},{3,5},{4,2},{5,3},{6,0},{7,1},{8,14},{9,15},{10,... | collective-permute-start | bytes 196616 | tf_op jit(solution)/shard_map/ppermute | solution.py:31
  7.7 5.0 %collective-permute-start.3 = (f32[1,64,256]{2,1,0:T(8,128)S(1)}, f32[1,64,256]{2,1,0:T(8,128)S(1)}, u32[]{:S(2)}, u32[]{:S(2)}) collective-permute-start(f32[1,64,256]{2,1,0:T(8,128)S(1)} %pack.1), channel_id=1, source_target_pairs={{0,2},{1,3},{2,0},{3,1},{4,6},{5,7},{6,4},{7,5},{8,10},{9,11},{10,... | collective-permute-start | bytes 196616 | tf_op jit(solution)/shard_map/ppermute | solution.py:21
  10.1 5.5 %collective-permute-start.1 = (f32[2,64,256]{2,1,0:T(8,128)S(1)}, f32[2,64,256]{2,1,0:T(8,128)S(1)}, u32[]{:S(2)}, u32[]{:S(2)}) collective-permute-start(f32[2,64,256]{2,1,0:T(8,128)S(1)} %pad_maximum_fusion.2), channel_id=1, source_target_pairs={{0,16},{8,24},{16,0},{24,8},{1,17},{9,25},{17,1},{25,9},{2,18},{10... | collective-permute-start | bytes 393224 | tf_op jit(solution)/shard_map/ppermute | solution.py:21
  12.8 6.5 %collective-permute-start.5 = (f32[2,64,256]{2,1,0:T(8,128)S(1)}, f32[2,64,256]{2,1,0:T(8,128)S(1)}, u32[]{:S(2)}, u32[]{:S(2)}) collective-permute-start(f32[2,64,256]{2,1,0:T(8,128)S(1)} %pad_maximum_fusion.3), channel_id=1, source_target_pairs={{0,1},{1,0},{2,3},{3,2},{4,5},{5,4},{6,7},{7,6},{8,9},{9,8},{10,11... | collective-permute-start | bytes 393224 | tf_op jit(solution)/shard_map/ppermute | solution.py:21
  15.7 6.6 %collective-permute-start.2 = (f32[4,64,256]{2,1,0:T(8,128)S(1)}, f32[4,64,256]{2,1,0:T(8,128)S(1)}, u32[]{:S(2)}, u32[]{:S(2)}) collective-permute-start(f32[4,64,256]{2,1,0:T(8,128)S(1)} %pad_maximum_fusion), channel_id=1, source_target_pairs={{0,1},{1,0},{2,3},{3,2},{4,5},{5,4},{6,7},{7,6},{8,9},{9,8},{10,11... | collective-permute-start | bytes 786440 | tf_op jit(solution)/shard_map/ppermute | solution.py:21
  19.3 6.4 %collective-permute-start.6 = (f32[4,64,256]{2,1,0:T(8,128)S(1)}, f32[4,64,256]{2,1,0:T(8,128)S(1)}, u32[]{:S(2)}, u32[]{:S(2)}) collective-permute-start(f32[4,64,256]{2,1,0:T(8,128)S(1)} %pad_maximum_fusion.1), channel_id=1, source_target_pairs={{0,16},{8,24},{16,0},{24,8},{1,17},{9,25},{17,1},{25,9},{2,18},{10... | collective-permute-start | bytes 786440 | tf_op jit(solution)/shard_map/ppermute | solution.py:21
  58.4 3.6 %collective-permute-start.10 = (f32[400,1024]{1,0:T(8,128)S(1)}, f32[400,1024]{1,0:T(8,128)S(1)}, u32[]{:S(2)}, u32[]{:S(2)}) collective-permute-start(f32[400,1024]{1,0:T(8,128)S(1)} %turn.7.one_ref), channel_id=1, source_target_pairs={{0,8},{8,0},{16,24},{24,16},{1,9},{9,1},{17,25},{25,17},{2,10},{10... | collective-permute-start | bytes 4915208 | tf_op jit(solution)/shard_map/ppermute | solution.py:21
  59.1 5.2 %collective-permute-start.9 = (f32[400,1024]{1,0:T(8,128)S(1)}, f32[400,1024]{1,0:T(8,128)S(1)}, u32[]{:S(2)}, u32[]{:S(2)}) collective-permute-start(f32[400,1024]{1,0:T(8,128)S(1)} %turn.6.one_ref), channel_id=1, source_target_pairs={{0,8},{8,0},{16,24},{24,16},{1,9},{9,1},{17,25},{25,17},{2,10},{10... | collective-permute-start | bytes 4915208 | tf_op jit(solution)/shard_map/ppermute | solution.py:21
  60.3 6.4 %collective-permute-start.8 = (f32[400,1024]{1,0:T(8,128)S(1)}, f32[400,1024]{1,0:T(8,128)S(1)}, u32[]{:S(2)}, u32[]{:S(2)}) collective-permute-start(f32[400,1024]{1,0:T(8,128)S(1)} %turn.5.one_ref), channel_id=1, source_target_pairs={{0,8},{8,0},{16,24},{24,16},{1,9},{9,1},{17,25},{25,17},{2,10},{10... | collective-permute-start | bytes 4915208 | tf_op jit(solution)/shard_map/ppermute | solution.py:21
  60.9 8.1 %collective-permute-start.7 = (f32[400,1024]{1,0:T(8,128)S(1)}, f32[400,1024]{1,0:T(8,128)S(1)}, u32[]{:S(2)}, u32[]{:S(2)}) collective-permute-start(f32[400,1024]{1,0:T(8,128)S(1)} %turn.4.one_ref), channel_id=1, source_target_pairs={{0,8},{8,0},{16,24},{24,16},{1,9},{9,1},{17,25},{25,17},{2,10},{10... | collective-permute-start | bytes 4915208 | tf_op jit(solution)/shard_map/ppermute | solution.py:21

commit v7 on v6

--- a/solution.py
+++ b/solution.py
@@ -327,7 +327,8 @@
         often = dot(which, times[x])
 
         sig = 1.0 / (1.0 + jnp.exp(-scores))
-        sig_neg = 1.0 / (1.0 + jnp.exp(scores))
+        positive = jnp.sum(jnp.where(target_col == lane, scores, 0.0), axis=1, keepdims=True)
+        sig_neg = 1.0 / (1.0 + jnp.exp(positive))
         g = sig * often - jnp.where(target_col == lane, sig_neg, 0.0)
         g = g * weight_col
         g_high, g_low = high_low(g)

time: 70.5 us -> 70.5 us (level)
  no operation moved by 1% of the time
where the time goes in v7:
time: 70.5 us; the launch traced here: 70.4 us
  Pallas kernels  41.5 us (59%)
  starting transfers between devices  14.8 us (21%)
  waiting for transfers between devices  13.2 us (19%)
  between operations  0.76 us (1%)
    pallas_call x1, Pallas kernels, gradients(): pl.pallas_call(functools.partial(main_kernel, spec), in_specs=[pl.BlockSp...  32.1 us
    ppermute x10, starting transfers between devices, swap(): return lax.ppermute(x, axis, [(i, i ^ 1 << bit) for i in range(count)])  13.4 us
    ppermute x10, waiting for transfers between devices, swap(): return lax.ppermute(x, axis, [(i, i ^ 1 << bit) for i in range(count)])  13.2 us
    pallas_call x4, Pallas kernels, summed(): pl.pallas_call(add_kernel, grid=(1,), in_specs=[block, block] + ([] if to...  5.32 us
    pallas_call x4, Pallas kernels, summed(): pl.pallas_call(functools.partial(finish_kernel, dim // 2, k * size), in_s...  2.38 us
    pallas_call x1, Pallas kernels, packed(): pl.pallas_call(functools.partial(pack_kernel, dim // 2, part_rows), in_sp...  1.64 us
  transfers between devices with their start and end apart: 11, of which 9 were waited for; matrix products, arithmetic and copies ran while one was open for 0% of the time, Pallas kernels for 8%

profile of v7, /device:TPU:0, one launch (start us, length us, event | category | flops | bytes accessed | tf_op | source)
XLA Modules:
  0.0 70.4 jit_solution(12902864690284921912)
XLA Ops:
  0.6 1.6 %pack.1 = f32[1,64,256]{2,1,0:T(8,128)S(1)} custom-call(s32[1,2]{1,0:T(1,128)} %counts.1, f32[32,400]{1,0:T(8,128)} %entities.1, s32[1,2,256]{2,1,0:T(2,128)} %src.1, s32[1,2,256]{2,1,0:T(2,128)} %dst.1, s32[1,2,256]{2,1,0:T(2,128)} %rel.1, s32[1,2,1024]{2,1,0:T(2,128)} %neg.1, f32[1,2,256]{2,1,0:T(2,128)} %weight.1), custom_call_target="tpu_custom_call" | custom-call | tf_op jit(solution)/shard_map/pack/pallas_call | solution.py:105
  2.3 4.1 %collective-permute-start = (f32[1,64,256]{2,1,0:T(8,128)S(1)}, f32[1,64,256]{2,1,0:T(8,128)S(1)}, u32[]{:S(2)}, u32[]{:S(2)}) collective-permute-start(f32[1,64,256]{2,1,0:T(8,128)S(1)} %pack.1), channel_id=1, source_target_pairs={{0,4},{1,5},{2,6},{3,7},{4,0},{5,1},{6,2},{7,3},{8,12},{9,13},{10,... | collective-permute-start | bytes 196616 | tf_op jit(solution)/shard_map/ppermute | solution.py:21
  6.4 1.3 %collective-permute-start.4 = (f32[1,64,256]{2,1,0:T(8,128)S(1)}, f32[1,64,256]{2,1,0:T(8,128)S(1)}, u32[]{:S(2)}, u32[]{:S(2)}) collective-permute-start(f32[1,64,256]{2,1,0:T(8,128)S(1)} %pack.1), channel_id=1, source_target_pairs={{0,6},{1,7},{2,4},{3,5},{4,2},{5,3},{6,0},{7,1},{8,14},{9,15},{10,... | collective-permute-start | bytes 196616 | tf_op jit(solution)/shard_map/ppermute | solution.py:31
  7.7 0.2 collective-permute-start.3
  8.0 2.2 %collective-permute-done = f32[1,64,256]{2,1,0:T(8,128)S(1)} collective-permute-done((f32[1,64,256]{2,1,0:T(8,128)S(1)}, f32[1,64,256]{2,1,0:T(8,128)S(1)}, u32[]{:S(2)}, u32[]{:S(2)}) %collective-permute-start) | collective-permute-done | bytes 65568 | tf_op jit(solution)/shard_map/ppermute | solution.py:21
  10.1 2.6 %collective-permute-start.1 = (f32[2,64,256]{2,1,0:T(8,128)S(1)}, f32[2,64,256]{2,1,0:T(8,128)S(1)}, u32[]{:S(2)}, u32[]{:S(2)}) collective-permute-start(f32[2,64,256]{2,1,0:T(8,128)S(1)} %pad_maximum_fusion.2), channel_id=1, source_target_pairs={{0,16},{8,24},{16,0},{24,8},{1,17},{9,25},{17,1},{25,9},{2,18},{10... | collective-permute-start | bytes 393224 | tf_op jit(solution)/shard_map/ppermute | solution.py:21
  12.7 0.0 collective-permute-done.4
  12.8 0.0 collective-permute-done.3
  12.8 1.6 %collective-permute-start.5 = (f32[2,64,256]{2,1,0:T(8,128)S(1)}, f32[2,64,256]{2,1,0:T(8,128)S(1)}, u32[]{:S(2)}, u32[]{:S(2)}) collective-permute-start(f32[2,64,256]{2,1,0:T(8,128)S(1)} %pad_maximum_fusion.3), channel_id=1, source_target_pairs={{0,1},{1,0},{2,3},{3,2},{4,5},{5,4},{6,7},{7,6},{8,9},{9,8},{10,11... | collective-permute-start | bytes 393224 | tf_op jit(solution)/shard_map/ppermute | solution.py:21
  14.4 1.3 %collective-permute-done.1 = f32[2,64,256]{2,1,0:T(8,128)S(1)} collective-permute-done((f32[2,64,256]{2,1,0:T(8,128)S(1)}, f32[2,64,256]{2,1,0:T(8,128)S(1)}, u32[]{:S(2)}, u32[]{:S(2)}) %collective-permute-start.1) | collective-permute-done | bytes 131104 | tf_op jit(solution)/shard_map/ppermute | solution.py:21
  15.7 2.1 %collective-permute-start.2 = (f32[4,64,256]{2,1,0:T(8,128)S(1)}, f32[4,64,256]{2,1,0:T(8,128)S(1)}, u32[]{:S(2)}, u32[]{:S(2)}) collective-permute-start(f32[4,64,256]{2,1,0:T(8,128)S(1)} %pad_maximum_fusion), channel_id=1, source_target_pairs={{0,1},{1,0},{2,3},{3,2},{4,5},{5,4},{6,7},{7,6},{8,9},{9,8},{10,11... | collective-permute-start | bytes 786440 | tf_op jit(solution)/shard_map/ppermute | solution.py:21
  17.8 1.4 %collective-permute-done.5 = f32[2,64,256]{2,1,0:T(8,128)S(1)} collective-permute-done((f32[2,64,256]{2,1,0:T(8,128)S(1)}, f32[2,64,256]{2,1,0:T(8,128)S(1)}, u32[]{:S(2)}, u32[]{:S(2)}) %collective-permute-start.5) | collective-permute-done | bytes 131104 | tf_op jit(solution)/shard_map/ppermute | solution.py:21
  19.3 1.5 %collective-permute-start.6 = (f32[4,64,256]{2,1,0:T(8,128)S(1)}, f32[4,64,256]{2,1,0:T(8,128)S(1)}, u32[]{:S(2)}, u32[]{:S(2)}) collective-permute-start(f32[4,64,256]{2,1,0:T(8,128)S(1)} %pad_maximum_fusion.1), channel_id=1, source_target_pairs={{0,16},{8,24},{16,0},{24,8},{1,17},{9,25},{17,1},{25,9},{2,18},{10... | collective-permute-start | bytes 786440 | tf_op jit(solution)/shard_map/ppermute | solution.py:21
  20.8 1.5 %collective-permute-done.2 = f32[4,64,256]{2,1,0:T(8,128)S(1)} collective-permute-done((f32[4,64,256]{2,1,0:T(8,128)S(1)}, f32[4,64,256]{2,1,0:T(8,128)S(1)}, u32[]{:S(2)}, u32[]{:S(2)}) %collective-permute-start.2) | collective-permute-done | bytes 262176 | tf_op jit(solution)/shard_map/ppermute | solution.py:21
  22.4 3.3 %collective-permute-done.6 = f32[4,64,256]{2,1,0:T(8,128)S(1)} collective-permute-done((f32[4,64,256]{2,1,0:T(8,128)S(1)}, f32[4,64,256]{2,1,0:T(8,128)S(1)}, u32[]{:S(2)}, u32[]{:S(2)}) %collective-permute-start.6) | collective-permute-done | bytes 262176 | tf_op jit(solution)/shard_map/ppermute | solution.py:21
  25.7 32.1 %gradients.1 = (f32[4096,4,128]{2,1,0:T(4,128)S(1)}, f32[4096,4,128]{2,1,0:T(4,128)S(1)}, f32[32,400]{1,0:T(8,128)}) custom-call(f32[400,4096]{1,0:T(8,128)} %bitcast.3, f32[16,64,256]{2,1,0:T(8,128)S(1)} %constant_dynamic-update-slice_fusion.blocks_of), custom_call_target="tpu_custom_call" | custom-call | tf_op jit(solution)/shard_map/gradients/pallas_call | solution.py:415
  57.9 0.6 turn.7.one_ref
  58.5 0.1 collective-permute-start.10
  58.5 0.6 turn.6.one_ref
  59.1 0.6 collective-permute-start.9
  59.7 0.6 turn.5.one_ref
  60.3 0.1 collective-permute-start.8
  60.4 0.6 turn.4.one_ref
  61.0 0.6 collective-permute-start.7
  61.5 0.5 collective-permute-done.10.other_ref
  62.0 1.3 %add_part.4.refs_0_ = f32[400,4096]{1,0:T(8,128)} custom-call(f32[400,1024]{1,0:T(8,128)S(1)} %turn.7.one_ref, f32[400,1024]{1,0:T(8,128)S(1)} %collective-permute-done.10.other_ref), custom_call_target="tpu_custom_call" | custom-call | flops 409600 | bytes 4915200 | tf_op jit(solution)/shard_map/add_part/pallas_call | solution.py:157
  63.4 1.0 %collective-permute-done.9.other_ref = f32[400,1024]{1,0:T(8,128)S(1)} collective-permute-done((f32[400,1024]{1,0:T(8,128)S(1)}, f32[400,1024]{1,0:T(8,128)S(1)}, u32[]{:S(2)}, u32[]{:S(2)}) %collective-permute-start.9) | collective-permute-done | bytes 1638432 | tf_op jit(solution)/shard_map/ppermute | solution.py:21
  64.4 1.3 %add_part.5.refs_0_ = f32[400,4096]{1,0:T(8,128)} custom-call(f32[400,1024]{1,0:T(8,128)S(1)} %turn.6.one_ref, f32[400,1024]{1,0:T(8,128)S(1)} %collective-permute-done.9.other_ref, f32[400,4096]{1,0:T(8,128)} %add_part.4.refs_0_), custom_call_target="tpu_custom_call", output_to_operand_aliasing={{}: (2, {})} | custom-call | flops 409600 | bytes 4915200 | tf_op jit(solution)/shard_map/add_part/pallas_call | solution.py:157
  65.7 1.0 %collective-permute-done.8.other_ref = f32[400,1024]{1,0:T(8,128)S(1)} collective-permute-done((f32[400,1024]{1,0:T(8,128)S(1)}, f32[400,1024]{1,0:T(8,128)S(1)}, u32[]{:S(2)}, u32[]{:S(2)}) %collective-permute-start.8) | collective-permute-done | bytes 1638432 | tf_op jit(solution)/shard_map/ppermute | solution.py:21
  66.7 1.3 %add_part.6.refs_0_ = f32[400,4096]{1,0:T(8,128)} custom-call(f32[400,1024]{1,0:T(8,128)S(1)} %turn.5.one_ref, f32[400,1024]{1,0:T(8,128)S(1)} %collective-permute-done.8.other_ref, f32[400,4096]{1,0:T(8,128)} %add_part.5.refs_0_), custom_call_target="tpu_custom_call", output_to_operand_aliasing={{}: (2, {})} | custom-call | flops 409600 | bytes 4915200 | tf_op jit(solution)/shard_map/add_part/pallas_call | solution.py:157
  68.0 1.0 %collective-permute-done.7.other_ref = f32[400,1024]{1,0:T(8,128)S(1)} collective-permute-done((f32[400,1024]{1,0:T(8,128)S(1)}, f32[400,1024]{1,0:T(8,128)S(1)}, u32[]{:S(2)}, u32[]{:S(2)}) %collective-permute-start.7) | collective-permute-done | bytes 1638432 | tf_op jit(solution)/shard_map/ppermute | solution.py:21
  69.1 1.3 %add_part.7 = f32[400,4096]{1,0:T(8,128)} custom-call(f32[400,1024]{1,0:T(8,128)S(1)} %turn.4.one_ref, f32[400,1024]{1,0:T(8,128)S(1)} %collective-permute-done.7.other_ref, f32[400,4096]{1,0:T(8,128)} %add_part.6.refs_0_), custom_call_target="tpu_custom_call", output_to_operand_aliasing={{}: (2, {})} | custom-call | flops 409600 | bytes 4915200 | tf_op jit(solution)/shard_map/add_part/pallas_call | solution.py:157
  (12 shorter events, 0.1 us)
Async XLA Ops:
  2.3 7.9 %collective-permute-start = (f32[1,64,256]{2,1,0:T(8,128)S(1)}, f32[1,64,256]{2,1,0:T(8,128)S(1)}, u32[]{:S(2)}, u32[]{:S(2)}) collective-permute-start(f32[1,64,256]{2,1,0:T(8,128)S(1)} %pack.1), channel_id=1, source_target_pairs={{0,4},{1,5},{2,6},{3,7},{4,0},{5,1},{6,2},{7,3},{8,12},{9,13},{10,... | collective-permute-start | bytes 196616 | tf_op jit(solution)/shard_map/ppermute | solution.py:21
  6.4 6.4 %collective-permute-start.4 = (f32[1,64,256]{2,1,0:T(8,128)S(1)}, f32[1,64,256]{2,1,0:T(8,128)S(1)}, u32[]{:S(2)}, u32[]{:S(2)}) collective-permute-start(f32[1,64,256]{2,1,0:T(8,128)S(1)} %pack.1), channel_id=1, source_target_pairs={{0,6},{1,7},{2,4},{3,5},{4,2},{5,3},{6,0},{7,1},{8,14},{9,15},{10,... | collective-permute-start | bytes 196616 | tf_op jit(solution)/shard_map/ppermute | solution.py:31
  7.7 5.0 %collective-permute-start.3 = (f32[1,64,256]{2,1,0:T(8,128)S(1)}, f32[1,64,256]{2,1,0:T(8,128)S(1)}, u32[]{:S(2)}, u32[]{:S(2)}) collective-permute-start(f32[1,64,256]{2,1,0:T(8,128)S(1)} %pack.1), channel_id=1, source_target_pairs={{0,2},{1,3},{2,0},{3,1},{4,6},{5,7},{6,4},{7,5},{8,10},{9,11},{10,... | collective-permute-start | bytes 196616 | tf_op jit(solution)/shard_map/ppermute | solution.py:21
  10.1 5.5 %collective-permute-start.1 = (f32[2,64,256]{2,1,0:T(8,128)S(1)}, f32[2,64,256]{2,1,0:T(8,128)S(1)}, u32[]{:S(2)}, u32[]{:S(2)}) collective-permute-start(f32[2,64,256]{2,1,0:T(8,128)S(1)} %pad_maximum_fusion.2), channel_id=1, source_target_pairs={{0,16},{8,24},{16,0},{24,8},{1,17},{9,25},{17,1},{25,9},{2,18},{10... | collective-permute-start | bytes 393224 | tf_op jit(solution)/shard_map/ppermute | solution.py:21
  12.8 6.5 %collective-permute-start.5 = (f32[2,64,256]{2,1,0:T(8,128)S(1)}, f32[2,64,256]{2,1,0:T(8,128)S(1)}, u32[]{:S(2)}, u32[]{:S(2)}) collective-permute-start(f32[2,64,256]{2,1,0:T(8,128)S(1)} %pad_maximum_fusion.3), channel_id=1, source_target_pairs={{0,1},{1,0},{2,3},{3,2},{4,5},{5,4},{6,7},{7,6},{8,9},{9,8},{10,11... | collective-permute-start | bytes 393224 | tf_op jit(solution)/shard_map/ppermute | solution.py:21
  15.7 6.6 %collective-permute-start.2 = (f32[4,64,256]{2,1,0:T(8,128)S(1)}, f32[4,64,256]{2,1,0:T(8,128)S(1)}, u32[]{:S(2)}, u32[]{:S(2)}) collective-permute-start(f32[4,64,256]{2,1,0:T(8,128)S(1)} %pad_maximum_fusion), channel_id=1, source_target_pairs={{0,1},{1,0},{2,3},{3,2},{4,5},{5,4},{6,7},{7,6},{8,9},{9,8},{10,11... | collective-permute-start | bytes 786440 | tf_op jit(solution)/shard_map/ppermute | solution.py:21
  19.3 6.4 %collective-permute-start.6 = (f32[4,64,256]{2,1,0:T(8,128)S(1)}, f32[4,64,256]{2,1,0:T(8,128)S(1)}, u32[]{:S(2)}, u32[]{:S(2)}) collective-permute-start(f32[4,64,256]{2,1,0:T(8,128)S(1)} %pad_maximum_fusion.1), channel_id=1, source_target_pairs={{0,16},{8,24},{16,0},{24,8},{1,17},{9,25},{17,1},{25,9},{2,18},{10... | collective-permute-start | bytes 786440 | tf_op jit(solution)/shard_map/ppermute | solution.py:21
  58.5 3.6 %collective-permute-start.10 = (f32[400,1024]{1,0:T(8,128)S(1)}, f32[400,1024]{1,0:T(8,128)S(1)}, u32[]{:S(2)}, u32[]{:S(2)}) collective-permute-start(f32[400,1024]{1,0:T(8,128)S(1)} %turn.7.one_ref), channel_id=1, source_target_pairs={{0,8},{8,0},{16,24},{24,16},{1,9},{9,1},{17,25},{25,17},{2,10},{10... | collective-permute-start | bytes 4915208 | tf_op jit(solution)/shard_map/ppermute | solution.py:21
  59.1 5.2 %collective-permute-start.9 = (f32[400,1024]{1,0:T(8,128)S(1)}, f32[400,1024]{1,0:T(8,128)S(1)}, u32[]{:S(2)}, u32[]{:S(2)}) collective-permute-start(f32[400,1024]{1,0:T(8,128)S(1)} %turn.6.one_ref), channel_id=1, source_target_pairs={{0,8},{8,0},{16,24},{24,16},{1,9},{9,1},{17,25},{25,17},{2,10},{10... | collective-permute-start | bytes 4915208 | tf_op jit(solution)/shard_map/ppermute | solution.py:21
  60.3 6.4 %collective-permute-start.8 = (f32[400,1024]{1,0:T(8,128)S(1)}, f32[400,1024]{1,0:T(8,128)S(1)}, u32[]{:S(2)}, u32[]{:S(2)}) collective-permute-start(f32[400,1024]{1,0:T(8,128)S(1)} %turn.5.one_ref), channel_id=1, source_target_pairs={{0,8},{8,0},{16,24},{24,16},{1,9},{9,1},{17,25},{25,17},{2,10},{10... | collective-permute-start | bytes 4915208 | tf_op jit(solution)/shard_map/ppermute | solution.py:21
  61.0 8.1 %collective-permute-start.7 = (f32[400,1024]{1,0:T(8,128)S(1)}, f32[400,1024]{1,0:T(8,128)S(1)}, u32[]{:S(2)}, u32[]{:S(2)}) collective-permute-start(f32[400,1024]{1,0:T(8,128)S(1)} %turn.4.one_ref), channel_id=1, source_target_pairs={{0,8},{8,0},{16,24},{24,16},{1,9},{9,1},{17,25},{25,17},{2,10},{10... | collective-permute-start | bytes 4915208 | tf_op jit(solution)/shard_map/ppermute | solution.py:21
